TPU v7x, 512 devices: a whole 4x8x8 slice. The times are simulated.
512 devices in a mesh: var: 2 (over core), tok: 4 (over x), wide: 64 (over y, z).
Axes of the slice: x: 4, y: 8, z: 8, core: 2. Of those that a mesh axis runs over, the one named last changes fastest.
Arguments:
- tokens: bfloat16 [512, 8192], P('wide', 'tok'), may hold values from -8 to 8
- norm_gain: float32 [8192], P('tok'), may hold values from 0 to 2
- gate_parent: bfloat16 [8192, 20480], P('tok', 'wide'), may hold values from -0.0625 to 0.0625
- up_parent: bfloat16 [8192, 20480], P('tok', 'wide'), may hold values from -1 to 1
- down_parent: bfloat16 [20480, 8192], P('wide', 'tok'), may hold values from -1 to 1
- kept: int32 [2, 10240], P('var'), may hold values from 0 to 20479, as said below
Outputs:
- loss: float32 [2], P('var')
- grad_down: bfloat16 [2, 10240, 8192], P('var', 'wide', 'tok')
Inputs may be any that keep to these rules, and one draw needn't show every extreme that they name: Each row is ascending and distinct. Entries 2 * 160 * m to 2 * 160 * (m + 1) - 1 of a row are units of parent blocks 2m and 2m+1 (parent block b holds units b * 320 to (b + 1) * 320 - 1); each parent block holds between 80 and 240 kept units of a row, and both ends are reached in every row.
All inputs are finite; a program needn't handle non-finite values.
Results may differ from a plain program's by a relative error of at most 0.0059.
Values may be sent and summed in bfloat16 or wider, within the bound.
No kernel may reach another device: no remote copies, remote signals or barrier semaphores. Data moves between devices by JAX's collectives and lax.ppermute only.
A program may use at most 64 MiB of HBM per device.

v0:
```python
import math

import jax
import jax.numpy as jnp
from jax import lax
from jax.sharding import PartitionSpec as P

D = 8192


def partner_2(shard, axis, stride):
    return lax.ppermute(shard, axis, [(i, i ^ 1 << stride) for i in range(lax.axis_size(axis))])


def per_device(tokens, norm_gain, gate_parent, up_parent, down_parent, kept):
    gathered = lax.all_gather(tokens, "wide", axis=0, tiled=True)
    widths = gathered.astype(jnp.float32)
    squares = lax.psum(jnp.sum(widths * widths, axis=1), "tok")
    scaled = lax.rsqrt(squares / D + 1e-05)
    normed = (widths * scaled[:, None] * norm_gain[None, :]).astype(jnp.bfloat16)
    local = gate_parent.shape[1]
    total_rows = normed.shape[0]
    gate, up = lax.psum(
        (
            jnp.dot(normed, gate_parent, preferred_element_type=jnp.float32),
            jnp.dot(normed, up_parent, preferred_element_type=jnp.float32),
        ),
        "tok",
    )
    hidden = (jax.nn.silu(gate) * up).astype(jnp.bfloat16)
    var_kept = kept[0]
    block = var_kept.shape[0] // lax.axis_size("wide")
    window = 3 * block // 2
    spare = 2 * block - window
    wide_index = lax.axis_index("wide")
    parity = wide_index % 2
    pair_kept = lax.dynamic_slice_in_dim(var_kept, wide_index // 2 * 2 * block, 2 * block)
    channels = wide_index * local + jnp.arange(local, dtype=jnp.int32)
    matches = channels[:, None] == pair_kept[None, :]
    dropped = jnp.where(jnp.any(matches, axis=1)[None, :], jnp.zeros((), jnp.bfloat16), hidden)
    piece = lax.psum_scatter(
        -jnp.dot(dropped, down_parent, preferred_element_type=jnp.float32),
        "wide",
        scatter_dimension=0,
        tiled=True,
    )
    error_sum = lax.psum(jnp.sum(piece * piece), ("tok", "wide"))
    rounded = lax.all_gather(piece.astype(jnp.bfloat16), "wide", axis=0, tiled=True)
    loss = error_sum / (total_rows * D)
    own_start = parity * spare
    out_start = parity * block
    picker = lax.dynamic_slice_in_dim(matches, own_start, window, 1).astype(jnp.bfloat16)
    selected = jnp.dot(hidden, picker, preferred_element_type=jnp.float32).astype(jnp.bfloat16)
    factor = 1.0 / math.sqrt(total_rows)
    contract = (((0,), (0,)), ((), ()))
    own_grad = (
        lax.dot_general(selected, rounded, contract, preferred_element_type=jnp.float32) * factor
    ).astype(jnp.bfloat16)
    partner = partner_2(own_grad, "wide", 0)
    full_shape = list(own_grad.shape)
    full_shape[0] = 2 * block
    placed = lax.dynamic_update_slice_in_dim(
        jnp.zeros(full_shape, own_grad.dtype), own_grad, own_start, 0
    )
    neighbour = lax.dynamic_update_slice_in_dim(
        jnp.zeros(full_shape, own_grad.dtype), partner, spare - own_start, 0
    )
    grad = lax.dynamic_slice_in_dim(placed + neighbour, out_start, block, 0)
    return (loss.reshape(1), grad[None])


def solution(mesh):
    in_specs = (
        P("wide", "tok"),
        P("tok"),
        P("tok", "wide"),
        P("tok", "wide"),
        P("wide", "tok"),
        P("var", None),
    )
    out_specs = (P("var"), P("var", "wide", "tok"))
    return jax.shard_map(
        per_device, mesh=mesh, in_specs=in_specs, out_specs=out_specs, check_vma=False
    )
```

profile of v0, /device:TPU:64, one launch (start us, length us, event | category | flops | bytes accessed | tf_op | source)
XLA Modules:
  0.0 1139.6 jit_solution(1320711407889946489)
XLA Ops:
  7.2 0.0 copy-start
  7.2 0.0 copy-start.3
  7.2 0.0 all-gather.3.cloned.1.call-start
  7.2 0.7 all-gather.3.cloned.1.call-update
  7.9 0.0 all-reduce.7.cloned.1.call-start
  8.0 89.8 %all-gather.3.cloned.1.call-done = bf16[512,2048]{1,0:T(8,128)(2,1)} async-done(((bf16[8,2048]{1,0:T(8,128)(2,1)}), bf16[512,2048]{1,0:T(8,128)(2,1)}) %all-gather.3.cloned.1.call-update) | async-done | bytes 2097168 | tf_op jit(solution)/shard_map/all_gather | solution.py:16
  97.8 0.0 copy-start.1
  97.8 2.2 fusion
  100.0 10.4 psum.28
  110.4 0.0 copy-done.3
  110.4 0.0 copy-done.1
  110.4 0.0 copy-start.2
  110.4 3.2 fusion.4
  113.7 0.0 copy-done.2
  113.7 1.8 fusion.6
  115.5 0.0 all-reduce.7.cloned.1.call-update
  115.5 0.0 all-reduce.5.cloned.1.call-start
  115.6 0.8 dynamic-slice_reduce_fusion
  116.4 0.3 broadcast_compare_fusion
  116.6 53.2 %all-reduce.7.cloned.1.call-done = (f32[512,320]{0,1:T(8,128)}, f32[512,320]{0,1:T(8,128)}) async-done(((f32[512,320]{0,1:T(8,128)}, f32[512,320]{0,1:T(8,128)}), (f32[512,320]{0,1:T(8,128)}, f32[512,320]{0,1:T(8,128)})) %all-reduce.7.cloned.1.call-update) | async-done | bytes 1310736 | tf_op jit(solution)/shard_map/psum | solution.py:23
  169.9 1.5 multiply_convert_fusion
  171.3 0.0 copy-done
  171.4 3.3 convolution_negate_fusion
  174.7 0.0 all-reduce.5.cloned.1.call-update
  174.7 0.0 all-gather.5.cloned.1.call-start
  174.8 1.3 dynamic-slice.2
  176.7 168.5 %all-reduce.5.cloned.1.call-done = f32[512,2048]{1,0:T(8,128)} async-done(((f32[512,2048]{1,0:T(8,128)}), f32[512,2048]{1,0:T(8,128)}) %all-reduce.5.cloned.1.call-update) | async-done | bytes 4194320
  345.2 1.5 dynamic-slice_convert_fusion
  346.6 0.0 all-gather.5.cloned.1.call-update
  346.7 82.0 %all-gather.5.cloned.1.call-done = bf16[512,2048]{1,0:T(8,128)(2,1)} async-done(((bf16[8,2048]{1,0:T(8,128)(2,1)}), bf16[512,2048]{1,0:T(8,128)(2,1)}) %all-gather.5.cloned.1.call-update) | async-done | bytes 2097168 | tf_op jit(solution)/shard_map/all_gather | solution.py:48
  428.7 0.1 broadcast.15
  428.9 3.7 constant_dynamic-update-slice_fusion
  432.6 3.3 collective-permute-start
  435.9 1.5 multiply_reduce_fusion
  437.3 691.5 %psum.31 = f32[]{:T(128)} all-reduce(f32[]{:T(128)} %multiply_reduce_fusion), channel_id=1, replica_groups=mesh['var'=2,'tok'=4,'wide'=64] {'tok','wide'}, use_global_device_ids=true, to_apply=%region_7.8 | all-reduce | flops 1 | bytes 8 | tf_op jit(solution)/shard_map/psum | solution.py:47
  1129.5 0.0 collective-permute-done
  1129.5 1.6 add_dynamic-update-slice_fusion
  1131.0 0.9 dynamic-slice_bitcast_fusion
  (2 shorter events, 0.0 us)
Async XLA Ops:
  7.2 164.2 %copy-start = (bf16[320,2048]{1,0:T(8,128)(2,1)S(1)}, bf16[320,2048]{1,0:T(8,128)(2,1)}, u32[]{:S(2)}) copy-start(bf16[320,2048]{1,0:T(8,128)(2,1)} %param.10) | copy-start | bytes 3932164
  7.2 103.2 %copy-start.3 = (f32[2048]{0:T(1024)S(1)}, f32[2048]{0:T(1024)}, u32[]{:S(2)}) copy-start(f32[2048]{0:T(1024)} %param.7) | copy-start | bytes 24580
  7.2 90.6 %all-gather.3.cloned.1.call-start = ((), (), s32[]{:S(2)}) async-start(), calls=%async_computation | async-start | bytes 2129920 | tf_op jit(solution)/shard_map/all_gather | solution.py:16
  7.9 161.9 %all-reduce.7.cloned.1.call-start = ((), (), s32[]{:S(2)}) async-start(), calls=%async_computation.3 | async-start | bytes 2621440 | tf_op jit(solution)/shard_map/psum | solution.py:23
  97.8 12.7 %copy-start.1 = (bf16[512,2048]{1,0:T(8,128)(2,1)S(1)}, bf16[512,2048]{1,0:T(8,128)(2,1)}, u32[]{:S(2)}) copy-start(bf16[512,2048]{1,0:T(8,128)(2,1)} %all-gather.3.cloned.1.call-done) | copy-start | bytes 6291460
  110.4 3.2 copy-start.2
  115.5 229.7 %all-reduce.5.cloned.1.call-start = ((), (), s32[]{:S(2)}) async-start(), calls=%async_computation.2 | async-start | bytes 8388608
  174.7 254.0 %all-gather.5.cloned.1.call-start = ((), (), s32[]{:S(2)}) async-start(), calls=%async_computation.1 | async-start | bytes 2129920 | tf_op jit(solution)/shard_map/all_gather | solution.py:48
  432.6 696.9 %collective-permute-start = (bf16[240,2048]{1,0:T(8,128)(2,1)}, bf16[240,2048]{1,0:T(8,128)(2,1)}, u32[]{:S(2)}, u32[]{:S(2)}) collective-permute-start(bf16[240,2048]{1,0:T(8,128)(2,1)} %get-tuple-element.7), channel_id=1, source_target_pairs={{0,1},{1,0},{2,3},{3,2},{4,5},{5,4},{6,7},{7,6},{8,9},{9,8},{10,11... | collective-permute-start | bytes 2949128 | tf_op jit(solution)/shard_map/ppermute | solution.py:12
Sparse Core Ops, SparseCore 0:
  11.0 86.6 all-gather.2
  115.6 54.1 all-reduce.6
  174.8 170.2 all-reduce.4
  348.6 80.0 all-gather.4
where the time goes:
time: 1140 us
  blocking collectives  702 us (62%)
  waiting for transfers between devices  394 us (35%)
  between operations  16.3 us (1%)
  matrix products  12.1 us (1%)
    psum x1, blocking collectives, per_device(): error_sum = lax.psum(jnp.sum(piece * piece), ('tok', 'wide'))  691 us
    unnamed x5, waiting for transfers between devices  169 us
    all_gather x1, waiting for transfers between devices, per_device(): gathered = lax.all_gather(tokens, 'wide', axis=0, tiled=True)  89.8 us
    all_gather x1, waiting for transfers between devices, per_device(): lax.all_gather(piece.astype(jnp.bfloat16), 'wide', axis=0, tiled=True)  82 us
    psum x1, waiting for transfers between devices, per_device(): lax.psum((jnp.dot(normed, gate_parent, preferred_element_type=jnp.float32...  53.2 us
  transfers between devices with their start and end apart: 5, of which 4 were waited for; matrix products, arithmetic and copies ran while one was open for 0% of the time, Pallas kernels for 0%

commit v1 on v0

v1 whole, which is shorter than its diff:
```python
import math

import jax
import jax.numpy as jnp
from jax import lax
from jax.sharding import PartitionSpec as P

D = 8192
SIDE = 8


def block_groups():
    return [
        [(2 * a + i) * SIDE + 2 * b + j for i in range(2) for j in range(2)]
        for a in range(SIDE // 2)
        for b in range(SIDE // 2)
    ]


def stride_groups():
    return [
        [(2 * a + i) * SIDE + 2 * b + j for a in range(SIDE // 2) for b in range(SIDE // 2)]
        for i in range(2)
        for j in range(2)
    ]


def spread(shard, count, axes, groups=None):
    stacked = jnp.broadcast_to(shard[None], (count,) + shard.shape)
    return lax.all_to_all(stacked, axes, 0, 0, axis_index_groups=groups)


def hi_lo(value):
    hi = lax.reduce_precision(value, 8, 7)
    return hi.astype(jnp.bfloat16), (value - hi).astype(jnp.bfloat16)


def per_device(tokens, norm_gain, gate_parent, up_parent, down_parent, kept):
    n_wide = lax.axis_size("wide")
    n_tok = lax.axis_size("tok")
    core = lax.axis_index("var")
    wide = lax.axis_index("wide")
    row, col = wide // SIDE, wide % SIDE
    slot = (row % 2) * 2 + col % 2
    local = gate_parent.shape[1]
    width = tokens.shape[1]
    blocks = block_groups()

    half = tokens.shape[0] // 2
    mine = lax.dynamic_slice_in_dim(tokens, core * half, half, 0)
    gathered = spread(mine, n_wide, "wide").reshape(n_wide * half, width)

    quarter = down_parent.shape[1] // 4
    gathered, down = lax.optimization_barrier((gathered, down_parent))
    down_block = jnp.zeros((4, local, quarter), jnp.bfloat16)
    own = lax.dynamic_slice_in_dim(down, slot * quarter, quarter, 1)
    down_block = lax.dynamic_update_slice_in_dim(down_block, own[None], slot, 0)
    for k in range(1, 4):
        perm = [(w, w ^ ((k // 2) * SIDE + k % 2)) for w in range(n_wide)]
        piece = lax.dynamic_slice_in_dim(down, (slot ^ k) * quarter, quarter, 1)
        piece = lax.ppermute(piece, "wide", perm)
        down_block = lax.dynamic_update_slice_in_dim(down_block, piece[None], slot ^ k, 0)
    down_block = down_block.reshape(4 * local, quarter)

    widths = gathered.astype(jnp.float32)
    squares = jnp.sum(widths * widths, axis=1)
    gained = (widths * norm_gain[None, :]).astype(jnp.bfloat16)
    sq_hi, sq_lo = hi_lo(squares)
    lanes = lax.broadcasted_iota(jnp.int32, (n_wide * half, 128), 1)
    extra = jnp.where(lanes == 0, sq_hi[:, None], jnp.where(lanes == 1, sq_lo[:, None], jnp.zeros((), jnp.bfloat16)))
    partial = jnp.concatenate(
        [
            jnp.dot(gained, gate_parent, preferred_element_type=jnp.float32).astype(jnp.bfloat16),
            jnp.dot(gained, up_parent, preferred_element_type=jnp.float32).astype(jnp.bfloat16),
            extra,
        ],
        axis=1,
    )
    rows = n_wide * half // n_tok
    scattered = lax.all_to_all(partial.reshape(n_tok, rows, 2 * local + 128), "tok", 0, 0)
    total = jnp.sum(scattered.astype(jnp.float32), axis=0)
    scale = lax.rsqrt((total[:, 2 * local] + total[:, 2 * local + 1]) / D + 1e-05)[:, None]
    gate = total[:, :local] * scale
    up = total[:, local : 2 * local] * scale
    hidden = (jax.nn.silu(gate) * up).astype(jnp.bfloat16)

    groups = [[t * n_wide + w for t in range(n_tok) for w in block] for block in blocks]
    hidden = spread(hidden, n_tok * 4, ("tok", "wide"), groups)
    hidden = spread(hidden, 2, "var").reshape(2, n_tok, 4, rows, local)
    total_rows = 2 * n_tok * rows
    hidden = hidden.transpose(0, 1, 3, 2, 4).reshape(total_rows, 4 * local)

    var_kept = kept[0]
    block = var_kept.shape[0] // n_wide
    selected = []
    masks = []
    for i in range(2):
        pair = (row // 2 * 2 + i) * (SIDE // 2) + col // 2
        names = lax.dynamic_slice_in_dim(var_kept, pair * 2 * block, 2 * block) - pair * 2 * local
        matches = jnp.arange(2 * local, dtype=jnp.int32)[:, None] == names[None, :]
        masks.append(jnp.any(matches, axis=1))
        units = hidden[:, i * 2 * local : (i + 1) * 2 * local]
        selected.append(
            jnp.dot(units, matches.astype(jnp.bfloat16), preferred_element_type=jnp.float32).astype(jnp.bfloat16)
        )
    dropped = jnp.where(jnp.concatenate(masks)[None, :], jnp.zeros((), jnp.bfloat16), hidden)
    share = -jnp.dot(dropped, down_block, preferred_element_type=jnp.float32)

    strides = stride_groups()
    n_blocks = n_wide // 4
    shares = share.astype(jnp.bfloat16).reshape(n_blocks, total_rows // n_blocks, quarter)
    shares = lax.all_to_all(shares, "wide", 0, 0, axis_index_groups=strides)
    piece = jnp.sum(shares.astype(jnp.float32), axis=0).astype(jnp.bfloat16)
    rounded = spread(piece, n_blocks, "wide", strides).reshape(total_rows, quarter)

    errors = rounded.astype(jnp.float32)
    error_sum = lax.psum(jnp.sum(errors * errors), "tok")
    err_hi, err_lo = hi_lo(error_sum)

    factor = 1.0 / math.sqrt(total_rows)
    contract = (((0,), (0,)), ((), ()))
    grads = [
        (lax.dot_general(s, rounded, contract, preferred_element_type=jnp.float32) * factor).astype(jnp.bfloat16)
        for s in selected
    ]
    grad = jnp.concatenate(grads, axis=0).reshape(4, block, quarter)
    lanes = lax.broadcasted_iota(jnp.int32, (4, 16, quarter), 2)
    extra = jnp.where(lanes == 0, err_hi, jnp.where(lanes == 1, err_lo, jnp.zeros((), jnp.bfloat16)))
    swapped = lax.all_to_all(jnp.concatenate([grad, extra], axis=1), "wide", 0, 0, axis_index_groups=blocks)
    grad = swapped[:, :block].transpose(1, 0, 2).reshape(block, 4 * quarter)
    loss = jnp.sum(swapped[:, block, :2].astype(jnp.float32)) / (total_rows * D)
    return (loss.reshape(1), grad[None])


def solution(mesh):
    in_specs = (
        P("wide", "tok"),
        P("tok"),
        P("tok", "wide"),
        P("tok", "wide"),
        P("wide", "tok"),
        P("var", None),
    )
    out_specs = (P("var"), P("var", "wide", "tok"))
    return jax.shard_map(
        per_device, mesh=mesh, in_specs=in_specs, out_specs=out_specs, check_vma=False
    )
```

time: 1140 us -> 198 us (0.17)
  the two profiles are of different devices: /device:TPU:64 before, /device:TPU:8 now
where the time goes in v1:
time: 198 us; the launch traced here: 197 us
  blocking collectives  60.1 us (30%)
  waiting for transfers between devices  52.8 us (27%)
  starting transfers between devices  41 us (21%)
  local copies, waits for them, and re-layouts  26.3 us (13%)
  matrix products  6.47 us (3%)
  between operations  5.94 us (3%)
  other arithmetic  4.78 us (2%)
    all_to_all x3, waiting for transfers between devices, spread(): return lax.all_to_all(stacked, axes, 0, 0, axis_index_groups=groups)  39.9 us
    all_to_all x3, starting transfers between devices, spread(): return lax.all_to_all(stacked, axes, 0, 0, axis_index_groups=groups)  27.5 us
    all_to_all x1, blocking collectives, per_device(): shares = lax.all_to_all(shares, 'wide', 0, 0, axis_index_groups=strides)  24.4 us
    all_to_all x1, blocking collectives, per_device(): lax.all_to_all(jnp.concatenate([grad, extra], axis=1), 'wide', 0, 0, axis...  16.6 us
    psum x1, blocking collectives, per_device(): error_sum = lax.psum(jnp.sum(errors * errors), 'tok')  14.1 us
    ppermute x3, starting transfers between devices, per_device(): piece = lax.ppermute(piece, 'wide', perm)  9.2 us
    all_to_all x1, waiting for transfers between devices, per_device(): lax.all_to_all(partial.reshape(n_tok, rows, 2 * local + 128), 'tok', 0, 0)  7.38 us
    select_n x2, local copies, waits for them, and re-layouts, per_device(): jnp.where(jnp.concatenate(masks)[None, :], jnp.zeros((), jnp.bfloat16), h...  6.3 us
  transfers between devices with their start and end apart: 7, of which 5 were waited for; matrix products, arithmetic and copies ran while one was open for 7% of the time, Pallas kernels for 0%

profile of v1, /device:TPU:8, one launch (start us, length us, event | category | flops | bytes accessed | tf_op | source)
XLA Modules:
  0.0 197.4 jit_solution(865197128118870583)
XLA Ops:
  0.6 0.0 copy-start
  0.7 0.9 constant_dynamic-slice_fusion.5
  1.5 1.5 broadcast_in_dim.92
  3.0 16.6 %all-to-all-start = ((bf16[64,4,2048]{2,1,0:T(4,128)(2,1)}), bf16[64,4,2048]{2,1,0:T(4,128)(2,1)S(1)}, u32[]{:S(2)}, u32[]{:S(2)}) async-start(bf16[64,4,2048]{2,1,0:T(4,128)(2,1)} %broadcast_in_dim.92), calls=%async_computation | async-start | bytes 2097152 | tf_op jit(solution)/shard_map/all_to_all | solution.py:30
  19.6 0.0 copy-start.3
  19.6 29.4 %all-to-all-done = bf16[64,4,2048]{2,1,0:T(4,128)(2,1)S(1)} async-done(((bf16[64,4,2048]{2,1,0:T(4,128)(2,1)}), bf16[64,4,2048]{2,1,0:T(4,128)(2,1)S(1)}, u32[]{:S(2)}, u32[]{:S(2)}) %all-to-all-start) | async-done | bytes 1048608 | tf_op jit(solution)/shard_map/all_to_all | solution.py:30
  49.0 0.3 reshape.56
  49.3 0.3 fusion.1
  49.6 0.0 copy-done
  49.6 0.0 copy-start.2
  49.6 0.5 convolution_convert_fusion.2
  50.2 0.8 copy-done.2
  50.9 0.6 convolution_convert_fusion.3
  51.5 0.1 select_select_fusion
  51.6 0.9 copy.26
  52.6 4.3 %all-to-all-start.1 = ((bf16[4,64,768]{2,1,0:T(8,128)(2,1)}), bf16[4,64,768]{2,1,0:T(8,128)(2,1)S(1)}, u32[]{:S(2)}, u32[]{:S(2)}) async-start(bf16[4,64,768]{2,1,0:T(8,128)(2,1)} %bitcast), calls=%async_computation.1 | async-start | bytes 786432 | tf_op jit(solution)/shard_map/all_to_all | solution.py:80
  56.8 7.4 %all-to-all-done.1 = bf16[4,64,768]{2,1,0:T(8,128)(2,1)S(1)} async-done(((bf16[4,64,768]{2,1,0:T(8,128)(2,1)}), bf16[4,64,768]{2,1,0:T(8,128)(2,1)S(1)}, u32[]{:S(2)}, u32[]{:S(2)}) %all-to-all-start.1) | async-done | bytes 393248 | tf_op jit(solution)/shard_map/all_to_all | solution.py:80
  64.2 0.1 convert_reduce_fusion
  64.3 0.2 fusion.22
  64.5 0.1 fusion.18
  64.6 0.0 copy-start.1
  64.6 1.0 broadcast_in_dim.96
  65.6 4.1 %all-to-all-start.2 = ((bf16[16,64,320]{2,1,0:T(8,128)(2,1)}), bf16[16,64,320]{2,1,0:T(8,128)(2,1)S(1)}, u32[]{:S(2)}, u32[]{:S(2)}) async-start(bf16[16,64,320]{2,1,0:T(8,128)(2,1)} %broadcast_in_dim.96), calls=%async_computation.2 | async-start | bytes 1572864 | tf_op jit(solution)/shard_map/all_to_all | solution.py:30
  69.7 0.8 fusion.26
  70.5 0.0 copy-done.1
  70.5 1.0 constant_dynamic-slice_fusion
  71.4 3.4 %collective-permute-start = (bf16[320,512]{1,0:T(8,128)(2,1)}, bf16[320,512]{1,0:T(8,128)(2,1)}, u32[]{:S(2)}, u32[]{:S(2)}) collective-permute-start(bf16[320,512]{1,0:T(8,128)(2,1)} %get-tuple-element.10), channel_id=1, source_target_pairs={{0,1},{1,0},{2,3},{3,2},{4,5},{5,4},{6,7},{7,6},{8,9},{9,8},{10,11... | collective-permute-start | bytes 983048 | tf_op jit(solution)/shard_map/ppermute | solution.py:61
  74.8 0.3 fusion.7
  75.1 0.1 concatenate.18
  75.2 0.1 concatenate.19
  75.3 2.5 %collective-permute-start.1 = (bf16[320,512]{1,0:T(8,128)(2,1)}, bf16[320,512]{1,0:T(8,128)(2,1)S(1)}, u32[]{:S(2)}, u32[]{:S(2)}) collective-permute-start(bf16[320,512]{1,0:T(8,128)(2,1)} %get-tuple-element.9), channel_id=1, source_target_pairs={{0,8},{1,9},{2,10},{3,11},{4,12},{5,13},{6,14},{7,15},{8,0},{9,1},... | collective-permute-start | bytes 983048 | tf_op jit(solution)/shard_map/ppermute | solution.py:61
  77.8 3.4 %collective-permute-start.2 = (bf16[320,512]{1,0:T(8,128)(2,1)}, bf16[320,512]{1,0:T(8,128)(2,1)S(1)}, u32[]{:S(2)}, u32[]{:S(2)}) collective-permute-start(bf16[320,512]{1,0:T(8,128)(2,1)} %get-tuple-element.8), channel_id=1, source_target_pairs={{0,9},{1,8},{2,11},{3,10},{4,13},{5,12},{6,15},{7,14},{8,1},{9,0},... | collective-permute-start | bytes 983048 | tf_op jit(solution)/shard_map/ppermute | solution.py:61
  81.2 1.2 broadcast_in_dim.100
  82.3 0.8 bitcast_dynamic-update-slice_fusion.3
  83.1 2.5 %collective-permute-done = bf16[320,512]{1,0:T(8,128)(2,1)} collective-permute-done((bf16[320,512]{1,0:T(8,128)(2,1)}, bf16[320,512]{1,0:T(8,128)(2,1)}, u32[]{:S(2)}, u32[]{:S(2)}) %collective-permute-start) | collective-permute-done | bytes 327712 | tf_op jit(solution)/shard_map/ppermute | solution.py:61
  85.5 1.7 bitcast_dynamic-update-slice_fusion.2
  87.3 0.0 collective-permute-done.1
  87.3 0.8 bitcast_dynamic-update-slice_fusion.1
  88.1 3.1 %collective-permute-done.2 = bf16[320,512]{1,0:T(8,128)(2,1)S(1)} collective-permute-done((bf16[320,512]{1,0:T(8,128)(2,1)}, bf16[320,512]{1,0:T(8,128)(2,1)S(1)}, u32[]{:S(2)}, u32[]{:S(2)}) %collective-permute-start.2) | collective-permute-done | bytes 327712 | tf_op jit(solution)/shard_map/ppermute | solution.py:61
  91.1 0.7 bitcast_dynamic-update-slice_fusion
  91.9 0.0 all-to-all-done.2
  91.9 0.3 broadcast_in_dim.97
  92.1 5.0 %all_to_all.35 = bf16[2,16,64,320]{3,2,1,0:T(8,128)(2,1)S(1)} all-to-all(bf16[2,16,64,320]{3,2,1,0:T(8,128)(2,1)S(1)} %broadcast_in_dim.97), channel_id=1, replica_groups=mesh['var'=2,'tok'=4,'wide'=64] {'var'}, dimensions={0} | all-to-all | bytes 2621440 | tf_op jit(solution)/shard_map/all_to_all | solution.py:30
  97.1 0.2 broadcast_select_fusion
  97.3 2.4 %copy.28 = bf16[2,4,64,4,320]{4,3,2,1,0:T(4,128)(2,1)} copy(bf16[2,4,64,4,320]{4,2,3,1,0:T(8,128)(2,1)S(1)} %broadcast_select_fusion) | data formatting | bytes 2621440 | tf_op jit(solution)/shard_map/jit(_where)/select_n | solution.py:106
  99.7 3.9 %select_n.94 = bf16[512,1280]{1,0:T(8,128)(2,1)} reshape(bf16[2,4,64,4,320]{4,3,2,1,0:T(4,128)(2,1)} %copy.28) | data formatting | bytes 2621440 | tf_op jit(solution)/shard_map/jit(_where)/select_n | solution.py:106
  103.6 2.5 %fusion.2 = bf16[512,512]{1,0:T(8,128)(2,1)S(1)} fusion(bf16[512,1280]{1,0:T(8,128)(2,1)} %select_n.94, bf16[1280,512]{1,0:T(8,128)(2,1)} %bitcast.8), kind=kOutput, calls=%fused_computation.6 | convolution fusion | flops 671612928 | bytes 3145728 | tf_op jit(solution)/shard_map/dot_general | solution.py:107
  106.2 24.4 %all_to_all.36 = bf16[16,32,512]{2,1,0:T(8,128)(2,1)S(1)} all-to-all(bf16[16,32,512]{2,1,0:T(8,128)(2,1)S(1)} %bitcast.30), channel_id=1, replica_groups={{0,2,4,6,16,18,20,22,32,34,36,38,48,50,52,54},{1,3,5,7,17,19,21,23,33,3..., dimensions={0} | all-to-all | bytes 1048576 | tf_op jit(solution)/shard_map/all_to_all | solution.py:112
  130.5 0.1 reduce_sum.50
  130.6 0.8 broadcast_in_dim.105
  131.5 6.9 %all-to-all-start.5 = ((bf16[16,32,512]{2,1,0:T(8,128)(2,1)}), bf16[16,32,512]{2,1,0:T(8,128)(2,1)S(1)}, u32[]{:S(2)}, u32[]{:S(2)}) async-start(bf16[16,32,512]{2,1,0:T(8,128)(2,1)} %broadcast_in_dim.105), calls=%async_computation.5 | async-start | bytes 1048576 | tf_op jit(solution)/shard_map/all_to_all | solution.py:30
  138.3 2.4 %copy.27 = bf16[2,4,64,4,320]{4,3,2,1,0:T(4,128)(2,1)} copy(bf16[2,4,64,4,320]{4,2,3,1,0:T(8,128)(2,1)S(1)} %bitcast.26) | data formatting | bytes 2621440 | tf_op jit(solution)/shard_map/transpose | solution.py:91
  140.7 3.0 %reshape.59 = bf16[512,1280]{1,0:T(8,128)(2,1)S(1)} reshape(bf16[2,4,64,4,320]{4,3,2,1,0:T(4,128)(2,1)} %copy.27) | data formatting | bytes 2621440 | tf_op jit(solution)/shard_map/reshape | solution.py:91
  143.8 10.5 %all-to-all-done.5 = bf16[16,32,512]{2,1,0:T(8,128)(2,1)S(1)} async-done(((bf16[16,32,512]{2,1,0:T(8,128)(2,1)}), bf16[16,32,512]{2,1,0:T(8,128)(2,1)S(1)}, u32[]{:S(2)}, u32[]{:S(2)}) %all-to-all-start.5) | async-done | bytes 524320 | tf_op jit(solution)/shard_map/all_to_all | solution.py:30
  154.3 1.4 fusion.3
  155.7 0.9 multiply_reduce_fusion
  156.5 1.4 fusion.4
  157.9 14.1 %psum.7 = f32[]{:T(128)} all-reduce(f32[]{:T(128)} %multiply_reduce_fusion), channel_id=1, replica_groups=mesh['var'=2,'tok'=4,'wide'=64] {'tok'}, use_global_device_ids=true, to_apply=%region_6.7 | all-reduce | flops 1 | bytes 8 | tf_op jit(solution)/shard_map/psum | solution.py:117
  175.4 1.1 pad_maximum_fusion.1
  176.5 0.1 pad_maximum_fusion
  176.6 16.6 %all_to_all.37 = bf16[4,176,512]{2,1,0:T(8,128)(2,1)S(1)} all-to-all(bf16[4,176,512]{2,1,0:T(8,128)(2,1)S(1)} %pad_maximum_fusion), channel_id=1, replica_groups={{0,1,8,9},{2,3,10,11},{4,5,12,13},{6,7,14,15},{16,17,24,25},{18,19,26,2..., dimensions={0} | all-to-all | bytes 1441792 | tf_op jit(solution)/shard_map/all_to_all | solution.py:129
  193.2 0.5 copy.29
  193.7 1.3 broadcast_in_dim_reshape.3
  195.0 0.6 fusion.23
  (9 shorter events, 0.1 us)
Async XLA Ops:
  0.6 49.0 %copy-start = (bf16[2048,320]{0,1:T(8,128)(2,1)S(1)}, bf16[2048,320]{0,1:T(8,128)(2,1)}, u32[]{:S(2)}) copy-start(bf16[2048,320]{0,1:T(8,128)(2,1)} %param.9) | copy-start | bytes 3932164
  3.0 46.0 %all-to-all-start = ((bf16[64,4,2048]{2,1,0:T(4,128)(2,1)}), bf16[64,4,2048]{2,1,0:T(4,128)(2,1)S(1)}, u32[]{:S(2)}, u32[]{:S(2)}) async-start(bf16[64,4,2048]{2,1,0:T(4,128)(2,1)} %broadcast_in_dim.92), calls=%async_computation | async-start | bytes 2097152 | tf_op jit(solution)/shard_map/all_to_all | solution.py:30
  19.6 30.0 %copy-start.3 = (f32[2048]{0:T(1024)S(1)}, f32[2048]{0:T(1024)}, u32[]{:S(2)}) copy-start(f32[2048]{0:T(1024)} %param.7) | copy-start | bytes 24580
  49.6 1.3 copy-start.2
  52.6 11.7 %all-to-all-start.1 = ((bf16[4,64,768]{2,1,0:T(8,128)(2,1)}), bf16[4,64,768]{2,1,0:T(8,128)(2,1)S(1)}, u32[]{:S(2)}, u32[]{:S(2)}) async-start(bf16[4,64,768]{2,1,0:T(8,128)(2,1)} %bitcast), calls=%async_computation.1 | async-start | bytes 786432 | tf_op jit(solution)/shard_map/all_to_all | solution.py:80
  64.6 5.9 %copy-start.1 = (bf16[320,2048]{1,0:T(8,128)(2,1)S(1)}, bf16[320,2048]{1,0:T(8,128)(2,1)}, u32[]{:S(2)}) copy-start(bf16[320,2048]{1,0:T(8,128)(2,1)} %param.10) | copy-start | bytes 3932164
  65.6 26.3 %all-to-all-start.2 = ((bf16[16,64,320]{2,1,0:T(8,128)(2,1)}), bf16[16,64,320]{2,1,0:T(8,128)(2,1)S(1)}, u32[]{:S(2)}, u32[]{:S(2)}) async-start(bf16[16,64,320]{2,1,0:T(8,128)(2,1)} %broadcast_in_dim.96), calls=%async_computation.2 | async-start | bytes 1572864 | tf_op jit(solution)/shard_map/all_to_all | solution.py:30
  71.4 14.1 %collective-permute-start = (bf16[320,512]{1,0:T(8,128)(2,1)}, bf16[320,512]{1,0:T(8,128)(2,1)}, u32[]{:S(2)}, u32[]{:S(2)}) collective-permute-start(bf16[320,512]{1,0:T(8,128)(2,1)} %get-tuple-element.10), channel_id=1, source_target_pairs={{0,1},{1,0},{2,3},{3,2},{4,5},{5,4},{6,7},{7,6},{8,9},{9,8},{10,11... | collective-permute-start | bytes 983048 | tf_op jit(solution)/shard_map/ppermute | solution.py:61
  75.3 12.0 %collective-permute-start.1 = (bf16[320,512]{1,0:T(8,128)(2,1)}, bf16[320,512]{1,0:T(8,128)(2,1)S(1)}, u32[]{:S(2)}, u32[]{:S(2)}) collective-permute-start(bf16[320,512]{1,0:T(8,128)(2,1)} %get-tuple-element.9), channel_id=1, source_target_pairs={{0,8},{1,9},{2,10},{3,11},{4,12},{5,13},{6,14},{7,15},{8,0},{9,1},... | collective-permute-start | bytes 983048 | tf_op jit(solution)/shard_map/ppermute | solution.py:61
  77.8 13.4 %collective-permute-start.2 = (bf16[320,512]{1,0:T(8,128)(2,1)}, bf16[320,512]{1,0:T(8,128)(2,1)S(1)}, u32[]{:S(2)}, u32[]{:S(2)}) collective-permute-start(bf16[320,512]{1,0:T(8,128)(2,1)} %get-tuple-element.8), channel_id=1, source_target_pairs={{0,9},{1,8},{2,11},{3,10},{4,13},{5,12},{6,15},{7,14},{8,1},{9,0},... | collective-permute-start | bytes 983048 | tf_op jit(solution)/shard_map/ppermute | solution.py:61
  131.5 22.8 %all-to-all-start.5 = ((bf16[16,32,512]{2,1,0:T(8,128)(2,1)}), bf16[16,32,512]{2,1,0:T(8,128)(2,1)S(1)}, u32[]{:S(2)}, u32[]{:S(2)}) async-start(bf16[16,32,512]{2,1,0:T(8,128)(2,1)} %broadcast_in_dim.105), calls=%async_computation.5 | async-start | bytes 1048576 | tf_op jit(solution)/shard_map/all_to_all | solution.py:30

commit v2 on v1

v2 whole, which is shorter than its diff:
```python
import functools
import math

import jax
import jax.numpy as jnp
from jax import lax
from jax.experimental import pallas as pl
from jax.experimental.pallas import tpu as pltpu
from jax.sharding import PartitionSpec as P

D = 8192
SIDE = 8


def block_groups():
    return [
        [(2 * a + i) * SIDE + 2 * b + j for i in range(2) for j in range(2)]
        for a in range(SIDE // 2)
        for b in range(SIDE // 2)
    ]


def stride_groups():
    return [
        [(2 * a + i) * SIDE + 2 * b + j for a in range(SIDE // 2) for b in range(SIDE // 2)]
        for i in range(2)
        for j in range(2)
    ]


def spread(shard, count, axes, groups=None):
    stacked = jnp.broadcast_to(shard[None], (count,) + shard.shape)
    return lax.all_to_all(stacked, axes, 0, 0, axis_index_groups=groups)


def hi_lo(value):
    hi = lax.reduce_precision(value, 8, 7)
    return hi.astype(jnp.bfloat16), (value - hi).astype(jnp.bfloat16)


VMEM = pl.BlockSpec(memory_space=pltpu.VMEM)
SMEM = pl.BlockSpec(memory_space=pltpu.SMEM)


def call(kernel, out_shape, in_specs, flops, size):
    out_specs = jax.tree.map(lambda _: VMEM, out_shape)
    return pl.pallas_call(
        kernel,
        out_shape=out_shape,
        in_specs=in_specs,
        out_specs=out_specs,
        compiler_params=pltpu.CompilerParams(vmem_limit_bytes=32 * 1024 * 1024),
        cost_estimate=pl.CostEstimate(flops=flops, bytes_accessed=size, transcendentals=0),
    )


def residual_kernel(slot_ref, hidden_ref, drop_ref, down0, down1, down2, down3, out_ref):
    slot = slot_ref[0]
    downs = (down0, down1, down2, down3)
    for core in range(2):
        total = None
        for k in range(4):
            index = slot ^ k
            units = hidden_ref[core, index] * drop_ref[index]
            term = jnp.dot(units, downs[k][...], preferred_element_type=jnp.float32)
            total = term if total is None else total + term
        out_ref[core] = (-total).astype(out_ref.dtype)


def select_kernel(names_ref, hidden_ref, out_ref):
    local = hidden_ref.shape[3]
    rows = hidden_ref.shape[2]
    count = names_ref.shape[1]
    for pair in range(2):
        names = names_ref[pair]
        for core in range(2):
            total = None
            for i in range(2):
                units = lax.broadcasted_iota(jnp.int32, (count, local), 1) + i * local
                picker = jnp.where(units == names, 1.0, 0.0).astype(jnp.bfloat16)
                term = lax.dot_general(
                    picker,
                    hidden_ref[core, 2 * pair + i],
                    (((1,), (1,)), ((), ())),
                    preferred_element_type=jnp.float32,
                )
                total = term if total is None else total + term
            out_ref[pair, :, core * rows : (core + 1) * rows] = total.astype(out_ref.dtype)


def gradient_kernel(factor, chosen_ref, rounded_ref, grad_ref, error_ref):
    rounded = rounded_ref[...]
    block = grad_ref.shape[1]
    for pair in range(2):
        product = jnp.dot(chosen_ref[pair], rounded, preferred_element_type=jnp.float32) * factor
        for i in range(2):
            grad_ref[2 * pair + i] = product[i * block : (i + 1) * block].astype(grad_ref.dtype)
    errors = rounded.astype(jnp.float32)
    columns = jnp.sum(errors * errors, axis=0, keepdims=True)
    total = columns[:, :128]
    for i in range(1, columns.shape[1] // 128):
        total = total + columns[:, i * 128 : (i + 1) * 128]
    error_ref[...] = total


def interleave_kernel(in_ref, out_ref):
    width = in_ref.shape[2]
    for i in range(in_ref.shape[0]):
        out_ref[:, i * width : (i + 1) * width] = in_ref[i]


def per_device(tokens, norm_gain, gate_parent, up_parent, down_parent, kept):
    n_wide = lax.axis_size("wide")
    n_tok = lax.axis_size("tok")
    core = lax.axis_index("var")
    wide = lax.axis_index("wide")
    row, col = wide // SIDE, wide % SIDE
    slot = (row % 2) * 2 + col % 2
    local = gate_parent.shape[1]
    width = tokens.shape[1]
    blocks = block_groups()

    half = tokens.shape[0] // 2
    mine = lax.dynamic_slice_in_dim(tokens, core * half, half, 0)
    gathered = spread(mine, n_wide, "wide").reshape(n_wide * half, width)

    widths = gathered.astype(jnp.float32)
    squares = jnp.sum(widths * widths, axis=1)
    gained = (widths * norm_gain[None, :]).astype(jnp.bfloat16)
    sq_hi, sq_lo = hi_lo(squares)
    lanes = lax.broadcasted_iota(jnp.int32, (n_wide * half, 128), 1)
    extra = jnp.where(lanes == 0, sq_hi[:, None], jnp.where(lanes == 1, sq_lo[:, None], jnp.zeros((), jnp.bfloat16)))
    partial = jnp.concatenate(
        [
            jnp.dot(gained, gate_parent, preferred_element_type=jnp.float32).astype(jnp.bfloat16),
            jnp.dot(gained, up_parent, preferred_element_type=jnp.float32).astype(jnp.bfloat16),
            extra,
        ],
        axis=1,
    )
    rows = n_wide * half // n_tok

    quarter = down_parent.shape[1] // 4
    partial, down = lax.optimization_barrier((partial, down_parent))
    downs = [lax.dynamic_slice_in_dim(down, (slot ^ k) * quarter, quarter, 1) for k in range(4)]
    for k in range(1, 4):
        perm = [(w, w ^ ((k // 2) * SIDE + k % 2)) for w in range(n_wide)]
        downs[k] = lax.ppermute(downs[k], "wide", perm)

    scattered = lax.all_to_all(partial.reshape(n_tok, rows, 2 * local + 128), "tok", 0, 0)
    scattered, *downs = lax.optimization_barrier((scattered, *downs))
    total = jnp.sum(scattered.astype(jnp.float32), axis=0)
    scale = lax.rsqrt((total[:, 2 * local] + total[:, 2 * local + 1]) / D + 1e-05)[:, None]
    gate = total[:, :local] * scale
    up = total[:, local : 2 * local] * scale
    hidden = (jax.nn.silu(gate) * up).astype(jnp.bfloat16)

    groups = [[t * n_wide + w for w in block for t in range(n_tok)] for block in blocks]
    hidden = spread(hidden, n_tok * 4, ("tok", "wide"), groups)
    hidden = spread(hidden, 2, "var").reshape(2, 4, n_tok * rows, local)
    total_rows = 2 * n_tok * rows

    var_kept = kept[0]
    block = var_kept.shape[0] // n_wide
    names = []
    drops = []
    for i in range(2):
        pair = (row // 2 * 2 + i) * (SIDE // 2) + col // 2
        name = lax.dynamic_slice_in_dim(var_kept, pair * 2 * block, 2 * block) - pair * 2 * local
        names.append(name)
        matches = jnp.arange(2 * local, dtype=jnp.int32)[:, None] == name[None, :]
        drops.append(jnp.where(jnp.any(matches, axis=1), 0.0, 1.0).astype(jnp.bfloat16))
    names = jnp.stack(names)[:, :, None]
    drop = jnp.concatenate(drops).reshape(4, 1, local)

    n_blocks = n_wide // 4
    product_flops = 2 * total_rows * 4 * local * quarter
    shares = call(
        residual_kernel,
        jax.ShapeDtypeStruct((2, total_rows // 2, quarter), jnp.bfloat16),
        [SMEM] + [VMEM] * 6,
        product_flops,
        4 * total_rows * quarter,
    )(slot.reshape(1), hidden, drop, *downs)
    shares = shares.reshape(n_blocks, total_rows // n_blocks, quarter)
    strides = stride_groups()
    shares = lax.all_to_all(shares, "wide", 0, 0, axis_index_groups=strides)
    piece = jnp.sum(shares.astype(jnp.float32), axis=0).astype(jnp.bfloat16)
    rounded = spread(piece, n_blocks, "wide", strides).reshape(total_rows, quarter)

    chosen = call(
        select_kernel,
        jax.ShapeDtypeStruct((2, 2 * block, total_rows), jnp.bfloat16),
        [VMEM] * 2,
        4 * total_rows * local * 4 * block,
        4 * total_rows * local,
    )(names, hidden)
    factor = 1.0 / math.sqrt(total_rows)
    grad, errors = call(
        functools.partial(gradient_kernel, factor),
        (
            jax.ShapeDtypeStruct((4, block, quarter), jnp.bfloat16),
            jax.ShapeDtypeStruct((1, 128), jnp.float32),
        ),
        [VMEM] * 2,
        2 * total_rows * 4 * block * quarter,
        4 * total_rows * quarter,
    )(chosen, rounded)

    for axis, count, flip in (("tok", n_tok, 1), ("tok", n_tok, 2), ("wide", n_wide, 1), ("wide", n_wide, SIDE)):
        errors = errors + lax.ppermute(errors, axis, [(i, i ^ flip) for i in range(count)])
    loss = jnp.sum(errors) / (total_rows * D)

    swapped = lax.all_to_all(grad, "wide", 0, 0, axis_index_groups=blocks)
    grad = call(
        interleave_kernel,
        jax.ShapeDtypeStruct((block, 4 * quarter), jnp.bfloat16),
        [VMEM],
        0,
        4 * block * quarter,
    )(swapped)
    return (loss.reshape(1), grad[None])


def solution(mesh):
    in_specs = (
        P("wide", "tok"),
        P("tok"),
        P("tok", "wide"),
        P("tok", "wide"),
        P("wide", "tok"),
        P("var", None),
    )
    out_specs = (P("var"), P("var", "wide", "tok"))
    return jax.shard_map(
        per_device, mesh=mesh, in_specs=in_specs, out_specs=out_specs, check_vma=False
    )
```

time: 198 us -> 190 us (0.960)
  blocking collectives: 60.1 us -> 42.2 us
  starting transfers between devices: 41 us -> 58.2 us
  local copies, waits for them, and re-layouts: 26.3 us -> 10.9 us
  waiting for transfers between devices: 52.8 us -> 65.6 us
  Pallas kernels: 0 us -> 5.45 us
  matrix products: 6.47 us -> 1.09 us
  between operations: 5.94 us -> 2.8 us
    psum x1 -> x0, blocking collectives: 14.1 us -> none  [per_device(): error_sum = lax.psum(jnp.sum(errors * errors), 'tok')]
    all_to_all x3, waiting for transfers between devices: 39.9 us -> 52.3 us  [spread(): return lax.all_to_all(stacked, axes, 0, 0, axis_index_groups=groups)]
    ppermute x3 -> x7, starting transfers between devices: 9.2 us -> 19.1 us  [the longest x4 9.86 us: per_device(): lax.ppermute(errors, axis, [(i, i ^ flip) for i in range(count)])]
    ppermute x3 -> x7, waiting for transfers between devices: 5.53 us -> 13.3 us  [the longest x4 13.3 us: per_device(): lax.ppermute(errors, axis, [(i, i ^ flip) for i in range(count)])]
    all_to_all x1, waiting for transfers between devices: 7.38 us -> 0.01 us  [per_device(): swapped = lax.all_to_all(grad, 'wide', 0, 0, axis_index_groups=blocks)]
    all_to_all x1, starting transfers between devices: 4.29 us -> 11 us  [per_device(): swapped = lax.all_to_all(grad, 'wide', 0, 0, axis_index_groups=blocks)]
    select_n x2 -> x0, local copies, waits for them, and re-layouts: 6.3 us -> none  [per_device(): jnp.where(jnp.concatenate(masks)[None, :], jnp.zeros((), jnp.bfloat16), h...]
    pallas_call x0 -> x4, Pallas kernels: none -> 5.45 us  [the longest x1 2.39 us: per_device(): call(functools.partial(gradient_kernel, factor), (jax.ShapeDtypeStruct((4...]
  transfers between devices with their start and end apart: 7 -> 11, of which waited for: 5 -> 7; matrix products, arithmetic and copies ran while one was open for 7% -> 1% of each run, Pallas kernels for 0% -> 0%
where the time goes in v2:
time: 190 us; the launch traced here: 189 us
  waiting for transfers between devices  65.6 us (35%)
  starting transfers between devices  58.2 us (31%)
  blocking collectives  42.2 us (22%)
  local copies, waits for them, and re-layouts  10.9 us (6%)
  Pallas kernels  5.45 us (3%)
  other arithmetic  2.93 us (2%)
  between operations  2.8 us (1%)
    all_to_all x3, waiting for transfers between devices, spread(): return lax.all_to_all(stacked, axes, 0, 0, axis_index_groups=groups)  52.3 us
    all_to_all x3, starting transfers between devices, spread(): return lax.all_to_all(stacked, axes, 0, 0, axis_index_groups=groups)  28.1 us
    all_to_all x1, blocking collectives, per_device(): shares = lax.all_to_all(shares, 'wide', 0, 0, axis_index_groups=strides)  25.6 us
    ppermute x4, waiting for transfers between devices, per_device(): lax.ppermute(errors, axis, [(i, i ^ flip) for i in range(count)])  13.3 us
    all_to_all x1, blocking collectives, per_device(): lax.all_to_all(partial.reshape(n_tok, rows, 2 * local + 128), 'tok', 0, 0)  11.5 us
    all_to_all x1, starting transfers between devices, per_device(): swapped = lax.all_to_all(grad, 'wide', 0, 0, axis_index_groups=blocks)  11 us
    ppermute x4, starting transfers between devices, per_device(): lax.ppermute(errors, axis, [(i, i ^ flip) for i in range(count)])  9.86 us
    ppermute x3, starting transfers between devices, per_device(): downs[k] = lax.ppermute(downs[k], 'wide', perm)  9.2 us
  transfers between devices with their start and end apart: 11, of which 7 were waited for; matrix products, arithmetic and copies ran while one was open for 1% of the time, Pallas kernels for 0%

profile of v2, /device:TPU:8, one launch (start us, length us, event | category | flops | bytes accessed | tf_op | source)
XLA Modules:
  0.0 189.2 jit_solution(1096239704177315702)
XLA Ops:
  0.6 0.0 copy-start
  0.7 0.9 constant_dynamic-slice_fusion.4
  1.5 1.5 broadcast_in_dim.43
  3.0 16.6 %all-to-all-start = ((bf16[64,4,2048]{2,1,0:T(4,128)(2,1)}), bf16[64,4,2048]{2,1,0:T(4,128)(2,1)S(1)}, u32[]{:S(2)}, u32[]{:S(2)}) async-start(bf16[64,4,2048]{2,1,0:T(4,128)(2,1)} %broadcast_in_dim.43), calls=%async_computation | async-start | bytes 2097152 | tf_op jit(solution)/shard_map/all_to_all | solution.py:33
  19.7 29.3 %all-to-all-done = bf16[64,4,2048]{2,1,0:T(4,128)(2,1)S(1)} async-done(((bf16[64,4,2048]{2,1,0:T(4,128)(2,1)}), bf16[64,4,2048]{2,1,0:T(4,128)(2,1)S(1)}, u32[]{:S(2)}, u32[]{:S(2)}) %all-to-all-start) | async-done | bytes 1048608 | tf_op jit(solution)/shard_map/all_to_all | solution.py:33
  49.0 0.6 multiply_reduce_fusion
  49.6 0.1 reduce_sum.42
  49.7 0.2 copy-done.7
  50.0 1.3 reshape.92
  51.3 0.0 copy-start.8
  51.3 0.5 convolution_convert_fusion
  51.9 0.8 copy-done.8
  52.6 0.5 convolution_convert_fusion.1
  53.2 0.1 select_select_fusion
  53.3 0.6 copy-done.9
  54.0 1.0 constant_dynamic-slice_fusion
  54.9 2.2 %collective-permute-start = (bf16[320,512]{1,0:T(8,128)(2,1)}, bf16[320,512]{1,0:T(8,128)(2,1)S(1)}, u32[]{:S(2)}, u32[]{:S(2)}) collective-permute-start(bf16[320,512]{1,0:T(8,128)(2,1)} %get-tuple-element.26), channel_id=1, source_target_pairs={{0,1},{1,0},{2,3},{3,2},{4,5},{5,4},{6,7},{7,6},{8,9},{9,8},{10,11... | collective-permute-start | bytes 983048 | tf_op jit(solution)/shard_map/ppermute | solution.py:148
  57.1 2.4 %collective-permute-start.1 = (bf16[320,512]{1,0:T(8,128)(2,1)}, bf16[320,512]{1,0:T(8,128)(2,1)S(1)}, u32[]{:S(2)}, u32[]{:S(2)}) collective-permute-start(bf16[320,512]{1,0:T(8,128)(2,1)} %get-tuple-element.25), channel_id=1, source_target_pairs={{0,8},{1,9},{2,10},{3,11},{4,12},{5,13},{6,14},{7,15},{8,0},{9,1},... | collective-permute-start | bytes 983048 | tf_op jit(solution)/shard_map/ppermute | solution.py:148
  59.5 4.6 %collective-permute-start.2 = (bf16[320,512]{1,0:T(8,128)(2,1)}, bf16[320,512]{1,0:T(8,128)(2,1)S(1)}, u32[]{:S(2)}, u32[]{:S(2)}) collective-permute-start(bf16[320,512]{1,0:T(8,128)(2,1)} %get-tuple-element.24), channel_id=1, source_target_pairs={{0,9},{1,8},{2,11},{3,10},{4,13},{5,12},{6,15},{7,14},{8,1},{9,0},... | collective-permute-start | bytes 983048 | tf_op jit(solution)/shard_map/ppermute | solution.py:148
  64.1 0.2 copy.29
  64.3 11.5 %all_to_all.35 = bf16[4,64,768]{2,1,0:T(8,128)(2,1)S(1)} all-to-all(bf16[4,64,768]{2,1,0:T(8,128)(2,1)S(1)} %bitcast.14), channel_id=1, replica_groups=mesh['var'=2,'tok'=4,'wide'=64] {'tok'}, dimensions={0} | all-to-all | bytes 786432 | tf_op jit(solution)/shard_map/all_to_all | solution.py:150
  75.8 0.0 collective-permute-done.down1
  75.8 0.0 collective-permute-done.1.down2
  75.8 0.0 collective-permute-done.2.down3
  75.8 0.0 copy-start.5
  75.8 0.1 convert_reduce_fusion
  75.9 0.2 fusion.7
  76.1 0.1 fusion.3
  76.2 1.0 broadcast_in_dim.73
  77.2 0.0 copy-done.3
  77.2 4.1 %all-to-all-start.2 = ((bf16[16,64,320]{2,1,0:T(8,128)(2,1)}), bf16[16,64,320]{2,1,0:T(8,128)(2,1)S(1)}, u32[]{:S(2)}, u32[]{:S(2)}) async-start(bf16[16,64,320]{2,1,0:T(8,128)(2,1)} %broadcast_in_dim.73), calls=%async_computation.2 | async-start | bytes 1572864 | tf_op jit(solution)/shard_map/all_to_all | solution.py:33
  81.3 0.8 fusion.11
  82.1 0.3 fusion
  82.4 0.1 convert_element_type.81
  82.5 0.1 convert_element_type.82
  82.6 8.5 %all-to-all-done.2 = bf16[16,64,320]{2,1,0:T(8,128)(2,1)S(1)} async-done(((bf16[16,64,320]{2,1,0:T(8,128)(2,1)}), bf16[16,64,320]{2,1,0:T(8,128)(2,1)S(1)}, u32[]{:S(2)}, u32[]{:S(2)}) %all-to-all-start.2) | async-done | bytes 655392 | tf_op jit(solution)/shard_map/all_to_all | solution.py:33
  91.2 0.3 broadcast_in_dim.74
  91.4 0.0 copy-start.6
  91.5 5.1 %all_to_all.36 = bf16[2,16,64,320]{3,2,1,0:T(8,128)(2,1)S(1)} all-to-all(bf16[2,16,64,320]{3,2,1,0:T(8,128)(2,1)S(1)} %broadcast_in_dim.74), channel_id=1, replica_groups=mesh['var'=2,'tok'=4,'wide'=64] {'var'}, dimensions={0} | all-to-all | bytes 2621440 | tf_op jit(solution)/shard_map/all_to_all | solution.py:33
  96.6 0.0 copy-done.6
  96.6 1.2 shard_map.78
  97.8 25.6 %all_to_all.37 = bf16[16,32,512]{2,1,0:T(8,128)(2,1)S(1)} all-to-all(bf16[16,32,512]{2,1,0:T(8,128)(2,1)S(1)} %bitcast.13), channel_id=1, replica_groups={{0,2,4,6,16,18,20,22,32,34,36,38,48,50,52,54},{1,3,5,7,17,19,21,23,33,3..., dimensions={0} | all-to-all | bytes 1048576 | tf_op jit(solution)/shard_map/all_to_all | solution.py:187
  123.4 0.1 reduce_sum.44
  123.5 0.8 broadcast_in_dim.77
  124.3 7.4 %all-to-all-start.5 = ((bf16[16,32,512]{2,1,0:T(8,128)(2,1)}), bf16[16,32,512]{2,1,0:T(8,128)(2,1)}, u32[]{:S(2)}, u32[]{:S(2)}) async-start(bf16[16,32,512]{2,1,0:T(8,128)(2,1)} %broadcast_in_dim.77), calls=%async_computation.5 | async-start | bytes 1048576 | tf_op jit(solution)/shard_map/all_to_all | solution.py:33
  131.8 0.2 copy.30.names_ref
  131.9 0.9 shard_map.77.chosen_ref
  132.9 0.0 copy-start.1
  132.9 0.8 copy-done.1
  133.7 14.4 %all-to-all-done.5 = bf16[16,32,512]{2,1,0:T(8,128)(2,1)} async-done(((bf16[16,32,512]{2,1,0:T(8,128)(2,1)}), bf16[16,32,512]{2,1,0:T(8,128)(2,1)}, u32[]{:S(2)}, u32[]{:S(2)}) %all-to-all-start.5) | async-done | bytes 524320 | tf_op jit(solution)/shard_map/all_to_all | solution.py:33
  148.2 1.1 copy-done.2
  149.3 2.4 %shard_map.79 = (bf16[4,160,512]{2,1,0:T(8,128)(2,1)}, f32[1,128]{1,0:T(1,128)S(1)}) custom-call(bf16[2,320,512]{2,1,0:T(8,128)(2,1)S(1)} %copy-done.2, bf16[512,512]{1,0:T(8,128)(2,1)} %bitcast.5.rounded_ref), custom_call_target="tpu_custom_call" | custom-call | flops 335544320 | bytes 1048576 | tf_op jit(solution)/shard_map/pallas_call | solution.py:199
  151.7 11.0 %all-to-all-start.6 = ((bf16[4,160,512]{2,1,0:T(8,128)(2,1)}), bf16[4,160,512]{2,1,0:T(8,128)(2,1)S(1)}, u32[]{:S(2)}, u32[]{:S(2)}) async-start(bf16[4,160,512]{2,1,0:T(8,128)(2,1)} %get-tuple-element.19), calls=%async_computation.6 | async-start | bytes 1310720 | tf_op jit(solution)/shard_map/all_to_all | solution.py:214
  162.7 2.6 %collective-permute-start.3 = (f32[1,128]{1,0:T(1,128)S(1)}, f32[1,128]{1,0:T(1,128)S(1)}, u32[]{:S(2)}, u32[]{:S(2)}) collective-permute-start(f32[1,128]{1,0:T(1,128)S(1)} %get-tuple-element.18), channel_id=1, source_target_pairs={{0,64},{64,0},{128,192},{192,128},{1,65},{65,1},{129,193},{193,129... | collective-permute-start | bytes 1544 | tf_op jit(solution)/shard_map/ppermute | solution.py:211
  165.3 2.8 %collective-permute-done.3 = f32[1,128]{1,0:T(1,128)S(1)} collective-permute-done((f32[1,128]{1,0:T(1,128)S(1)}, f32[1,128]{1,0:T(1,128)S(1)}, u32[]{:S(2)}, u32[]{:S(2)}) %collective-permute-start.3) | collective-permute-done | bytes 544 | tf_op jit(solution)/shard_map/ppermute | solution.py:211
  168.1 1.9 %collective-permute-start.4 = (f32[1,128]{1,0:T(1,128)S(1)}, f32[1,128]{1,0:T(1,128)S(1)}, u32[]{:S(2)}, u32[]{:S(2)}) collective-permute-start(f32[1,128]{1,0:T(1,128)S(1)} %add.91), channel_id=1, source_target_pairs={{0,128},{64,192},{128,0},{192,64},{1,129},{65,193},{129,1},{193,65... | collective-permute-start | bytes 1544 | tf_op jit(solution)/shard_map/ppermute | solution.py:211
  170.0 5.0 %collective-permute-done.4 = f32[1,128]{1,0:T(1,128)S(1)} collective-permute-done((f32[1,128]{1,0:T(1,128)S(1)}, f32[1,128]{1,0:T(1,128)S(1)}, u32[]{:S(2)}, u32[]{:S(2)}) %collective-permute-start.4) | collective-permute-done | bytes 544 | tf_op jit(solution)/shard_map/ppermute | solution.py:211
  175.0 3.4 %collective-permute-start.5 = (f32[1,128]{1,0:T(1,128)S(1)}, f32[1,128]{1,0:T(1,128)S(1)}, u32[]{:S(2)}, u32[]{:S(2)}) collective-permute-start(f32[1,128]{1,0:T(1,128)S(1)} %add.92), channel_id=1, source_target_pairs={{0,1},{1,0},{2,3},{3,2},{4,5},{5,4},{6,7},{7,6},{8,9},{9,8},{10,11... | collective-permute-start | bytes 1544 | tf_op jit(solution)/shard_map/ppermute | solution.py:211
  178.4 2.1 %collective-permute-done.5 = f32[1,128]{1,0:T(1,128)S(1)} collective-permute-done((f32[1,128]{1,0:T(1,128)S(1)}, f32[1,128]{1,0:T(1,128)S(1)}, u32[]{:S(2)}, u32[]{:S(2)}) %collective-permute-start.5) | collective-permute-done | bytes 544 | tf_op jit(solution)/shard_map/ppermute | solution.py:211
  180.5 1.9 %collective-permute-start.6 = (f32[1,128]{1,0:T(1,128)S(1)}, f32[1,128]{1,0:T(1,128)S(1)}, u32[]{:S(2)}, u32[]{:S(2)}) collective-permute-start(f32[1,128]{1,0:T(1,128)S(1)} %add.93), channel_id=1, source_target_pairs={{0,8},{1,9},{2,10},{3,11},{4,12},{5,13},{6,14},{7,15},{8,0},{9,1},... | collective-permute-start | bytes 1544 | tf_op jit(solution)/shard_map/ppermute | solution.py:211
  182.4 3.5 %collective-permute-done.6 = f32[1,128]{1,0:T(1,128)S(1)} collective-permute-done((f32[1,128]{1,0:T(1,128)S(1)}, f32[1,128]{1,0:T(1,128)S(1)}, u32[]{:S(2)}, u32[]{:S(2)}) %collective-permute-start.6) | collective-permute-done | bytes 544 | tf_op jit(solution)/shard_map/ppermute | solution.py:211
  185.9 0.6 add_reduce_fusion
  187.1 0.0 all-to-all-done.6.in_ref
  187.1 0.9 shard_map.80
  (20 shorter events, 0.1 us)
Async XLA Ops:
  0.6 50.7 %copy-start = (bf16[2048,320]{0,1:T(8,128)(2,1)S(1)}, bf16[2048,320]{0,1:T(8,128)(2,1)}, u32[]{:S(2)}) copy-start(bf16[2048,320]{0,1:T(8,128)(2,1)} %param.9) | copy-start | bytes 3932164
  3.0 46.0 %all-to-all-start = ((bf16[64,4,2048]{2,1,0:T(4,128)(2,1)}), bf16[64,4,2048]{2,1,0:T(4,128)(2,1)S(1)}, u32[]{:S(2)}, u32[]{:S(2)}) async-start(bf16[64,4,2048]{2,1,0:T(4,128)(2,1)} %broadcast_in_dim.43), calls=%async_computation | async-start | bytes 2097152 | tf_op jit(solution)/shard_map/all_to_all | solution.py:33
  49.0 1.0 copy-start.7
  50.0 1.3 copy-start.10
  51.3 1.3 copy-start.8
  52.6 1.3 copy-start.9
  54.9 20.9 %collective-permute-start = (bf16[320,512]{1,0:T(8,128)(2,1)}, bf16[320,512]{1,0:T(8,128)(2,1)S(1)}, u32[]{:S(2)}, u32[]{:S(2)}) collective-permute-start(bf16[320,512]{1,0:T(8,128)(2,1)} %get-tuple-element.26), channel_id=1, source_target_pairs={{0,1},{1,0},{2,3},{3,2},{4,5},{5,4},{6,7},{7,6},{8,9},{9,8},{10,11... | collective-permute-start | bytes 983048 | tf_op jit(solution)/shard_map/ppermute | solution.py:148
  57.1 18.7 %collective-permute-start.1 = (bf16[320,512]{1,0:T(8,128)(2,1)}, bf16[320,512]{1,0:T(8,128)(2,1)S(1)}, u32[]{:S(2)}, u32[]{:S(2)}) collective-permute-start(bf16[320,512]{1,0:T(8,128)(2,1)} %get-tuple-element.25), channel_id=1, source_target_pairs={{0,8},{1,9},{2,10},{3,11},{4,12},{5,13},{6,14},{7,15},{8,0},{9,1},... | collective-permute-start | bytes 983048 | tf_op jit(solution)/shard_map/ppermute | solution.py:148
  59.5 16.3 %collective-permute-start.2 = (bf16[320,512]{1,0:T(8,128)(2,1)}, bf16[320,512]{1,0:T(8,128)(2,1)S(1)}, u32[]{:S(2)}, u32[]{:S(2)}) collective-permute-start(bf16[320,512]{1,0:T(8,128)(2,1)} %get-tuple-element.24), channel_id=1, source_target_pairs={{0,9},{1,8},{2,11},{3,10},{4,13},{5,12},{6,15},{7,14},{8,1},{9,0},... | collective-permute-start | bytes 983048 | tf_op jit(solution)/shard_map/ppermute | solution.py:148
  75.8 1.4 copy-start.3
  75.8 1.4 copy-start.5
  77.2 14.0 %all-to-all-start.2 = ((bf16[16,64,320]{2,1,0:T(8,128)(2,1)}), bf16[16,64,320]{2,1,0:T(8,128)(2,1)S(1)}, u32[]{:S(2)}, u32[]{:S(2)}) async-start(bf16[16,64,320]{2,1,0:T(8,128)(2,1)} %broadcast_in_dim.73), calls=%async_computation.2 | async-start | bytes 1572864 | tf_op jit(solution)/shard_map/all_to_all | solution.py:33
  91.4 5.2 %copy-start.4 = (bf16[320,512]{1,0:T(8,128)(2,1)S(1)}, bf16[320,512]{1,0:T(8,128)(2,1)}, u32[]{:S(2)}) copy-start(bf16[320,512]{1,0:T(8,128)(2,1)} %copy-done.3) | copy-start | bytes 983044
  91.4 5.1 %copy-start.6 = (bf16[320,512]{1,0:T(8,128)(2,1)S(1)}, bf16[320,512]{1,0:T(8,128)(2,1)}, u32[]{:S(2)}) copy-start(bf16[320,512]{1,0:T(8,128)(2,1)} %copy-done.5) | copy-start | bytes 983044
  124.3 23.8 %all-to-all-start.5 = ((bf16[16,32,512]{2,1,0:T(8,128)(2,1)}), bf16[16,32,512]{2,1,0:T(8,128)(2,1)}, u32[]{:S(2)}, u32[]{:S(2)}) async-start(bf16[16,32,512]{2,1,0:T(8,128)(2,1)} %broadcast_in_dim.77), calls=%async_computation.5 | async-start | bytes 1048576 | tf_op jit(solution)/shard_map/all_to_all | solution.py:33
  132.9 0.8 copy-start.1
  148.2 1.1 copy-start.2
  151.7 35.5 %all-to-all-start.6 = ((bf16[4,160,512]{2,1,0:T(8,128)(2,1)}), bf16[4,160,512]{2,1,0:T(8,128)(2,1)S(1)}, u32[]{:S(2)}, u32[]{:S(2)}) async-start(bf16[4,160,512]{2,1,0:T(8,128)(2,1)} %get-tuple-element.19), calls=%async_computation.6 | async-start | bytes 1310720 | tf_op jit(solution)/shard_map/all_to_all | solution.py:214
  162.7 5.4 %collective-permute-start.3 = (f32[1,128]{1,0:T(1,128)S(1)}, f32[1,128]{1,0:T(1,128)S(1)}, u32[]{:S(2)}, u32[]{:S(2)}) collective-permute-start(f32[1,128]{1,0:T(1,128)S(1)} %get-tuple-element.18), channel_id=1, source_target_pairs={{0,64},{64,0},{128,192},{192,128},{1,65},{65,1},{129,193},{193,129... | collective-permute-start | bytes 1544 | tf_op jit(solution)/shard_map/ppermute | solution.py:211
  168.1 6.9 %collective-permute-start.4 = (f32[1,128]{1,0:T(1,128)S(1)}, f32[1,128]{1,0:T(1,128)S(1)}, u32[]{:S(2)}, u32[]{:S(2)}) collective-permute-start(f32[1,128]{1,0:T(1,128)S(1)} %add.91), channel_id=1, source_target_pairs={{0,128},{64,192},{128,0},{192,64},{1,129},{65,193},{129,1},{193,65... | collective-permute-start | bytes 1544 | tf_op jit(solution)/shard_map/ppermute | solution.py:211
  175.0 5.4 %collective-permute-start.5 = (f32[1,128]{1,0:T(1,128)S(1)}, f32[1,128]{1,0:T(1,128)S(1)}, u32[]{:S(2)}, u32[]{:S(2)}) collective-permute-start(f32[1,128]{1,0:T(1,128)S(1)} %add.92), channel_id=1, source_target_pairs={{0,1},{1,0},{2,3},{3,2},{4,5},{5,4},{6,7},{7,6},{8,9},{9,8},{10,11... | collective-permute-start | bytes 1544 | tf_op jit(solution)/shard_map/ppermute | solution.py:211
  180.5 5.4 %collective-permute-start.6 = (f32[1,128]{1,0:T(1,128)S(1)}, f32[1,128]{1,0:T(1,128)S(1)}, u32[]{:S(2)}, u32[]{:S(2)}) collective-permute-start(f32[1,128]{1,0:T(1,128)S(1)} %add.93), channel_id=1, source_target_pairs={{0,8},{1,9},{2,10},{3,11},{4,12},{5,13},{6,14},{7,15},{8,0},{9,1},... | collective-permute-start | bytes 1544 | tf_op jit(solution)/shard_map/ppermute | solution.py:211

commit v3 on v2

--- a/solution.py
+++ b/solution.py
@@ -31,11 +31,6 @@
 def spread(shard, count, axes, groups=None):
     stacked = jnp.broadcast_to(shard[None], (count,) + shard.shape)
     return lax.all_to_all(stacked, axes, 0, 0, axis_index_groups=groups)
-
-
-def hi_lo(value):
-    hi = lax.reduce_precision(value, 8, 7)
-    return hi.astype(jnp.bfloat16), (value - hi).astype(jnp.bfloat16)
 
 
 VMEM = pl.BlockSpec(memory_space=pltpu.VMEM)
@@ -54,38 +49,37 @@
     )
 
 
-def residual_kernel(slot_ref, hidden_ref, drop_ref, down0, down1, down2, down3, out_ref):
+def residual_kernel(slot_ref, own_ref, other_ref, drop_ref, down0, down1, down2, down3, out_ref):
     slot = slot_ref[0]
     downs = (down0, down1, down2, down3)
-    for core in range(2):
+    for half, hidden_ref in enumerate((own_ref, other_ref)):
         total = None
         for k in range(4):
             index = slot ^ k
-            units = hidden_ref[core, index] * drop_ref[index]
+            units = hidden_ref[index] * drop_ref[index]
             term = jnp.dot(units, downs[k][...], preferred_element_type=jnp.float32)
             total = term if total is None else total + term
-        out_ref[core] = (-total).astype(out_ref.dtype)
-
-
-def select_kernel(names_ref, hidden_ref, out_ref):
-    local = hidden_ref.shape[3]
-    rows = hidden_ref.shape[2]
+        out_ref[half] = (-total).astype(out_ref.dtype)
+
+
+def select_kernel(names_ref, own_ref, other_ref, out_ref):
+    rows, local = own_ref.shape[1:]
     count = names_ref.shape[1]
     for pair in range(2):
         names = names_ref[pair]
-        for core in range(2):
+        for half, hidden_ref in enumerate((own_ref, other_ref)):
             total = None
             for i in range(2):
                 units = lax.broadcasted_iota(jnp.int32, (count, local), 1) + i * local
                 picker = jnp.where(units == names, 1.0, 0.0).astype(jnp.bfloat16)
                 term = lax.dot_general(
                     picker,
-                    hidden_ref[core, 2 * pair + i],
+                    hidden_ref[2 * pair + i],
                     (((1,), (1,)), ((), ())),
                     preferred_element_type=jnp.float32,
                 )
                 total = term if total is None else total + term
-            out_ref[pair, :, core * rows : (core + 1) * rows] = total.astype(out_ref.dtype)
+            out_ref[pair, :, half * rows : (half + 1) * rows] = total.astype(out_ref.dtype)
 
 
 def gradient_kernel(factor, chosen_ref, rounded_ref, grad_ref, error_ref):
@@ -127,14 +121,11 @@
     widths = gathered.astype(jnp.float32)
     squares = jnp.sum(widths * widths, axis=1)
     gained = (widths * norm_gain[None, :]).astype(jnp.bfloat16)
-    sq_hi, sq_lo = hi_lo(squares)
-    lanes = lax.broadcasted_iota(jnp.int32, (n_wide * half, 128), 1)
-    extra = jnp.where(lanes == 0, sq_hi[:, None], jnp.where(lanes == 1, sq_lo[:, None], jnp.zeros((), jnp.bfloat16)))
     partial = jnp.concatenate(
         [
-            jnp.dot(gained, gate_parent, preferred_element_type=jnp.float32).astype(jnp.bfloat16),
-            jnp.dot(gained, up_parent, preferred_element_type=jnp.float32).astype(jnp.bfloat16),
-            extra,
+            jnp.dot(gained, gate_parent, preferred_element_type=jnp.float32),
+            jnp.dot(gained, up_parent, preferred_element_type=jnp.float32),
+            jnp.broadcast_to(squares[:, None], (n_wide * half, 128)),
         ],
         axis=1,
     )
@@ -149,15 +140,16 @@
 
     scattered = lax.all_to_all(partial.reshape(n_tok, rows, 2 * local + 128), "tok", 0, 0)
     scattered, *downs = lax.optimization_barrier((scattered, *downs))
-    total = jnp.sum(scattered.astype(jnp.float32), axis=0)
-    scale = lax.rsqrt((total[:, 2 * local] + total[:, 2 * local + 1]) / D + 1e-05)[:, None]
+    total = jnp.sum(scattered, axis=0)
+    scale = lax.rsqrt(total[:, 2 * local :][:, :1] / D + 1e-05)
     gate = total[:, :local] * scale
     up = total[:, local : 2 * local] * scale
     hidden = (jax.nn.silu(gate) * up).astype(jnp.bfloat16)
 
     groups = [[t * n_wide + w for w in block for t in range(n_tok)] for block in blocks]
     hidden = spread(hidden, n_tok * 4, ("tok", "wide"), groups)
-    hidden = spread(hidden, 2, "var").reshape(2, 4, n_tok * rows, local)
+    hidden = hidden.reshape(4, n_tok * rows, local)
+    other = lax.ppermute(hidden, "var", [(0, 1), (1, 0)])
     total_rows = 2 * n_tok * rows
 
     var_kept = kept[0]
@@ -178,10 +170,10 @@
     shares = call(
         residual_kernel,
         jax.ShapeDtypeStruct((2, total_rows // 2, quarter), jnp.bfloat16),
-        [SMEM] + [VMEM] * 6,
+        [SMEM] + [VMEM] * 7,
         product_flops,
         4 * total_rows * quarter,
-    )(slot.reshape(1), hidden, drop, *downs)
+    )(slot.reshape(1), hidden, other, drop, *downs)
     shares = shares.reshape(n_blocks, total_rows // n_blocks, quarter)
     strides = stride_groups()
     shares = lax.all_to_all(shares, "wide", 0, 0, axis_index_groups=strides)
@@ -191,10 +183,10 @@
     chosen = call(
         select_kernel,
         jax.ShapeDtypeStruct((2, 2 * block, total_rows), jnp.bfloat16),
-        [VMEM] * 2,
+        [VMEM] * 3,
         4 * total_rows * local * 4 * block,
         4 * total_rows * local,
-    )(names, hidden)
+    )(names, hidden, other)
     factor = 1.0 / math.sqrt(total_rows)
     grad, errors = call(
         functools.partial(gradient_kernel, factor),
@@ -207,8 +199,7 @@
         4 * total_rows * quarter,
     )(chosen, rounded)
 
-    for axis, count, flip in (("tok", n_tok, 1), ("tok", n_tok, 2), ("wide", n_wide, 1), ("wide", n_wide, SIDE)):
-        errors = errors + lax.ppermute(errors, axis, [(i, i ^ flip) for i in range(count)])
+    errors = lax.psum(lax.psum(errors, "tok"), "wide", axis_index_groups=blocks)
     loss = jnp.sum(errors) / (total_rows * D)
 
     swapped = lax.all_to_all(grad, "wide", 0, 0, axis_index_groups=blocks)

time: 190 us -> 196 us (1.032)
  the two profiles are of different devices: /device:TPU:8 before, /device:TPU:2 now
where the time goes in v3:
time: 196 us; the launch traced here: 195 us
  blocking collectives  96.1 us (49%)
  waiting for transfers between devices  39.1 us (20%)
  starting transfers between devices  29.8 us (15%)
  local copies, waits for them, and re-layouts  13.1 us (7%)
  other arithmetic  6.31 us (3%)
  Pallas kernels  5.44 us (3%)
  between operations  2.65 us (1%)
  matrix products  2.55 us (1%)
    all_to_all x1, blocking collectives, spread(): return lax.all_to_all(stacked, axes, 0, 0, axis_index_groups=groups)  46.1 us
    all_to_all x1, blocking collectives, per_device(): shares = lax.all_to_all(shares, 'wide', 0, 0, axis_index_groups=strides)  29.9 us
    all_to_all x2, waiting for transfers between devices, spread(): return lax.all_to_all(stacked, axes, 0, 0, axis_index_groups=groups)  28.8 us
    psum x2, blocking collectives, per_device(): errors = lax.psum(lax.psum(errors, 'tok'), 'wide', axis_index_groups=blocks)  20.1 us
    all_to_all x2, starting transfers between devices, spread(): return lax.all_to_all(stacked, axes, 0, 0, axis_index_groups=groups)  10.3 us
    ppermute x3, starting transfers between devices, per_device(): downs[k] = lax.ppermute(downs[k], 'wide', perm)  9.21 us
    ppermute x3, waiting for transfers between devices, per_device(): downs[k] = lax.ppermute(downs[k], 'wide', perm)  8.68 us
    all_to_all x1, starting transfers between devices, per_device(): lax.all_to_all(partial.reshape(n_tok, rows, 2 * local + 128), 'tok', 0, 0)  4.82 us
  transfers between devices with their start and end apart: 8, of which 6 were waited for; matrix products, arithmetic and copies ran while one was open for 2% of the time, Pallas kernels for 0%

profile of v3, /device:TPU:2, one launch (start us, length us, event | category | flops | bytes accessed | tf_op | source)
XLA Modules:
  0.0 195.1 jit_solution(10547684613867843138)
XLA Ops:
  0.6 0.0 copy-start
  0.7 0.9 constant_dynamic-slice_fusion.4
  1.5 0.5 broadcast_in_dim.25
  2.0 0.0 copy-start.9
  2.0 46.1 %all_to_all.30 = bf16[64,4,2048]{2,1,0:T(4,128)(2,1)} all-to-all(bf16[64,4,2048]{2,1,0:T(4,128)(2,1)S(1)} %broadcast_in_dim.25), channel_id=1, replica_groups=mesh['var'=2,'tok'=4,'wide'=64] {'wide'}, dimensions={0} | all-to-all | bytes 2097152 | tf_op jit(solution)/shard_map/all_to_all | solution.py:33
  48.2 1.3 reshape.77
  49.5 0.0 copy-done
  49.5 0.0 copy-done.9
  49.5 0.0 copy-start.8
  49.5 1.3 fusion.2
  50.8 0.0 copy-done.8
  50.8 0.0 copy-start.7
  50.8 1.3 fusion.3
  52.1 0.0 copy-done.7
  52.1 0.6 multiply_reduce_fusion
  52.7 0.1 broadcast_in_dim.26
  52.8 1.1 pad_maximum_fusion
  54.0 1.1 copy.38
  55.1 4.8 %all-to-all-start.1 = ((f32[4,64,768]{2,1,0:T(8,128)}), f32[4,64,768]{2,1,0:T(8,128)S(1)}, u32[]{:S(2)}, u32[]{:S(2)}) async-start(f32[4,64,768]{2,1,0:T(8,128)} %bitcast.1), calls=%async_computation.1 | async-start | bytes 1572864 | tf_op jit(solution)/shard_map/all_to_all | solution.py:141
  59.9 1.4 constant_dynamic-slice_fusion
  61.3 2.0 %collective-permute-start = (bf16[320,512]{1,0:T(8,128)(2,1)S(1)}, bf16[320,512]{1,0:T(8,128)(2,1)S(1)}, u32[]{:S(2)}, u32[]{:S(2)}) collective-permute-start(bf16[320,512]{1,0:T(8,128)(2,1)S(1)} %get-tuple-element.26), channel_id=1, source_target_pairs={{0,1},{1,0},{2,3},{3,2},{4,5},{5,4},{6,7},{7,6},{8,9},{9,8},{10,11... | collective-permute-start | bytes 983048 | tf_op jit(solution)/shard_map/ppermute | solution.py:139
  63.3 3.4 %collective-permute-start.1 = (bf16[320,512]{1,0:T(8,128)(2,1)S(1)}, bf16[320,512]{1,0:T(8,128)(2,1)S(1)}, u32[]{:S(2)}, u32[]{:S(2)}) collective-permute-start(bf16[320,512]{1,0:T(8,128)(2,1)S(1)} %get-tuple-element.25), channel_id=1, source_target_pairs={{0,8},{1,9},{2,10},{3,11},{4,12},{5,13},{6,14},{7,15},{8,0},{9,1},... | collective-permute-start | bytes 983048 | tf_op jit(solution)/shard_map/ppermute | solution.py:139
  66.8 3.7 %collective-permute-start.2 = (bf16[320,512]{1,0:T(8,128)(2,1)S(1)}, bf16[320,512]{1,0:T(8,128)(2,1)S(1)}, u32[]{:S(2)}, u32[]{:S(2)}) collective-permute-start(bf16[320,512]{1,0:T(8,128)(2,1)S(1)} %get-tuple-element.24), channel_id=1, source_target_pairs={{0,9},{1,8},{2,11},{3,10},{4,13},{5,12},{6,15},{7,14},{8,1},{9,0},... | collective-permute-start | bytes 983048 | tf_op jit(solution)/shard_map/ppermute | solution.py:139
  70.5 2.8 %collective-permute-done.down1 = bf16[320,512]{1,0:T(8,128)(2,1)S(1)} collective-permute-done((bf16[320,512]{1,0:T(8,128)(2,1)S(1)}, bf16[320,512]{1,0:T(8,128)(2,1)S(1)}, u32[]{:S(2)}, u32[]{:S(2)}) %collective-permute-start) | collective-permute-done | bytes 327712 | tf_op jit(solution)/shard_map/ppermute | solution.py:139
  73.4 2.1 %collective-permute-done.1.down2 = bf16[320,512]{1,0:T(8,128)(2,1)S(1)} collective-permute-done((bf16[320,512]{1,0:T(8,128)(2,1)S(1)}, bf16[320,512]{1,0:T(8,128)(2,1)S(1)}, u32[]{:S(2)}, u32[]{:S(2)}) %collective-permute-start.1) | collective-permute-done | bytes 327712 | tf_op jit(solution)/shard_map/ppermute | solution.py:139
  75.4 3.8 %collective-permute-done.2.down3 = bf16[320,512]{1,0:T(8,128)(2,1)S(1)} collective-permute-done((bf16[320,512]{1,0:T(8,128)(2,1)S(1)}, bf16[320,512]{1,0:T(8,128)(2,1)S(1)}, u32[]{:S(2)}, u32[]{:S(2)}) %collective-permute-start.2) | collective-permute-done | bytes 327712 | tf_op jit(solution)/shard_map/ppermute | solution.py:139
  79.2 0.0 all-to-all-done.1
  79.2 0.8 reduce_sum.40
  80.0 0.9 fusion.8
  80.9 1.1 fusion.5
  82.0 1.0 broadcast_in_dim.51
  83.0 0.0 copy-done.3
  83.0 0.0 copy-done.5
  83.0 6.1 %all-to-all-start.2 = ((bf16[16,64,320]{2,1,0:T(8,128)(2,1)}), bf16[16,64,320]{2,1,0:T(8,128)(2,1)S(1)}, u32[]{:S(2)}, u32[]{:S(2)}) async-start(bf16[16,64,320]{2,1,0:T(8,128)(2,1)} %broadcast_in_dim.51), calls=%async_computation.2 | async-start | bytes 1572864 | tf_op jit(solution)/shard_map/all_to_all | solution.py:33
  89.1 0.8 fusion.11
  89.8 9.1 %all-to-all-done.2 = bf16[16,64,320]{2,1,0:T(8,128)(2,1)S(1)} async-done(((bf16[16,64,320]{2,1,0:T(8,128)(2,1)}), bf16[16,64,320]{2,1,0:T(8,128)(2,1)S(1)}, u32[]{:S(2)}, u32[]{:S(2)}) %all-to-all-start.2) | async-done | bytes 655392 | tf_op jit(solution)/shard_map/all_to_all | solution.py:33
  98.9 0.3 copy.39
  99.2 1.9 collective-permute-start.3
  101.1 0.3 fusion
  101.4 0.1 convert_element_type.53
  101.5 0.1 convert_element_type.54
  101.6 1.7 collective-permute-done.3
  103.3 1.4 copy.41.other_ref
  104.8 0.0 copy-start.4
  104.8 1.0 copy-done.4
  105.8 1.0 copy-done.6
  106.7 1.2 shard_map.78
  108.0 29.9 %all_to_all.31 = bf16[16,32,512]{2,1,0:T(8,128)(2,1)S(1)} all-to-all(bf16[16,32,512]{2,1,0:T(8,128)(2,1)S(1)} %bitcast.14), channel_id=1, replica_groups={{0,2,4,6,16,18,20,22,32,34,36,38,48,50,52,54},{1,3,5,7,17,19,21,23,33,3..., dimensions={0} | all-to-all | bytes 1048576 | tf_op jit(solution)/shard_map/all_to_all | solution.py:179
  137.8 0.1 reduce_sum.41
  137.9 0.9 broadcast_in_dim.54
  138.8 4.2 %all-to-all-start.4 = ((bf16[16,32,512]{2,1,0:T(8,128)(2,1)}), bf16[16,32,512]{2,1,0:T(8,128)(2,1)}, u32[]{:S(2)}, u32[]{:S(2)}) async-start(bf16[16,32,512]{2,1,0:T(8,128)(2,1)} %broadcast_in_dim.54), calls=%async_computation.4 | async-start | bytes 1048576 | tf_op jit(solution)/shard_map/all_to_all | solution.py:33
  143.0 0.2 copy.40.names_ref
  143.2 0.9 shard_map.77.chosen_ref
  144.2 0.0 copy-start.1
  144.2 0.8 copy-done.1
  145.0 19.7 %all-to-all-done.4 = bf16[16,32,512]{2,1,0:T(8,128)(2,1)} async-done(((bf16[16,32,512]{2,1,0:T(8,128)(2,1)}), bf16[16,32,512]{2,1,0:T(8,128)(2,1)}, u32[]{:S(2)}, u32[]{:S(2)}) %all-to-all-start.4) | async-done | bytes 524320 | tf_op jit(solution)/shard_map/all_to_all | solution.py:33
  164.7 1.1 copy-done.2
  165.8 2.4 %shard_map.79 = (bf16[4,160,512]{2,1,0:T(8,128)(2,1)}, f32[1,128]{1,0:T(1,128)S(1)}) custom-call(bf16[2,320,512]{2,1,0:T(8,128)(2,1)S(1)} %copy-done.2, bf16[512,512]{1,0:T(8,128)(2,1)} %bitcast.5.rounded_ref), custom_call_target="tpu_custom_call" | custom-call | flops 335544320 | bytes 1048576 | tf_op jit(solution)/shard_map/pallas_call | solution.py:191
  168.2 3.5 %all-to-all-start.5 = ((bf16[4,160,512]{2,1,0:T(8,128)(2,1)}), bf16[4,160,512]{2,1,0:T(8,128)(2,1)S(1)}, u32[]{:S(2)}, u32[]{:S(2)}) async-start(bf16[4,160,512]{2,1,0:T(8,128)(2,1)} %get-tuple-element.19), calls=%async_computation.5 | async-start | bytes 1310720 | tf_op jit(solution)/shard_map/all_to_all | solution.py:205
  171.7 9.9 %psum.14 = f32[1,128]{1,0:T(1,128)S(1)} all-reduce(f32[1,128]{1,0:T(1,128)S(1)} %get-tuple-element.18), channel_id=1, replica_groups=mesh['var'=2,'tok'=4,'wide'=64] {'tok'}, use_global_device_ids=true, to_apply=%region_5.6 | all-reduce | flops 128 | bytes 1024 | tf_op jit(solution)/shard_map/psum | solution.py:202
  181.5 10.3 %psum.15 = f32[1,128]{1,0:T(1,128)S(1)} all-reduce(f32[1,128]{1,0:T(1,128)S(1)} %psum.14), channel_id=1, replica_groups={{0,1,8,9},{2,3,10,11},{4,5,12,13},{6,7,14,15},{16,17,24,25},{18,19,26,2..., use_global_device_ids=true, to_apply=%region_6.7 | all-reduce | flops 128 | bytes 1024 | tf_op jit(solution)/shard_map/psum | solution.py:202
  191.8 0.6 reduce_sum.42
  193.0 0.0 all-to-all-done.5.in_ref
  193.0 0.9 shard_map.80
  (9 shorter events, 0.1 us)
Async XLA Ops:
  0.6 48.8 %copy-start = (bf16[2048,320]{0,1:T(8,128)(2,1)S(1)}, bf16[2048,320]{0,1:T(8,128)(2,1)}, u32[]{:S(2)}) copy-start(bf16[2048,320]{0,1:T(8,128)(2,1)} %param.9) | copy-start | bytes 3932164
  2.0 47.4 %copy-start.9 = (f32[2048]{0:T(1024)S(1)}, f32[2048]{0:T(1024)}, u32[]{:S(2)}) copy-start(f32[2048]{0:T(1024)} %param.7) | copy-start | bytes 24580
  49.5 1.3 copy-start.8
  50.8 1.3 copy-start.7
  55.1 24.1 %all-to-all-start.1 = ((f32[4,64,768]{2,1,0:T(8,128)}), f32[4,64,768]{2,1,0:T(8,128)S(1)}, u32[]{:S(2)}, u32[]{:S(2)}) async-start(f32[4,64,768]{2,1,0:T(8,128)} %bitcast.1), calls=%async_computation.1 | async-start | bytes 1572864 | tf_op jit(solution)/shard_map/all_to_all | solution.py:141
  61.3 12.1 %collective-permute-start = (bf16[320,512]{1,0:T(8,128)(2,1)S(1)}, bf16[320,512]{1,0:T(8,128)(2,1)S(1)}, u32[]{:S(2)}, u32[]{:S(2)}) collective-permute-start(bf16[320,512]{1,0:T(8,128)(2,1)S(1)} %get-tuple-element.26), channel_id=1, source_target_pairs={{0,1},{1,0},{2,3},{3,2},{4,5},{5,4},{6,7},{7,6},{8,9},{9,8},{10,11... | collective-permute-start | bytes 983048 | tf_op jit(solution)/shard_map/ppermute | solution.py:139
  63.3 12.1 %collective-permute-start.1 = (bf16[320,512]{1,0:T(8,128)(2,1)S(1)}, bf16[320,512]{1,0:T(8,128)(2,1)S(1)}, u32[]{:S(2)}, u32[]{:S(2)}) collective-permute-start(bf16[320,512]{1,0:T(8,128)(2,1)S(1)} %get-tuple-element.25), channel_id=1, source_target_pairs={{0,8},{1,9},{2,10},{3,11},{4,12},{5,13},{6,14},{7,15},{8,0},{9,1},... | collective-permute-start | bytes 983048 | tf_op jit(solution)/shard_map/ppermute | solution.py:139
  66.8 12.4 %collective-permute-start.2 = (bf16[320,512]{1,0:T(8,128)(2,1)S(1)}, bf16[320,512]{1,0:T(8,128)(2,1)S(1)}, u32[]{:S(2)}, u32[]{:S(2)}) collective-permute-start(bf16[320,512]{1,0:T(8,128)(2,1)S(1)} %get-tuple-element.24), channel_id=1, source_target_pairs={{0,9},{1,8},{2,11},{3,10},{4,13},{5,12},{6,15},{7,14},{8,1},{9,0},... | collective-permute-start | bytes 983048 | tf_op jit(solution)/shard_map/ppermute | solution.py:139
  75.4 7.5 %copy-start.3 = (bf16[320,512]{1,0:T(8,128)(2,1)}, bf16[320,512]{1,0:T(8,128)(2,1)S(1)}, u32[]{:S(2)}) copy-start(bf16[320,512]{1,0:T(8,128)(2,1)S(1)} %collective-permute-done.1.down2) | copy-start | bytes 983044
  79.2 3.8 %copy-start.5 = (bf16[320,512]{1,0:T(8,128)(2,1)}, bf16[320,512]{1,0:T(8,128)(2,1)S(1)}, u32[]{:S(2)}) copy-start(bf16[320,512]{1,0:T(8,128)(2,1)S(1)} %collective-permute-done.2.down3) | copy-start | bytes 983044
  83.0 16.0 %all-to-all-start.2 = ((bf16[16,64,320]{2,1,0:T(8,128)(2,1)}), bf16[16,64,320]{2,1,0:T(8,128)(2,1)S(1)}, u32[]{:S(2)}, u32[]{:S(2)}) async-start(bf16[16,64,320]{2,1,0:T(8,128)(2,1)} %broadcast_in_dim.51), calls=%async_computation.2 | async-start | bytes 1572864 | tf_op jit(solution)/shard_map/all_to_all | solution.py:33
  99.2 4.1 %collective-permute-start.3 = (bf16[4,256,320]{1,2,0:T(8,128)(2,1)S(1)}, bf16[4,256,320]{1,2,0:T(8,128)(2,1)}, u32[]{:S(2)}, u32[]{:S(2)}) collective-permute-start(bf16[4,256,320]{1,2,0:T(8,128)(2,1)S(1)} %copy.39), channel_id=1, source_target_pairs={{0,256},{256,0},{1,257},{257,1},{2,258},{258,2},{3,259},{259,3},{4... | collective-permute-start | bytes 1966088 | tf_op jit(solution)/shard_map/ppermute | solution.py:152
  104.8 1.0 copy-start.4
  105.8 1.0 copy-start.6
  138.8 25.9 %all-to-all-start.4 = ((bf16[16,32,512]{2,1,0:T(8,128)(2,1)}), bf16[16,32,512]{2,1,0:T(8,128)(2,1)}, u32[]{:S(2)}, u32[]{:S(2)}) async-start(bf16[16,32,512]{2,1,0:T(8,128)(2,1)} %broadcast_in_dim.54), calls=%async_computation.4 | async-start | bytes 1048576 | tf_op jit(solution)/shard_map/all_to_all | solution.py:33
  144.2 0.8 copy-start.1
  164.7 1.1 copy-start.2
  168.2 24.9 %all-to-all-start.5 = ((bf16[4,160,512]{2,1,0:T(8,128)(2,1)}), bf16[4,160,512]{2,1,0:T(8,128)(2,1)S(1)}, u32[]{:S(2)}, u32[]{:S(2)}) async-start(bf16[4,160,512]{2,1,0:T(8,128)(2,1)} %get-tuple-element.19), calls=%async_computation.5 | async-start | bytes 1310720 | tf_op jit(solution)/shard_map/all_to_all | solution.py:205

commit v4 on v2

--- a/solution.py
+++ b/solution.py
@@ -124,6 +124,13 @@
     mine = lax.dynamic_slice_in_dim(tokens, core * half, half, 0)
     gathered = spread(mine, n_wide, "wide").reshape(n_wide * half, width)
 
+    quarter = down_parent.shape[1] // 4
+    downs = [lax.dynamic_slice_in_dim(down_parent, (slot ^ k) * quarter, quarter, 1) for k in range(4)]
+    for k in range(1, 4):
+        perm = [(w, w ^ ((k // 2) * SIDE + k % 2)) for w in range(n_wide)]
+        downs[k] = lax.ppermute(downs[k], "wide", perm)
+    gathered, *downs = lax.optimization_barrier((gathered, *downs))
+
     widths = gathered.astype(jnp.float32)
     squares = jnp.sum(widths * widths, axis=1)
     gained = (widths * norm_gain[None, :]).astype(jnp.bfloat16)
@@ -140,15 +147,7 @@
     )
     rows = n_wide * half // n_tok
 
-    quarter = down_parent.shape[1] // 4
-    partial, down = lax.optimization_barrier((partial, down_parent))
-    downs = [lax.dynamic_slice_in_dim(down, (slot ^ k) * quarter, quarter, 1) for k in range(4)]
-    for k in range(1, 4):
-        perm = [(w, w ^ ((k // 2) * SIDE + k % 2)) for w in range(n_wide)]
-        downs[k] = lax.ppermute(downs[k], "wide", perm)
-
     scattered = lax.all_to_all(partial.reshape(n_tok, rows, 2 * local + 128), "tok", 0, 0)
-    scattered, *downs = lax.optimization_barrier((scattered, *downs))
     total = jnp.sum(scattered.astype(jnp.float32), axis=0)
     scale = lax.rsqrt((total[:, 2 * local] + total[:, 2 * local + 1]) / D + 1e-05)[:, None]
     gate = total[:, :local] * scale
@@ -207,8 +206,7 @@
         4 * total_rows * quarter,
     )(chosen, rounded)
 
-    for axis, count, flip in (("tok", n_tok, 1), ("tok", n_tok, 2), ("wide", n_wide, 1), ("wide", n_wide, SIDE)):
-        errors = errors + lax.ppermute(errors, axis, [(i, i ^ flip) for i in range(count)])
+    errors = lax.psum(lax.psum(errors, "tok"), "wide", axis_index_groups=blocks)
     loss = jnp.sum(errors) / (total_rows * D)
 
     swapped = lax.all_to_all(grad, "wide", 0, 0, axis_index_groups=blocks)

time: 190 us -> 187 us (0.984)
  the two profiles are of different devices: /device:TPU:8 before, /device:TPU:2 now
where the time goes in v4:
time: 187 us; the launch traced here: 186 us
  blocking collectives  65.8 us (35%)
  waiting for transfers between devices  56 us (30%)
  starting transfers between devices  39.6 us (21%)
  local copies, waits for them, and re-layouts  10.2 us (5%)
  Pallas kernels  5.45 us (3%)
  other arithmetic  3.93 us (2%)
  between operations  2.8 us (1%)
  matrix products  2.53 us (1%)
    all_to_all x3, waiting for transfers between devices, spread(): return lax.all_to_all(stacked, axes, 0, 0, axis_index_groups=groups)  48.8 us
    all_to_all x1, blocking collectives, per_device(): shares = lax.all_to_all(shares, 'wide', 0, 0, axis_index_groups=strides)  30.8 us
    all_to_all x3, starting transfers between devices, spread(): return lax.all_to_all(stacked, axes, 0, 0, axis_index_groups=groups)  26.9 us
    psum x2, blocking collectives, per_device(): errors = lax.psum(lax.psum(errors, 'tok'), 'wide', axis_index_groups=blocks)  19.3 us
    all_to_all x1, blocking collectives, per_device(): lax.all_to_all(partial.reshape(n_tok, rows, 2 * local + 128), 'tok', 0, 0)  10.5 us
    ppermute x3, starting transfers between devices, per_device(): downs[k] = lax.ppermute(downs[k], 'wide', perm)  9.2 us
    ppermute x3, waiting for transfers between devices, per_device(): downs[k] = lax.ppermute(downs[k], 'wide', perm)  7.18 us
    all_to_all x1, blocking collectives, spread(): return lax.all_to_all(stacked, axes, 0, 0, axis_index_groups=groups)  5.13 us
  transfers between devices with their start and end apart: 7, of which 5 were waited for; matrix products, arithmetic and copies ran while one was open for 3% of the time, Pallas kernels for 1%

profile of v4, /device:TPU:2, one launch (start us, length us, event | category | flops | bytes accessed | tf_op | source)
XLA Modules:
  0.0 186.3 jit_solution(15293054859350915011)
XLA Ops:
  0.6 0.0 copy-start
  0.7 0.9 constant_dynamic-slice_fusion.4
  1.5 0.0 copy-start.8
  1.5 1.5 broadcast_in_dim.43
  3.1 16.9 %all-to-all-start = ((bf16[64,4,2048]{2,1,0:T(4,128)(2,1)}), bf16[64,4,2048]{2,1,0:T(4,128)(2,1)}, u32[]{:S(2)}, u32[]{:S(2)}) async-start(bf16[64,4,2048]{2,1,0:T(4,128)(2,1)} %broadcast_in_dim.43), calls=%async_computation | async-start | bytes 2097152 | tf_op jit(solution)/shard_map/all_to_all | solution.py:33
  20.0 0.0 copy-done.8
  20.0 1.0 constant_dynamic-slice_fusion
  21.1 3.4 %collective-permute-start = (bf16[320,512]{1,0:T(8,128)(2,1)}, bf16[320,512]{1,0:T(8,128)(2,1)S(1)}, u32[]{:S(2)}, u32[]{:S(2)}) collective-permute-start(bf16[320,512]{1,0:T(8,128)(2,1)} %get-tuple-element.21), channel_id=1, source_target_pairs={{0,1},{1,0},{2,3},{3,2},{4,5},{5,4},{6,7},{7,6},{8,9},{9,8},{10,11... | collective-permute-start | bytes 983048 | tf_op jit(solution)/shard_map/ppermute | solution.py:131
  24.5 3.4 %collective-permute-start.1 = (bf16[320,512]{1,0:T(8,128)(2,1)}, bf16[320,512]{1,0:T(8,128)(2,1)S(1)}, u32[]{:S(2)}, u32[]{:S(2)}) collective-permute-start(bf16[320,512]{1,0:T(8,128)(2,1)} %get-tuple-element.23), channel_id=1, source_target_pairs={{0,8},{1,9},{2,10},{3,11},{4,12},{5,13},{6,14},{7,15},{8,0},{9,1},... | collective-permute-start | bytes 983048 | tf_op jit(solution)/shard_map/ppermute | solution.py:131
  27.8 2.4 %collective-permute-start.2 = (bf16[320,512]{1,0:T(8,128)(2,1)S(1)}, bf16[320,512]{1,0:T(8,128)(2,1)S(1)}, u32[]{:S(2)}, u32[]{:S(2)}) collective-permute-start(bf16[320,512]{1,0:T(8,128)(2,1)S(1)} %get-tuple-element.20), channel_id=1, source_target_pairs={{0,9},{1,8},{2,11},{3,10},{4,13},{5,12},{6,15},{7,14},{8,1},{9,0},... | collective-permute-start | bytes 983048 | tf_op jit(solution)/shard_map/ppermute | solution.py:131
  30.3 0.0 copy-start.10
  30.3 19.0 %all-to-all-done = bf16[64,4,2048]{2,1,0:T(4,128)(2,1)} async-done(((bf16[64,4,2048]{2,1,0:T(4,128)(2,1)}), bf16[64,4,2048]{2,1,0:T(4,128)(2,1)}, u32[]{:S(2)}, u32[]{:S(2)}) %all-to-all-start) | async-done | bytes 1048608 | tf_op jit(solution)/shard_map/all_to_all | solution.py:33
  49.3 2.2 %reshape.77 = bf16[256,2048]{1,0:T(8,128)(2,1)} reshape(bf16[64,4,2048]{2,1,0:T(4,128)(2,1)} %all-to-all-done) | data formatting | bytes 2097152 | tf_op jit(solution)/shard_map/reshape | solution.py:125
  51.5 1.3 collective-permute-done.down1
  52.8 0.0 collective-permute-done.1.down2
  52.8 5.9 %collective-permute-done.2.down3 = bf16[320,512]{1,0:T(8,128)(2,1)S(1)} collective-permute-done((bf16[320,512]{1,0:T(8,128)(2,1)S(1)}, bf16[320,512]{1,0:T(8,128)(2,1)S(1)}, u32[]{:S(2)}, u32[]{:S(2)}) %collective-permute-start.2) | collective-permute-done | bytes 327712 | tf_op jit(solution)/shard_map/ppermute | solution.py:131
  58.7 1.6 fusion.1
  60.3 0.0 copy-done
  60.4 0.0 copy-done.10
  60.4 0.0 copy-start.7
  60.4 0.0 copy-start.9
  60.4 1.9 %convolution_convert_fusion = bf16[256,320]{0,1:T(8,128)(2,1)S(1)} fusion(bf16[2048,320]{0,1:T(8,128)(2,1)S(1)} %copy-done, bf16[256,2048]{1,0:T(8,128)(2,1)} %reshape.77, f32[2048]{0:T(1024)S(1)} %copy-done.10), kind=kOutput, calls=%fused_computation.4 | convolution fusion | flops 337199104 | bytes 2531328 | tf_op jit(solution)/shard_map/dot_general | solution.py:143
  62.3 0.0 copy-done.3
  62.3 0.0 copy-done.5
  62.3 0.0 copy-done.7
  62.4 0.0 copy-done.9
  62.4 0.6 convolution_convert_fusion.1
  63.0 0.1 select_select_fusion
  63.1 0.2 copy.22
  63.3 10.5 %all_to_all.35 = bf16[4,64,768]{2,1,0:T(8,128)(2,1)S(1)} all-to-all(bf16[4,64,768]{2,1,0:T(8,128)(2,1)S(1)} %bitcast.14), channel_id=1, replica_groups=mesh['var'=2,'tok'=4,'wide'=64] {'tok'}, dimensions={0} | all-to-all | bytes 786432 | tf_op jit(solution)/shard_map/all_to_all | solution.py:150
  73.8 0.1 convert_reduce_fusion
  73.9 0.2 fusion.11
  74.1 0.1 fusion.7
  74.2 1.0 broadcast_in_dim.73
  75.2 5.9 %all-to-all-start.2 = ((bf16[16,64,320]{2,1,0:T(8,128)(2,1)}), bf16[16,64,320]{2,1,0:T(8,128)(2,1)S(1)}, u32[]{:S(2)}, u32[]{:S(2)}) async-start(bf16[16,64,320]{2,1,0:T(8,128)(2,1)} %broadcast_in_dim.73), calls=%async_computation.2 | async-start | bytes 1572864 | tf_op jit(solution)/shard_map/all_to_all | solution.py:33
  81.0 0.8 fusion.15
  81.8 0.3 fusion.4
  82.1 0.1 convert_element_type.72
  82.2 0.1 convert_element_type.73
  82.3 10.1 %all-to-all-done.2 = bf16[16,64,320]{2,1,0:T(8,128)(2,1)S(1)} async-done(((bf16[16,64,320]{2,1,0:T(8,128)(2,1)}), bf16[16,64,320]{2,1,0:T(8,128)(2,1)S(1)}, u32[]{:S(2)}, u32[]{:S(2)}) %all-to-all-start.2) | async-done | bytes 655392 | tf_op jit(solution)/shard_map/all_to_all | solution.py:33
  92.5 0.3 broadcast_in_dim.74
  92.7 0.0 copy-start.4
  92.7 0.0 copy-start.6
  92.7 5.1 %all_to_all.36 = bf16[2,16,64,320]{3,2,1,0:T(8,128)(2,1)S(1)} all-to-all(bf16[2,16,64,320]{3,2,1,0:T(8,128)(2,1)S(1)} %broadcast_in_dim.74), channel_id=1, replica_groups=mesh['var'=2,'tok'=4,'wide'=64] {'var'}, dimensions={0} | all-to-all | bytes 2621440 | tf_op jit(solution)/shard_map/all_to_all | solution.py:33
  97.9 0.0 copy-done.4
  97.9 0.0 copy-done.6
  97.9 1.2 shard_map.78
  99.1 30.8 %all_to_all.37 = bf16[16,32,512]{2,1,0:T(8,128)(2,1)S(1)} all-to-all(bf16[16,32,512]{2,1,0:T(8,128)(2,1)S(1)} %bitcast.13), channel_id=1, replica_groups={{0,2,4,6,16,18,20,22,32,34,36,38,48,50,52,54},{1,3,5,7,17,19,21,23,33,3..., dimensions={0} | all-to-all | bytes 1048576 | tf_op jit(solution)/shard_map/all_to_all | solution.py:186
  130.0 0.1 reduce_sum.41
  130.0 0.9 broadcast_in_dim.77
  130.9 4.2 %all-to-all-start.5 = ((bf16[16,32,512]{2,1,0:T(8,128)(2,1)}), bf16[16,32,512]{2,1,0:T(8,128)(2,1)}, u32[]{:S(2)}, u32[]{:S(2)}) async-start(bf16[16,32,512]{2,1,0:T(8,128)(2,1)} %broadcast_in_dim.77), calls=%async_computation.5 | async-start | bytes 1048576 | tf_op jit(solution)/shard_map/all_to_all | solution.py:33
  135.2 0.2 copy.23.names_ref
  135.3 0.9 shard_map.77.chosen_ref
  136.3 0.0 copy-start.1
  136.3 0.8 copy-done.1
  137.1 19.6 %all-to-all-done.5 = bf16[16,32,512]{2,1,0:T(8,128)(2,1)} async-done(((bf16[16,32,512]{2,1,0:T(8,128)(2,1)}), bf16[16,32,512]{2,1,0:T(8,128)(2,1)}, u32[]{:S(2)}, u32[]{:S(2)}) %all-to-all-start.5) | async-done | bytes 524320 | tf_op jit(solution)/shard_map/all_to_all | solution.py:33
  156.8 1.1 copy-done.2
  157.8 2.4 %shard_map.79 = (bf16[4,160,512]{2,1,0:T(8,128)(2,1)}, f32[1,128]{1,0:T(1,128)S(1)}) custom-call(bf16[2,320,512]{2,1,0:T(8,128)(2,1)S(1)} %copy-done.2, bf16[512,512]{1,0:T(8,128)(2,1)} %bitcast.5.rounded_ref), custom_call_target="tpu_custom_call" | custom-call | flops 335544320 | bytes 1048576 | tf_op jit(solution)/shard_map/pallas_call | solution.py:198
  160.2 3.5 %all-to-all-start.6 = ((bf16[4,160,512]{2,1,0:T(8,128)(2,1)}), bf16[4,160,512]{2,1,0:T(8,128)(2,1)S(1)}, u32[]{:S(2)}, u32[]{:S(2)}) async-start(bf16[4,160,512]{2,1,0:T(8,128)(2,1)} %get-tuple-element.15), calls=%async_computation.6 | async-start | bytes 1310720 | tf_op jit(solution)/shard_map/all_to_all | solution.py:212
  163.7 9.1 %psum.14 = f32[1,128]{1,0:T(1,128)S(1)} all-reduce(f32[1,128]{1,0:T(1,128)S(1)} %get-tuple-element.14), channel_id=1, replica_groups=mesh['var'=2,'tok'=4,'wide'=64] {'tok'}, use_global_device_ids=true, to_apply=%region_5.6 | all-reduce | flops 128 | bytes 1024 | tf_op jit(solution)/shard_map/psum | solution.py:209
  172.8 10.3 %psum.15 = f32[1,128]{1,0:T(1,128)S(1)} all-reduce(f32[1,128]{1,0:T(1,128)S(1)} %psum.14), channel_id=1, replica_groups={{0,1,8,9},{2,3,10,11},{4,5,12,13},{6,7,14,15},{16,17,24,25},{18,19,26,2..., use_global_device_ids=true, to_apply=%region_6.7 | all-reduce | flops 128 | bytes 1024 | tf_op jit(solution)/shard_map/psum | solution.py:209
  183.0 0.6 reduce_sum.42
  184.3 0.0 all-to-all-done.6.in_ref
  184.3 0.9 shard_map.80
  (10 shorter events, 0.1 us)
Async XLA Ops:
  0.6 59.7 %copy-start = (bf16[2048,320]{0,1:T(8,128)(2,1)S(1)}, bf16[2048,320]{0,1:T(8,128)(2,1)}, u32[]{:S(2)}) copy-start(bf16[2048,320]{0,1:T(8,128)(2,1)} %param.9) | copy-start | bytes 3932164
  1.5 18.5 %copy-start.8 = (bf16[320,2048]{1,0:T(8,128)(2,1)S(1)}, bf16[320,2048]{1,0:T(8,128)(2,1)}, u32[]{:S(2)}) copy-start(bf16[320,2048]{1,0:T(8,128)(2,1)} %param.10) | copy-start | bytes 3932164
  3.1 46.3 %all-to-all-start = ((bf16[64,4,2048]{2,1,0:T(4,128)(2,1)}), bf16[64,4,2048]{2,1,0:T(4,128)(2,1)}, u32[]{:S(2)}, u32[]{:S(2)}) async-start(bf16[64,4,2048]{2,1,0:T(4,128)(2,1)} %broadcast_in_dim.43), calls=%async_computation | async-start | bytes 2097152 | tf_op jit(solution)/shard_map/all_to_all | solution.py:33
  21.1 31.8 %collective-permute-start = (bf16[320,512]{1,0:T(8,128)(2,1)}, bf16[320,512]{1,0:T(8,128)(2,1)S(1)}, u32[]{:S(2)}, u32[]{:S(2)}) collective-permute-start(bf16[320,512]{1,0:T(8,128)(2,1)} %get-tuple-element.21), channel_id=1, source_target_pairs={{0,1},{1,0},{2,3},{3,2},{4,5},{5,4},{6,7},{7,6},{8,9},{9,8},{10,11... | collective-permute-start | bytes 983048 | tf_op jit(solution)/shard_map/ppermute | solution.py:131
  24.5 28.4 %collective-permute-start.1 = (bf16[320,512]{1,0:T(8,128)(2,1)}, bf16[320,512]{1,0:T(8,128)(2,1)S(1)}, u32[]{:S(2)}, u32[]{:S(2)}) collective-permute-start(bf16[320,512]{1,0:T(8,128)(2,1)} %get-tuple-element.23), channel_id=1, source_target_pairs={{0,8},{1,9},{2,10},{3,11},{4,12},{5,13},{6,14},{7,15},{8,0},{9,1},... | collective-permute-start | bytes 983048 | tf_op jit(solution)/shard_map/ppermute | solution.py:131
  27.8 30.9 %collective-permute-start.2 = (bf16[320,512]{1,0:T(8,128)(2,1)S(1)}, bf16[320,512]{1,0:T(8,128)(2,1)S(1)}, u32[]{:S(2)}, u32[]{:S(2)}) collective-permute-start(bf16[320,512]{1,0:T(8,128)(2,1)S(1)} %get-tuple-element.20), channel_id=1, source_target_pairs={{0,9},{1,8},{2,11},{3,10},{4,13},{5,12},{6,15},{7,14},{8,1},{9,0},... | collective-permute-start | bytes 983048 | tf_op jit(solution)/shard_map/ppermute | solution.py:131
  30.3 30.1 %copy-start.10 = (f32[2048]{0:T(1024)S(1)}, f32[2048]{0:T(1024)}, u32[]{:S(2)}) copy-start(f32[2048]{0:T(1024)} %param.7) | copy-start | bytes 24580
  52.8 9.5 %copy-start.3 = (bf16[320,512]{1,0:T(8,128)(2,1)}, bf16[320,512]{1,0:T(8,128)(2,1)S(1)}, u32[]{:S(2)}) copy-start(bf16[320,512]{1,0:T(8,128)(2,1)S(1)} %collective-permute-done.1.down2) | copy-start | bytes 983044
  58.7 3.6 %copy-start.5 = (bf16[320,512]{1,0:T(8,128)(2,1)}, bf16[320,512]{1,0:T(8,128)(2,1)S(1)}, u32[]{:S(2)}) copy-start(bf16[320,512]{1,0:T(8,128)(2,1)S(1)} %collective-permute-done.2.down3) | copy-start | bytes 983044
  60.4 2.0 %copy-start.7 = (bf16[256,2048]{1,0:T(8,128)(2,1)S(1)}, bf16[256,2048]{1,0:T(8,128)(2,1)}, u32[]{:S(2)}) copy-start(bf16[256,2048]{1,0:T(8,128)(2,1)} %reshape.77) | copy-start | bytes 3145732
  60.4 2.0 %copy-start.9 = (bf16[2048,320]{0,1:T(8,128)(2,1)S(1)}, bf16[2048,320]{0,1:T(8,128)(2,1)}, u32[]{:S(2)}) copy-start(bf16[2048,320]{0,1:T(8,128)(2,1)} %param.8) | copy-start | bytes 3932164
  75.2 17.3 %all-to-all-start.2 = ((bf16[16,64,320]{2,1,0:T(8,128)(2,1)}), bf16[16,64,320]{2,1,0:T(8,128)(2,1)S(1)}, u32[]{:S(2)}, u32[]{:S(2)}) async-start(bf16[16,64,320]{2,1,0:T(8,128)(2,1)} %broadcast_in_dim.73), calls=%async_computation.2 | async-start | bytes 1572864 | tf_op jit(solution)/shard_map/all_to_all | solution.py:33
  92.7 5.2 %copy-start.4 = (bf16[320,512]{1,0:T(8,128)(2,1)S(1)}, bf16[320,512]{1,0:T(8,128)(2,1)}, u32[]{:S(2)}) copy-start(bf16[320,512]{1,0:T(8,128)(2,1)} %copy-done.3) | copy-start | bytes 983044
  92.7 5.1 %copy-start.6 = (bf16[320,512]{1,0:T(8,128)(2,1)S(1)}, bf16[320,512]{1,0:T(8,128)(2,1)}, u32[]{:S(2)}) copy-start(bf16[320,512]{1,0:T(8,128)(2,1)} %copy-done.5) | copy-start | bytes 983044
  130.9 25.8 %all-to-all-start.5 = ((bf16[16,32,512]{2,1,0:T(8,128)(2,1)}), bf16[16,32,512]{2,1,0:T(8,128)(2,1)}, u32[]{:S(2)}, u32[]{:S(2)}) async-start(bf16[16,32,512]{2,1,0:T(8,128)(2,1)} %broadcast_in_dim.77), calls=%async_computation.5 | async-start | bytes 1048576 | tf_op jit(solution)/shard_map/all_to_all | solution.py:33
  136.3 0.8 copy-start.1
  156.7 1.1 copy-start.2
  160.2 24.1 %all-to-all-start.6 = ((bf16[4,160,512]{2,1,0:T(8,128)(2,1)}), bf16[4,160,512]{2,1,0:T(8,128)(2,1)S(1)}, u32[]{:S(2)}, u32[]{:S(2)}) async-start(bf16[4,160,512]{2,1,0:T(8,128)(2,1)} %get-tuple-element.15), calls=%async_computation.6 | async-start | bytes 1310720 | tf_op jit(solution)/shard_map/all_to_all | solution.py:212

commit v5 on v4

--- a/solution.py
+++ b/solution.py
@@ -49,7 +49,7 @@
         out_shape=out_shape,
         in_specs=in_specs,
         out_specs=out_specs,
-        compiler_params=pltpu.CompilerParams(vmem_limit_bytes=32 * 1024 * 1024),
+        compiler_params=pltpu.CompilerParams(vmem_limit_bytes=16 * 1024 * 1024),
         cost_estimate=pl.CostEstimate(flops=flops, bytes_accessed=size, transcendentals=0),
     )
 
@@ -88,25 +88,59 @@
             out_ref[pair, :, core * rows : (core + 1) * rows] = total.astype(out_ref.dtype)
 
 
-def gradient_kernel(factor, chosen_ref, rounded_ref, grad_ref, error_ref):
+def hidden_kernel(sums_ref, out_ref):
+    local = out_ref.shape[2]
+    total = sums_ref[0].astype(jnp.float32)
+    for i in range(1, sums_ref.shape[0]):
+        total = total + sums_ref[i].astype(jnp.float32)
+    squares = total[:, local : local + 1] + total[:, local + 1 : local + 2]
+    scale = lax.rsqrt(squares / D + 1e-05)
+    half = total.shape[1] // 2
+    gate = total[:, :local] * scale
+    up = total[:, half : half + local] * scale
+    hidden = (gate / (1.0 + jnp.exp(-gate)) * up).astype(out_ref.dtype)
+    for i in range(out_ref.shape[0]):
+        out_ref[i] = hidden
+
+
+def piece_kernel(shares_ref, out_ref):
+    total = shares_ref[0].astype(jnp.float32)
+    for i in range(1, shares_ref.shape[0]):
+        total = total + shares_ref[i].astype(jnp.float32)
+    piece = total.astype(out_ref.dtype)
+    for i in range(out_ref.shape[0]):
+        out_ref[i] = piece
+
+
+def gradient_kernel(factor, chosen_ref, rounded_ref, out_ref):
     rounded = rounded_ref[...]
-    block = grad_ref.shape[1]
+    block = chosen_ref.shape[1] // 2
     for pair in range(2):
         product = jnp.dot(chosen_ref[pair], rounded, preferred_element_type=jnp.float32) * factor
         for i in range(2):
-            grad_ref[2 * pair + i] = product[i * block : (i + 1) * block].astype(grad_ref.dtype)
+            out_ref[2 * pair + i, :block] = product[i * block : (i + 1) * block].astype(out_ref.dtype)
     errors = rounded.astype(jnp.float32)
     columns = jnp.sum(errors * errors, axis=0, keepdims=True)
-    total = columns[:, :128]
-    for i in range(1, columns.shape[1] // 128):
-        total = total + columns[:, i * 128 : (i + 1) * 128]
-    error_ref[...] = total
-
-
-def interleave_kernel(in_ref, out_ref):
+    hi = columns.astype(out_ref.dtype).astype(jnp.float32)
+    line = lax.broadcasted_iota(jnp.int32, (16, columns.shape[1]), 0)
+    extra = jnp.where(line == 0, hi, jnp.where(line == 1, columns - hi, 0.0)).astype(out_ref.dtype)
+    for i in range(4):
+        out_ref[i, block:] = extra
+
+
+def interleave_kernel(in_ref, out_ref, error_ref):
+    block = out_ref.shape[0]
     width = in_ref.shape[2]
+    total = None
     for i in range(in_ref.shape[0]):
-        out_ref[:, i * width : (i + 1) * width] = in_ref[i]
+        out_ref[:, i * width : (i + 1) * width] = in_ref[i, :block]
+        term = in_ref[i, block:].astype(jnp.float32)
+        total = term if total is None else total + term
+    columns = jnp.sum(total, axis=0, keepdims=True)
+    lanes = columns[:, :128]
+    for i in range(1, width // 128):
+        lanes = lanes + columns[:, i * 128 : (i + 1) * 128]
+    error_ref[...] = lanes
 
 
 def per_device(tokens, norm_gain, gate_parent, up_parent, down_parent, kept):
@@ -129,33 +163,37 @@
     for k in range(1, 4):
         perm = [(w, w ^ ((k // 2) * SIDE + k % 2)) for w in range(n_wide)]
         downs[k] = lax.ppermute(downs[k], "wide", perm)
-    gathered, *downs = lax.optimization_barrier((gathered, *downs))
 
     widths = gathered.astype(jnp.float32)
     squares = jnp.sum(widths * widths, axis=1)
     gained = (widths * norm_gain[None, :]).astype(jnp.bfloat16)
     sq_hi, sq_lo = hi_lo(squares)
-    lanes = lax.broadcasted_iota(jnp.int32, (n_wide * half, 128), 1)
+    pad = (-local) % 128
+    lanes = lax.broadcasted_iota(jnp.int32, (n_wide * half, pad), 1)
     extra = jnp.where(lanes == 0, sq_hi[:, None], jnp.where(lanes == 1, sq_lo[:, None], jnp.zeros((), jnp.bfloat16)))
     partial = jnp.concatenate(
         [
             jnp.dot(gained, gate_parent, preferred_element_type=jnp.float32).astype(jnp.bfloat16),
+            extra,
             jnp.dot(gained, up_parent, preferred_element_type=jnp.float32).astype(jnp.bfloat16),
-            extra,
+            jnp.zeros((n_wide * half, pad), jnp.bfloat16),
         ],
         axis=1,
     )
     rows = n_wide * half // n_tok
 
-    scattered = lax.all_to_all(partial.reshape(n_tok, rows, 2 * local + 128), "tok", 0, 0)
-    total = jnp.sum(scattered.astype(jnp.float32), axis=0)
-    scale = lax.rsqrt((total[:, 2 * local] + total[:, 2 * local + 1]) / D + 1e-05)[:, None]
-    gate = total[:, :local] * scale
-    up = total[:, local : 2 * local] * scale
-    hidden = (jax.nn.silu(gate) * up).astype(jnp.bfloat16)
+    scattered = lax.all_to_all(partial.reshape(n_tok, rows, 2 * (local + pad)), "tok", 0, 0)
+    scattered, *downs = lax.optimization_barrier((scattered, *downs))
+    hidden = call(
+        hidden_kernel,
+        jax.ShapeDtypeStruct((4 * n_tok, rows, local), jnp.bfloat16),
+        [VMEM],
+        0,
+        16 * rows * local,
+    )(scattered)
 
     groups = [[t * n_wide + w for w in block for t in range(n_tok)] for block in blocks]
-    hidden = spread(hidden, n_tok * 4, ("tok", "wide"), groups)
+    hidden = lax.all_to_all(hidden, ("tok", "wide"), 0, 0, axis_index_groups=groups)
     hidden = spread(hidden, 2, "var").reshape(2, 4, n_tok * rows, local)
     total_rows = 2 * n_tok * rows
 
@@ -184,8 +222,8 @@
     shares = shares.reshape(n_blocks, total_rows // n_blocks, quarter)
     strides = stride_groups()
     shares = lax.all_to_all(shares, "wide", 0, 0, axis_index_groups=strides)
-    piece = jnp.sum(shares.astype(jnp.float32), axis=0).astype(jnp.bfloat16)
-    rounded = spread(piece, n_blocks, "wide", strides).reshape(total_rows, quarter)
+    pieces = call(piece_kernel, jax.ShapeDtypeStruct(shares.shape, jnp.bfloat16), [VMEM], 0, 4 * total_rows * quarter)(shares)
+    rounded = lax.all_to_all(pieces, "wide", 0, 0, axis_index_groups=strides).reshape(total_rows, quarter)
 
     chosen = call(
         select_kernel,
@@ -195,28 +233,25 @@
         4 * total_rows * local,
     )(names, hidden)
     factor = 1.0 / math.sqrt(total_rows)
-    grad, errors = call(
+    grad = call(
         functools.partial(gradient_kernel, factor),
-        (
-            jax.ShapeDtypeStruct((4, block, quarter), jnp.bfloat16),
-            jax.ShapeDtypeStruct((1, 128), jnp.float32),
-        ),
+        jax.ShapeDtypeStruct((4, block + 16, quarter), jnp.bfloat16),
         [VMEM] * 2,
         2 * total_rows * 4 * block * quarter,
         4 * total_rows * quarter,
     )(chosen, rounded)
-
-    errors = lax.psum(lax.psum(errors, "tok"), "wide", axis_index_groups=blocks)
-    loss = jnp.sum(errors) / (total_rows * D)
-
     swapped = lax.all_to_all(grad, "wide", 0, 0, axis_index_groups=blocks)
-    grad = call(
+    grad, errors = call(
         interleave_kernel,
-        jax.ShapeDtypeStruct((block, 4 * quarter), jnp.bfloat16),
+        (
+            jax.ShapeDtypeStruct((block, 4 * quarter), jnp.bfloat16),
+            jax.ShapeDtypeStruct((1, 128), jnp.float32),
+        ),
         [VMEM],
         0,
         4 * block * quarter,
     )(swapped)
+    loss = jnp.sum(lax.psum(errors, "tok")) / (total_rows * D)
     return (loss.reshape(1), grad[None])
 
 

time: 187 us -> 175 us (0.936)
  blocking collectives: 65.8 us -> 54.6 us
  waiting for transfers between devices: 56 us -> 52.4 us
    all_to_all x1 -> x3, waiting for transfers between devices: 0.01 us -> 33.4 us  [the longest x1 18.9 us: per_device(): lax.all_to_all(pieces, 'wide', 0, 0, axis_index_groups=strides)]
    all_to_all x3 -> x1, waiting for transfers between devices: 48.8 us -> 19.1 us  [spread(): return lax.all_to_all(stacked, axes, 0, 0, axis_index_groups=groups)]
    all_to_all x1 -> x3, starting transfers between devices: 3.48 us -> 15.2 us  [the longest x1 6.1 us: per_device(): lax.all_to_all(hidden, ('tok', 'wide'), 0, 0, axis_index_groups=groups)]
    psum x2 -> x1, blocking collectives: 19.3 us -> 9.1 us  [per_device(): loss = jnp.sum(lax.psum(errors, 'tok')) / (total_rows * D)]
    all_to_all x3 -> x1, starting transfers between devices: 26.9 us -> 16.9 us  [spread(): return lax.all_to_all(stacked, axes, 0, 0, axis_index_groups=groups)]
    ppermute x3, waiting for transfers between devices: 7.18 us -> 0.01 us  [per_device(): downs[k] = lax.ppermute(downs[k], 'wide', perm)]
    all_to_all x1, blocking collectives: 30.8 us -> 27.6 us  [per_device(): shares = lax.all_to_all(shares, 'wide', 0, 0, axis_index_groups=strides)]
    convert_element_type x0 -> x1, local copies, waits for them, and re-layouts: none -> 2.47 us  [per_device(): widths = gathered.astype(jnp.float32)]
  transfers between devices with their start and end apart: 7 -> 7, of which waited for: 5 -> 4; matrix products, arithmetic and copies ran while one was open for 3% -> 7% of each run, Pallas kernels for 1% -> 1%
where the time goes in v5:
time: 175 us; the launch traced here: 174 us
  blocking collectives  54.6 us (31%)
  waiting for transfers between devices  52.4 us (30%)
  starting transfers between devices  41.2 us (24%)
  local copies, waits for them, and re-layouts  9.44 us (5%)
  Pallas kernels  6.65 us (4%)
  other arithmetic  3.7 us (2%)
  matrix products  2.84 us (2%)
  between operations  2.74 us (2%)
    all_to_all x1, blocking collectives, per_device(): shares = lax.all_to_all(shares, 'wide', 0, 0, axis_index_groups=strides)  27.6 us
    all_to_all x1, waiting for transfers between devices, spread(): return lax.all_to_all(stacked, axes, 0, 0, axis_index_groups=groups)  19.1 us
    all_to_all x1, waiting for transfers between devices, per_device(): lax.all_to_all(pieces, 'wide', 0, 0, axis_index_groups=strides)  18.9 us
    all_to_all x1, starting transfers between devices, spread(): return lax.all_to_all(stacked, axes, 0, 0, axis_index_groups=groups)  16.9 us
    all_to_all x1, blocking collectives, per_device(): swapped = lax.all_to_all(grad, 'wide', 0, 0, axis_index_groups=blocks)  12.8 us
    ppermute x3, starting transfers between devices, per_device(): downs[k] = lax.ppermute(downs[k], 'wide', perm)  9.2 us
    psum x1, blocking collectives, per_device(): loss = jnp.sum(lax.psum(errors, 'tok')) / (total_rows * D)  9.1 us
    all_to_all x1, waiting for transfers between devices, per_device(): lax.all_to_all(hidden, ('tok', 'wide'), 0, 0, axis_index_groups=groups)  8.57 us
  transfers between devices with their start and end apart: 7, of which 4 were waited for; matrix products, arithmetic and copies ran while one was open for 7% of the time, Pallas kernels for 1%

profile of v5, /device:TPU:2, one launch (start us, length us, event | category | flops | bytes accessed | tf_op | source)
XLA Modules:
  0.0 173.7 jit_solution(1580740890533777081)
XLA Ops:
  0.6 0.0 copy-start
  0.7 0.9 constant_dynamic-slice_fusion.4
  1.5 0.0 copy-start.8
  1.5 1.5 broadcast_in_dim.57
  3.0 16.9 %all-to-all-start = ((bf16[64,4,2048]{2,1,0:T(4,128)(2,1)}), bf16[64,4,2048]{2,1,0:T(4,128)(2,1)}, u32[]{:S(2)}, u32[]{:S(2)}) async-start(bf16[64,4,2048]{2,1,0:T(4,128)(2,1)} %broadcast_in_dim.57), calls=%async_computation | async-start | bytes 2097152 | tf_op jit(solution)/shard_map/all_to_all | solution.py:33
  20.0 0.0 copy-done.8
  20.0 1.0 constant_dynamic-slice_fusion
  21.0 3.4 %collective-permute-start = (bf16[320,512]{1,0:T(8,128)(2,1)}, bf16[320,512]{1,0:T(8,128)(2,1)S(1)}, u32[]{:S(2)}, u32[]{:S(2)}) collective-permute-start(bf16[320,512]{1,0:T(8,128)(2,1)} %get-tuple-element.21), channel_id=1, source_target_pairs={{0,1},{1,0},{2,3},{3,2},{4,5},{5,4},{6,7},{7,6},{8,9},{9,8},{10,11... | collective-permute-start | bytes 983048 | tf_op jit(solution)/shard_map/ppermute | solution.py:165
  24.4 3.4 %collective-permute-start.1 = (bf16[320,512]{1,0:T(8,128)(2,1)}, bf16[320,512]{1,0:T(8,128)(2,1)S(1)}, u32[]{:S(2)}, u32[]{:S(2)}) collective-permute-start(bf16[320,512]{1,0:T(8,128)(2,1)} %get-tuple-element.23), channel_id=1, source_target_pairs={{0,8},{1,9},{2,10},{3,11},{4,12},{5,13},{6,14},{7,15},{8,0},{9,1},... | collective-permute-start | bytes 983048 | tf_op jit(solution)/shard_map/ppermute | solution.py:165
  27.7 2.4 %collective-permute-start.2 = (bf16[320,512]{1,0:T(8,128)(2,1)S(1)}, bf16[320,512]{1,0:T(8,128)(2,1)S(1)}, u32[]{:S(2)}, u32[]{:S(2)}) collective-permute-start(bf16[320,512]{1,0:T(8,128)(2,1)S(1)} %get-tuple-element.20), channel_id=1, source_target_pairs={{0,9},{1,8},{2,11},{3,10},{4,13},{5,12},{6,15},{7,14},{8,1},{9,0},... | collective-permute-start | bytes 983048 | tf_op jit(solution)/shard_map/ppermute | solution.py:165
  30.2 19.1 %all-to-all-done = bf16[64,4,2048]{2,1,0:T(4,128)(2,1)} async-done(((bf16[64,4,2048]{2,1,0:T(4,128)(2,1)}), bf16[64,4,2048]{2,1,0:T(4,128)(2,1)}, u32[]{:S(2)}, u32[]{:S(2)}) %all-to-all-start) | async-done | bytes 1048608 | tf_op jit(solution)/shard_map/all_to_all | solution.py:33
  49.3 1.8 %multiply_reduce_fusion = f32[64,4]{1,0:T(8,128)S(1)} fusion(bf16[64,4,2048]{2,1,0:T(4,128)(2,1)} %all-to-all-done), kind=kLoop, calls=%fused_computation | loop fusion | flops 1572608 | bytes 1049600 | tf_op jit(solution)/shard_map/reduce_sum | solution.py:168
  51.1 0.1 reduce_sum.21
  51.2 0.0 copy-start.9
  51.3 2.5 %reshape.90 = f32[256,2048]{1,0:T(8,128)} reshape(bf16[64,4,2048]{2,1,0:T(4,128)(2,1)} %all-to-all-done) | data formatting | bytes 3145728 | tf_op jit(solution)/shard_map/convert_element_type | solution.py:167
  53.7 0.0 copy-done
  53.7 0.0 copy-done.9
  53.7 0.0 copy-start.6
  53.7 0.0 copy-start.7
  53.7 2.3 %convolution_convert_fusion = bf16[256,320]{0,1:T(8,128)(2,1)S(1)} fusion(bf16[2048,320]{0,1:T(8,128)(2,1)S(1)} %copy-done, f32[256,2048]{1,0:T(8,128)} %reshape.90, f32[2048]{0:T(1024)S(1)} %copy-done.9), kind=kOutput, calls=%fused_computation.2 | convolution fusion | flops 336674816 | bytes 3579904 | tf_op jit(solution)/shard_map/dot_general | solution.py:178
  56.0 0.0 copy-done.6
  56.1 0.3 copy-done.7
  56.3 0.5 convolution_convert_fusion.1
  56.9 0.1 select_select_fusion
  57.0 0.9 copy.20
  57.9 4.8 %all-to-all-start.1 = ((bf16[4,64,768]{2,1,0:T(8,128)(2,1)}), bf16[4,64,768]{2,1,0:T(8,128)(2,1)S(1)}, u32[]{:S(2)}, u32[]{:S(2)}) async-start(bf16[4,64,768]{2,1,0:T(8,128)(2,1)} %bitcast.1), calls=%async_computation.1 | async-start | bytes 786432 | tf_op jit(solution)/shard_map/all_to_all | solution.py:185
  62.7 0.0 collective-permute-done.down1
  62.8 0.0 collective-permute-done.1.down2
  62.8 0.0 copy-start.2
  62.8 0.0 collective-permute-done.2.down3
  62.8 0.0 copy-start.4
  62.8 5.9 %all-to-all-done.1.sums_ref = bf16[4,64,768]{2,1,0:T(8,128)(2,1)S(1)} async-done(((bf16[4,64,768]{2,1,0:T(8,128)(2,1)}), bf16[4,64,768]{2,1,0:T(8,128)(2,1)S(1)}, u32[]{:S(2)}, u32[]{:S(2)}) %all-to-all-start.1) | async-done | bytes 393248 | tf_op jit(solution)/shard_map/all_to_all | solution.py:185
  68.7 1.2 shard_map.77
  69.8 6.1 %all-to-all-start.2 = ((bf16[16,64,320]{2,1,0:T(8,128)(2,1)}), bf16[16,64,320]{2,1,0:T(8,128)(2,1)S(1)}, u32[]{:S(2)}, u32[]{:S(2)}) async-start(bf16[16,64,320]{2,1,0:T(8,128)(2,1)} %shard_map.77), calls=%async_computation.2 | async-start | bytes 1572864 | tf_op jit(solution)/shard_map/all_to_all | solution.py:196
  75.9 0.8 fusion.5
  76.7 0.3 fusion
  77.0 0.1 convert_element_type.71
  77.1 0.1 convert_element_type.72
  77.2 8.6 %all-to-all-done.2 = bf16[16,64,320]{2,1,0:T(8,128)(2,1)S(1)} async-done(((bf16[16,64,320]{2,1,0:T(8,128)(2,1)}), bf16[16,64,320]{2,1,0:T(8,128)(2,1)S(1)}, u32[]{:S(2)}, u32[]{:S(2)}) %all-to-all-start.2) | async-done | bytes 655392 | tf_op jit(solution)/shard_map/all_to_all | solution.py:196
  85.8 0.0 copy-done.2
  85.8 0.0 copy-done.4
  85.8 0.3 broadcast_in_dim.61
  86.1 0.0 copy-start.3
  86.1 0.0 copy-start.5
  86.1 5.1 %all_to_all.35 = bf16[2,16,64,320]{3,2,1,0:T(8,128)(2,1)S(1)} all-to-all(bf16[2,16,64,320]{3,2,1,0:T(8,128)(2,1)S(1)} %broadcast_in_dim.61), channel_id=1, replica_groups=mesh['var'=2,'tok'=4,'wide'=64] {'var'}, dimensions={0} | all-to-all | bytes 2621440 | tf_op jit(solution)/shard_map/all_to_all | solution.py:33
  91.2 0.0 copy-done.3
  91.2 0.0 copy-done.5
  91.2 1.2 shard_map.79
  92.5 27.6 %all_to_all.36.shares_ref = bf16[16,32,512]{2,1,0:T(8,128)(2,1)S(1)} all-to-all(bf16[16,32,512]{2,1,0:T(8,128)(2,1)S(1)} %bitcast.13), channel_id=1, replica_groups={{0,2,4,6,16,18,20,22,32,34,36,38,48,50,52,54},{1,3,5,7,17,19,21,23,33,3..., dimensions={0} | all-to-all | bytes 1048576 | tf_op jit(solution)/shard_map/all_to_all | solution.py:224
  120.1 0.9 shard_map.80
  121.0 4.3 %all-to-all-start.5 = ((bf16[16,32,512]{2,1,0:T(8,128)(2,1)}), bf16[16,32,512]{2,1,0:T(8,128)(2,1)}, u32[]{:S(2)}, u32[]{:S(2)}) async-start(bf16[16,32,512]{2,1,0:T(8,128)(2,1)} %shard_map.80), calls=%async_computation.5 | async-start | bytes 1048576 | tf_op jit(solution)/shard_map/all_to_all | solution.py:226
  125.2 0.9 copy.21.names_ref
  126.1 0.0 copy-start.1
  126.1 1.0 copy-done.1
  127.1 0.9 shard_map.78.chosen_ref
  128.1 18.9 %all-to-all-done.5 = bf16[16,32,512]{2,1,0:T(8,128)(2,1)} async-done(((bf16[16,32,512]{2,1,0:T(8,128)(2,1)}), bf16[16,32,512]{2,1,0:T(8,128)(2,1)}, u32[]{:S(2)}, u32[]{:S(2)}) %all-to-all-start.5) | async-done | bytes 524320 | tf_op jit(solution)/shard_map/all_to_all | solution.py:226
  147.0 1.5 shard_map.81
  148.5 12.8 %all_to_all.37.in_ref = bf16[4,176,512]{2,1,0:T(8,128)(2,1)S(1)} all-to-all(bf16[4,176,512]{2,1,0:T(8,128)(2,1)S(1)} %shard_map.81), channel_id=1, replica_groups={{0,1,8,9},{2,3,10,11},{4,5,12,13},{6,7,14,15},{16,17,24,25},{18,19,26,2..., dimensions={0} | all-to-all | bytes 1441792 | tf_op jit(solution)/shard_map/all_to_all | solution.py:243
  161.3 0.9 shard_map.82
  162.2 9.1 %psum.7 = f32[1,128]{1,0:T(1,128)S(1)} all-reduce(f32[1,128]{1,0:T(1,128)S(1)} %get-tuple-element.14), channel_id=1, replica_groups=mesh['var'=2,'tok'=4,'wide'=64] {'tok'}, use_global_device_ids=true, to_apply=%region_3.4 | all-reduce | flops 128 | bytes 1024 | tf_op jit(solution)/shard_map/psum | solution.py:254
  171.3 0.6 reduce_sum.22
  (8 shorter events, 0.1 us)
Async XLA Ops:
  0.6 53.1 %copy-start = (bf16[2048,320]{0,1:T(8,128)(2,1)S(1)}, bf16[2048,320]{0,1:T(8,128)(2,1)}, u32[]{:S(2)}) copy-start(bf16[2048,320]{0,1:T(8,128)(2,1)} %param.9) | copy-start | bytes 3932164
  1.5 18.4 %copy-start.8 = (bf16[320,2048]{1,0:T(8,128)(2,1)S(1)}, bf16[320,2048]{1,0:T(8,128)(2,1)}, u32[]{:S(2)}) copy-start(bf16[320,2048]{1,0:T(8,128)(2,1)} %param.10) | copy-start | bytes 3932164
  3.0 46.3 %all-to-all-start = ((bf16[64,4,2048]{2,1,0:T(4,128)(2,1)}), bf16[64,4,2048]{2,1,0:T(4,128)(2,1)}, u32[]{:S(2)}, u32[]{:S(2)}) async-start(bf16[64,4,2048]{2,1,0:T(4,128)(2,1)} %broadcast_in_dim.57), calls=%async_computation | async-start | bytes 2097152 | tf_op jit(solution)/shard_map/all_to_all | solution.py:33
  21.0 41.8 %collective-permute-start = (bf16[320,512]{1,0:T(8,128)(2,1)}, bf16[320,512]{1,0:T(8,128)(2,1)S(1)}, u32[]{:S(2)}, u32[]{:S(2)}) collective-permute-start(bf16[320,512]{1,0:T(8,128)(2,1)} %get-tuple-element.21), channel_id=1, source_target_pairs={{0,1},{1,0},{2,3},{3,2},{4,5},{5,4},{6,7},{7,6},{8,9},{9,8},{10,11... | collective-permute-start | bytes 983048 | tf_op jit(solution)/shard_map/ppermute | solution.py:165
  24.4 38.4 %collective-permute-start.1 = (bf16[320,512]{1,0:T(8,128)(2,1)}, bf16[320,512]{1,0:T(8,128)(2,1)S(1)}, u32[]{:S(2)}, u32[]{:S(2)}) collective-permute-start(bf16[320,512]{1,0:T(8,128)(2,1)} %get-tuple-element.23), channel_id=1, source_target_pairs={{0,8},{1,9},{2,10},{3,11},{4,12},{5,13},{6,14},{7,15},{8,0},{9,1},... | collective-permute-start | bytes 983048 | tf_op jit(solution)/shard_map/ppermute | solution.py:165
  27.7 35.0 %collective-permute-start.2 = (bf16[320,512]{1,0:T(8,128)(2,1)S(1)}, bf16[320,512]{1,0:T(8,128)(2,1)S(1)}, u32[]{:S(2)}, u32[]{:S(2)}) collective-permute-start(bf16[320,512]{1,0:T(8,128)(2,1)S(1)} %get-tuple-element.20), channel_id=1, source_target_pairs={{0,9},{1,8},{2,11},{3,10},{4,13},{5,12},{6,15},{7,14},{8,1},{9,0},... | collective-permute-start | bytes 983048 | tf_op jit(solution)/shard_map/ppermute | solution.py:165
  51.2 2.5 %copy-start.9 = (f32[2048]{0:T(1024)S(1)}, f32[2048]{0:T(1024)}, u32[]{:S(2)}) copy-start(f32[2048]{0:T(1024)} %param.7) | copy-start | bytes 24580
  53.7 2.3 %copy-start.6 = (f32[256,2048]{1,0:T(8,128)S(1)}, f32[256,2048]{1,0:T(8,128)}, u32[]{:S(2)}) copy-start(f32[256,2048]{1,0:T(8,128)} %reshape.90) | copy-start | bytes 6291460
  53.7 2.6 %copy-start.7 = (bf16[2048,320]{0,1:T(8,128)(2,1)S(1)}, bf16[2048,320]{0,1:T(8,128)(2,1)}, u32[]{:S(2)}) copy-start(bf16[2048,320]{0,1:T(8,128)(2,1)} %param.8) | copy-start | bytes 3932164
  57.9 10.7 %all-to-all-start.1 = ((bf16[4,64,768]{2,1,0:T(8,128)(2,1)}), bf16[4,64,768]{2,1,0:T(8,128)(2,1)S(1)}, u32[]{:S(2)}, u32[]{:S(2)}) async-start(bf16[4,64,768]{2,1,0:T(8,128)(2,1)} %bitcast.1), calls=%async_computation.1 | async-start | bytes 786432 | tf_op jit(solution)/shard_map/all_to_all | solution.py:185
  62.8 23.1 %copy-start.2 = (bf16[320,512]{1,0:T(8,128)(2,1)}, bf16[320,512]{1,0:T(8,128)(2,1)S(1)}, u32[]{:S(2)}) copy-start(bf16[320,512]{1,0:T(8,128)(2,1)S(1)} %collective-permute-done.1.down2) | copy-start | bytes 983044
  62.8 23.0 %copy-start.4 = (bf16[320,512]{1,0:T(8,128)(2,1)}, bf16[320,512]{1,0:T(8,128)(2,1)S(1)}, u32[]{:S(2)}) copy-start(bf16[320,512]{1,0:T(8,128)(2,1)S(1)} %collective-permute-done.2.down3) | copy-start | bytes 983044
  69.8 16.0 %all-to-all-start.2 = ((bf16[16,64,320]{2,1,0:T(8,128)(2,1)}), bf16[16,64,320]{2,1,0:T(8,128)(2,1)S(1)}, u32[]{:S(2)}, u32[]{:S(2)}) async-start(bf16[16,64,320]{2,1,0:T(8,128)(2,1)} %shard_map.77), calls=%async_computation.2 | async-start | bytes 1572864 | tf_op jit(solution)/shard_map/all_to_all | solution.py:196
  86.1 5.2 %copy-start.3 = (bf16[320,512]{1,0:T(8,128)(2,1)S(1)}, bf16[320,512]{1,0:T(8,128)(2,1)}, u32[]{:S(2)}) copy-start(bf16[320,512]{1,0:T(8,128)(2,1)} %copy-done.2) | copy-start | bytes 983044
  86.1 5.1 %copy-start.5 = (bf16[320,512]{1,0:T(8,128)(2,1)S(1)}, bf16[320,512]{1,0:T(8,128)(2,1)}, u32[]{:S(2)}) copy-start(bf16[320,512]{1,0:T(8,128)(2,1)} %copy-done.4) | copy-start | bytes 983044
  121.0 26.0 %all-to-all-start.5 = ((bf16[16,32,512]{2,1,0:T(8,128)(2,1)}), bf16[16,32,512]{2,1,0:T(8,128)(2,1)}, u32[]{:S(2)}, u32[]{:S(2)}) async-start(bf16[16,32,512]{2,1,0:T(8,128)(2,1)} %shard_map.80), calls=%async_computation.5 | async-start | bytes 1048576 | tf_op jit(solution)/shard_map/all_to_all | solution.py:226
  126.1 1.0 copy-start.1

commit v6 on v5

--- a/solution.py
+++ b/solution.py
@@ -28,76 +28,113 @@
     ]
 
 
-def spread(shard, count, axes, groups=None):
-    stacked = jnp.broadcast_to(shard[None], (count,) + shard.shape)
-    return lax.all_to_all(stacked, axes, 0, 0, axis_index_groups=groups)
-
-
-def hi_lo(value):
-    hi = lax.reduce_precision(value, 8, 7)
-    return hi.astype(jnp.bfloat16), (value - hi).astype(jnp.bfloat16)
-
-
 VMEM = pl.BlockSpec(memory_space=pltpu.VMEM)
 SMEM = pl.BlockSpec(memory_space=pltpu.SMEM)
 
 
-def call(kernel, out_shape, in_specs, flops, size):
+def call(kernel, out_shape, in_specs, flops, size, scratch=()):
     out_specs = jax.tree.map(lambda _: VMEM, out_shape)
     return pl.pallas_call(
         kernel,
         out_shape=out_shape,
         in_specs=in_specs,
         out_specs=out_specs,
+        scratch_shapes=list(scratch),
         compiler_params=pltpu.CompilerParams(vmem_limit_bytes=16 * 1024 * 1024),
         cost_estimate=pl.CostEstimate(flops=flops, bytes_accessed=size, transcendentals=0),
     )
 
 
-def residual_kernel(slot_ref, hidden_ref, drop_ref, down0, down1, down2, down3, out_ref):
+def spread_kernel(place_ref, tokens_ref, out_ref):
+    width = out_ref.shape[2]
+    tokens = tokens_ref[...].astype(jnp.float32)
+    left, right = tokens[:, :width], tokens[:, width:]
+    odd = place_ref[1] == 1
+    first = jnp.where(odd, right, left)
+    second = jnp.where(odd, left, right)
+    upper = lax.broadcasted_iota(jnp.int32, first.shape, 0) < 4
+    low = jnp.where(upper, first, pltpu.roll(second, 4, 0))
+    high = jnp.where(upper, pltpu.roll(first, 4, 0), second)
+    piece = jnp.where(place_ref[0] == 0, low, high).astype(out_ref.dtype)
+    for i in range(out_ref.shape[0]):
+        out_ref[i] = piece
+
+
+def parent_kernel(tokens_ref, gain_ref, gate_ref, up_ref, out_ref, rows_ref):
+    n_shards, _, width = tokens_ref.shape
+    local = gate_ref.shape[0]
+    lanes = out_ref.shape[1] // 2
+    step = 16
+    squares = []
+    for i in range(0, n_shards, step):
+        part = tokens_ref[i : i + step].astype(jnp.float32).reshape(step // 2, 2, 8, width)
+        even, odd = part[:, 0], part[:, 1]
+        upper = lax.broadcasted_iota(jnp.int32, even.shape, 1) < 4
+        left = jnp.where(upper, even, odd)
+        right = jnp.where(upper, odd, even)
+        rows = slice(i * 4, (i + step) * 4)
+        left = left.reshape(step * 4, width)
+        right = pltpu.roll(right, 4, 1).reshape(step * 4, width)
+        squares.append(jnp.sum(left * left + right * right, axis=1, keepdims=True))
+        rows_ref[rows, :width] = (left * gain_ref[:, :width]).astype(rows_ref.dtype)
+        rows_ref[rows, width:] = (right * gain_ref[:, width:]).astype(rows_ref.dtype)
+    squares = jnp.concatenate(squares, axis=0)
+    hi = squares.astype(jnp.bfloat16).astype(jnp.float32)
+    contract = (((1,), (1,)), ((), ()))
+    gate = lax.dot_general(rows_ref[...], gate_ref[...], contract, preferred_element_type=jnp.float32)
+    up = lax.dot_general(rows_ref[...], up_ref[...], contract, preferred_element_type=jnp.float32)
+    lane = lax.broadcasted_iota(jnp.int32, (squares.shape[0], lanes - local), 1)
+    extra = jnp.where(lane == 0, hi, jnp.where(lane == 1, squares - hi, 0.0))
+    out_ref[:, :local] = gate.astype(out_ref.dtype)
+    out_ref[:, local:lanes] = extra.astype(out_ref.dtype)
+    out_ref[:, lanes : lanes + local] = up.astype(out_ref.dtype)
+    out_ref[:, lanes + local :] = jnp.zeros_like(extra).astype(out_ref.dtype)
+
+
+def residual_kernel(slot_ref, own_ref, other_ref, drop_ref, down0, down1, down2, down3, out_ref):
     slot = slot_ref[0]
     downs = (down0, down1, down2, down3)
-    for core in range(2):
+    local = down0.shape[0]
+    for half, hidden_ref in enumerate((own_ref, other_ref)):
         total = None
         for k in range(4):
             index = slot ^ k
-            units = hidden_ref[core, index] * drop_ref[index]
+            units = hidden_ref[index][:, :local] * drop_ref[index]
             term = jnp.dot(units, downs[k][...], preferred_element_type=jnp.float32)
             total = term if total is None else total + term
-        out_ref[core] = (-total).astype(out_ref.dtype)
-
-
-def select_kernel(names_ref, hidden_ref, out_ref):
-    local = hidden_ref.shape[3]
-    rows = hidden_ref.shape[2]
+        out_ref[half] = (-total).astype(out_ref.dtype)
+
+
+def select_kernel(names_ref, own_ref, other_ref, out_ref):
+    rows = own_ref.shape[1]
     count = names_ref.shape[1]
+    local = count
     for pair in range(2):
         names = names_ref[pair]
-        for core in range(2):
+        for half, hidden_ref in enumerate((own_ref, other_ref)):
             total = None
             for i in range(2):
                 units = lax.broadcasted_iota(jnp.int32, (count, local), 1) + i * local
                 picker = jnp.where(units == names, 1.0, 0.0).astype(jnp.bfloat16)
                 term = lax.dot_general(
                     picker,
-                    hidden_ref[core, 2 * pair + i],
+                    hidden_ref[2 * pair + i][:, :local],
                     (((1,), (1,)), ((), ())),
                     preferred_element_type=jnp.float32,
                 )
                 total = term if total is None else total + term
-            out_ref[pair, :, core * rows : (core + 1) * rows] = total.astype(out_ref.dtype)
-
-
-def hidden_kernel(sums_ref, out_ref):
-    local = out_ref.shape[2]
+            out_ref[pair, :, half * rows : (half + 1) * rows] = total.astype(out_ref.dtype)
+
+
+def hidden_kernel(local, sums_ref, out_ref):
     total = sums_ref[0].astype(jnp.float32)
     for i in range(1, sums_ref.shape[0]):
         total = total + sums_ref[i].astype(jnp.float32)
     squares = total[:, local : local + 1] + total[:, local + 1 : local + 2]
     scale = lax.rsqrt(squares / D + 1e-05)
     half = total.shape[1] // 2
-    gate = total[:, :local] * scale
-    up = total[:, half : half + local] * scale
+    gate = total[:, :half] * scale
+    up = total[:, half:] * scale
     hidden = (gate / (1.0 + jnp.exp(-gate)) * up).astype(out_ref.dtype)
     for i in range(out_ref.shape[0]):
         out_ref[i] = hidden
@@ -140,7 +177,10 @@
     lanes = columns[:, :128]
     for i in range(1, width // 128):
         lanes = lanes + columns[:, i * 128 : (i + 1) * 128]
-    error_ref[...] = lanes
+    line = lax.broadcasted_iota(jnp.int32, (8, 128), 0)
+    lanes = jnp.where(line == 0, lanes, 0.0)
+    for i in range(error_ref.shape[0]):
+        error_ref[i] = lanes
 
 
 def per_device(tokens, norm_gain, gate_parent, up_parent, down_parent, kept):
@@ -155,8 +195,14 @@
     blocks = block_groups()
 
     half = tokens.shape[0] // 2
-    mine = lax.dynamic_slice_in_dim(tokens, core * half, half, 0)
-    gathered = spread(mine, n_wide, "wide").reshape(n_wide * half, width)
+    pieces = call(
+        spread_kernel,
+        jax.ShapeDtypeStruct((n_wide, 2 * half, width // 2), jnp.bfloat16),
+        [SMEM, VMEM],
+        0,
+        2 * n_wide * half * width,
+    )(jnp.stack([core, wide % 2]), tokens)
+    gathered = lax.all_to_all(pieces, "wide", 0, 0)
 
     quarter = down_parent.shape[1] // 4
     downs = [lax.dynamic_slice_in_dim(down_parent, (slot ^ k) * quarter, quarter, 1) for k in range(4)]
@@ -164,29 +210,22 @@
         perm = [(w, w ^ ((k // 2) * SIDE + k % 2)) for w in range(n_wide)]
         downs[k] = lax.ppermute(downs[k], "wide", perm)
 
-    widths = gathered.astype(jnp.float32)
-    squares = jnp.sum(widths * widths, axis=1)
-    gained = (widths * norm_gain[None, :]).astype(jnp.bfloat16)
-    sq_hi, sq_lo = hi_lo(squares)
     pad = (-local) % 128
-    lanes = lax.broadcasted_iota(jnp.int32, (n_wide * half, pad), 1)
-    extra = jnp.where(lanes == 0, sq_hi[:, None], jnp.where(lanes == 1, sq_lo[:, None], jnp.zeros((), jnp.bfloat16)))
-    partial = jnp.concatenate(
-        [
-            jnp.dot(gained, gate_parent, preferred_element_type=jnp.float32).astype(jnp.bfloat16),
-            extra,
-            jnp.dot(gained, up_parent, preferred_element_type=jnp.float32).astype(jnp.bfloat16),
-            jnp.zeros((n_wide * half, pad), jnp.bfloat16),
-        ],
-        axis=1,
-    )
+    partial = call(
+        parent_kernel,
+        jax.ShapeDtypeStruct((n_wide * half, 2 * (local + pad)), jnp.bfloat16),
+        [VMEM] * 4,
+        4 * n_wide * half * width * local,
+        8 * width * local,
+        [pltpu.VMEM((n_wide * half, width), jnp.bfloat16)],
+    )(gathered, norm_gain.reshape(1, width), gate_parent.T, up_parent.T)
     rows = n_wide * half // n_tok
 
     scattered = lax.all_to_all(partial.reshape(n_tok, rows, 2 * (local + pad)), "tok", 0, 0)
     scattered, *downs = lax.optimization_barrier((scattered, *downs))
     hidden = call(
-        hidden_kernel,
-        jax.ShapeDtypeStruct((4 * n_tok, rows, local), jnp.bfloat16),
+        functools.partial(hidden_kernel, local),
+        jax.ShapeDtypeStruct((4 * n_tok, rows, local + pad), jnp.bfloat16),
         [VMEM],
         0,
         16 * rows * local,
@@ -194,7 +233,8 @@
 
     groups = [[t * n_wide + w for w in block for t in range(n_tok)] for block in blocks]
     hidden = lax.all_to_all(hidden, ("tok", "wide"), 0, 0, axis_index_groups=groups)
-    hidden = spread(hidden, 2, "var").reshape(2, 4, n_tok * rows, local)
+    hidden = hidden.reshape(4, n_tok * rows, local + pad)
+    other = lax.ppermute(hidden, "var", [(0, 1), (1, 0)])
     total_rows = 2 * n_tok * rows
 
     var_kept = kept[0]
@@ -215,10 +255,10 @@
     shares = call(
         residual_kernel,
         jax.ShapeDtypeStruct((2, total_rows // 2, quarter), jnp.bfloat16),
-        [SMEM] + [VMEM] * 6,
+        [SMEM] + [VMEM] * 7,
         product_flops,
         4 * total_rows * quarter,
-    )(slot.reshape(1), hidden, drop, *downs)
+    )(slot.reshape(1), hidden, other, drop, *downs)
     shares = shares.reshape(n_blocks, total_rows // n_blocks, quarter)
     strides = stride_groups()
     shares = lax.all_to_all(shares, "wide", 0, 0, axis_index_groups=strides)
@@ -228,10 +268,10 @@
     chosen = call(
         select_kernel,
         jax.ShapeDtypeStruct((2, 2 * block, total_rows), jnp.bfloat16),
-        [VMEM] * 2,
+        [VMEM] * 3,
         4 * total_rows * local * 4 * block,
         4 * total_rows * local,
-    )(names, hidden)
+    )(names, hidden, other)
     factor = 1.0 / math.sqrt(total_rows)
     grad = call(
         functools.partial(gradient_kernel, factor),
@@ -245,13 +285,13 @@
         interleave_kernel,
         (
             jax.ShapeDtypeStruct((block, 4 * quarter), jnp.bfloat16),
-            jax.ShapeDtypeStruct((1, 128), jnp.float32),
+            jax.ShapeDtypeStruct((n_tok, 8, 128), jnp.float32),
         ),
         [VMEM],
         0,
         4 * block * quarter,
     )(swapped)
-    loss = jnp.sum(lax.psum(errors, "tok")) / (total_rows * D)
+    loss = jnp.sum(lax.all_to_all(errors, "tok", 0, 0)) / (total_rows * D)
     return (loss.reshape(1), grad[None])
 
 

time: 175 us -> 168 us (0.960)
  the two profiles are of different devices: /device:TPU:2 before, /device:TPU:8 now
where the time goes in v6:
time: 168 us; the launch traced here: 167 us
  waiting for transfers between devices  52.2 us (31%)
  blocking collectives  50.7 us (30%)
  starting transfers between devices  44.1 us (26%)
  Pallas kernels  10.3 us (6%)
  local copies, waits for them, and re-layouts  5.77 us (3%)
  between operations  2.64 us (2%)
  other arithmetic  1.81 us (1%)
    all_to_all x1, blocking collectives, per_device(): shares = lax.all_to_all(shares, 'wide', 0, 0, axis_index_groups=strides)  24.3 us
    all_to_all x1, waiting for transfers between devices, per_device(): gathered = lax.all_to_all(pieces, 'wide', 0, 0)  18.8 us
    all_to_all x1, blocking collectives, per_device(): swapped = lax.all_to_all(grad, 'wide', 0, 0, axis_index_groups=blocks)  18 us
    all_to_all x1, starting transfers between devices, per_device(): gathered = lax.all_to_all(pieces, 'wide', 0, 0)  16.6 us
    all_to_all x1, waiting for transfers between devices, per_device(): lax.all_to_all(pieces, 'wide', 0, 0, axis_index_groups=strides)  15.2 us
    all_to_all x1, waiting for transfers between devices, per_device(): lax.all_to_all(hidden, ('tok', 'wide'), 0, 0, axis_index_groups=groups)  9.86 us
    ppermute x3, starting transfers between devices, per_device(): downs[k] = lax.ppermute(downs[k], 'wide', perm)  9.2 us
    all_to_all x1, blocking collectives, per_device(): loss = jnp.sum(lax.all_to_all(errors, 'tok', 0, 0)) / (total_rows * D)  8.43 us
  transfers between devices with their start and end apart: 8, of which 6 were waited for; matrix products, arithmetic and copies ran while one was open for 2% of the time, Pallas kernels for 2%

profile of v6, /device:TPU:8, one launch (start us, length us, event | category | flops | bytes accessed | tf_op | source)
XLA Modules:
  0.0 167.5 jit_solution(15238581743866472581)
XLA Ops:
  0.6 0.1 pad_add_fusion.place_ref
  0.7 0.0 copy-start.4
  0.7 0.8 copy-done.4
  1.5 1.6 shard_map.77
  3.1 16.6 %all-to-all-start = ((bf16[64,8,1024]{2,1,0:T(8,128)(2,1)}), bf16[64,8,1024]{2,1,0:T(8,128)(2,1)S(1)}, u32[]{:S(2)}, u32[]{:S(2)}) async-start(bf16[64,8,1024]{2,1,0:T(8,128)(2,1)} %shard_map.77), calls=%async_computation | async-start | bytes 2097152 | tf_op jit(solution)/shard_map/all_to_all | solution.py:205
  19.8 0.0 copy-start
  19.8 0.0 copy-start.5
  19.8 2.4 %constant_dynamic-slice_fusion = (bf16[320,512]{1,0:T(8,128)(2,1)}, bf16[320,512]{1,0:T(8,128)(2,1)}, bf16[320,512]{1,0:T(8,128)(2,1)S(1)}, bf16[320,512]{1,0:T(8,128)(2,1)}) fusion(bf16[320,2048]{1,0:T(8,128)(2,1)} %param.10, s32[]{:T(128)S(6)} %select_n.84, s32[]{:T(128)S(6)} %select_n.82, s32[]{:T(128)S(6)} %select_n.81, s32[]{:T(128)S(6)} %select_n.83), kind=kLoop, calls=%fused_computation.10 | loop fusion | bytes 2621456 | tf_op jit(solution)/shard_map/dynamic_slice | solution.py:208
  22.2 3.4 %collective-permute-start = (bf16[320,512]{1,0:T(8,128)(2,1)}, bf16[320,512]{1,0:T(8,128)(2,1)S(1)}, u32[]{:S(2)}, u32[]{:S(2)}) collective-permute-start(bf16[320,512]{1,0:T(8,128)(2,1)} %get-tuple-element.21), channel_id=1, source_target_pairs={{0,1},{1,0},{2,3},{3,2},{4,5},{5,4},{6,7},{7,6},{8,9},{9,8},{10,11... | collective-permute-start | bytes 983048 | tf_op jit(solution)/shard_map/ppermute | solution.py:211
  25.6 2.5 %collective-permute-start.1 = (bf16[320,512]{1,0:T(8,128)(2,1)}, bf16[320,512]{1,0:T(8,128)(2,1)S(1)}, u32[]{:S(2)}, u32[]{:S(2)}) collective-permute-start(bf16[320,512]{1,0:T(8,128)(2,1)} %get-tuple-element.23), channel_id=1, source_target_pairs={{0,8},{1,9},{2,10},{3,11},{4,12},{5,13},{6,14},{7,15},{8,0},{9,1},... | collective-permute-start | bytes 983048 | tf_op jit(solution)/shard_map/ppermute | solution.py:211
  28.0 3.4 %collective-permute-start.2 = (bf16[320,512]{1,0:T(8,128)(2,1)}, bf16[320,512]{1,0:T(8,128)(2,1)}, u32[]{:S(2)}, u32[]{:S(2)}) collective-permute-start(bf16[320,512]{1,0:T(8,128)(2,1)} %get-tuple-element.20), channel_id=1, source_target_pairs={{0,9},{1,8},{2,11},{3,10},{4,13},{5,12},{6,15},{7,14},{8,1},{9,0},... | collective-permute-start | bytes 983048 | tf_op jit(solution)/shard_map/ppermute | solution.py:211
  31.4 18.8 %all-to-all-done.tokens_ref = bf16[64,8,1024]{2,1,0:T(8,128)(2,1)S(1)} async-done(((bf16[64,8,1024]{2,1,0:T(8,128)(2,1)}), bf16[64,8,1024]{2,1,0:T(8,128)(2,1)S(1)}, u32[]{:S(2)}, u32[]{:S(2)}) %all-to-all-start) | async-done | bytes 1048608 | tf_op jit(solution)/shard_map/all_to_all | solution.py:205
  50.2 0.0 copy-done
  50.2 0.0 copy-done.5
  50.2 0.0 copy-start.1
  50.2 1.3 copy-done.1
  51.6 2.1 %shard_map.78 = bf16[256,768]{1,0:T(8,128)(2,1)} custom-call(bf16[64,8,1024]{2,1,0:T(8,128)(2,1)S(1)} %all-to-all-done.tokens_ref, f32[1,2048]{1,0:T(1,128)S(1)} %bitcast.21, bf16[320,2048]{1,0:T(8,128)(2,1)S(1)} %bitcast.19, bf16[320,2048]{1,0:T(8,128)(2,1)S(1)} %bitcast.20), custom_call_target="tpu_custom_call" | custom-call | flops 671088640 | bytes 5242880 | tf_op jit(solution)/shard_map/pallas_call | solution.py:214
  53.7 4.3 %all-to-all-start.1 = ((bf16[4,64,768]{2,1,0:T(8,128)(2,1)}), bf16[4,64,768]{2,1,0:T(8,128)(2,1)S(1)}, u32[]{:S(2)}, u32[]{:S(2)}) async-start(bf16[4,64,768]{2,1,0:T(8,128)(2,1)} %bitcast.6), calls=%async_computation.1 | async-start | bytes 786432 | tf_op jit(solution)/shard_map/all_to_all | solution.py:224
  57.9 1.0 collective-permute-done.down1
  58.9 0.0 collective-permute-done.1.down2
  58.9 0.0 copy-start.2
  58.9 0.0 collective-permute-done.2.down3
  58.9 6.4 %all-to-all-done.1.sums_ref = bf16[4,64,768]{2,1,0:T(8,128)(2,1)S(1)} async-done(((bf16[4,64,768]{2,1,0:T(8,128)(2,1)}), bf16[4,64,768]{2,1,0:T(8,128)(2,1)S(1)}, u32[]{:S(2)}, u32[]{:S(2)}) %all-to-all-start.1) | async-done | bytes 393248 | tf_op jit(solution)/shard_map/all_to_all | solution.py:224
  65.3 1.2 shard_map.79
  66.5 0.0 copy-done.2
  66.5 4.1 %all-to-all-start.2 = ((bf16[16,64,384]{2,1,0:T(8,128)(2,1)}), bf16[16,64,384]{2,1,0:T(8,128)(2,1)S(1)}, u32[]{:S(2)}, u32[]{:S(2)}) async-start(bf16[16,64,384]{2,1,0:T(8,128)(2,1)} %shard_map.79), calls=%async_computation.2 | async-start | bytes 1572864 | tf_op jit(solution)/shard_map/all_to_all | solution.py:235
  70.6 9.9 %all-to-all-done.2 = bf16[16,64,384]{2,1,0:T(8,128)(2,1)S(1)} async-done(((bf16[16,64,384]{2,1,0:T(8,128)(2,1)}), bf16[16,64,384]{2,1,0:T(8,128)(2,1)S(1)}, u32[]{:S(2)}, u32[]{:S(2)}) %all-to-all-start.2) | async-done | bytes 786464 | tf_op jit(solution)/shard_map/all_to_all | solution.py:235
  80.5 1.9 %collective-permute-start.3 = (bf16[4,256,384]{2,1,0:T(8,128)(2,1)S(1)}, bf16[4,256,384]{2,1,0:T(8,128)(2,1)S(1)}, u32[]{:S(2)}, u32[]{:S(2)}) collective-permute-start(bf16[4,256,384]{2,1,0:T(8,128)(2,1)S(1)} %bitcast.14), channel_id=1, source_target_pairs={{0,256},{256,0},{1,257},{257,1},{2,258},{258,2},{3,259},{259,3},{4... | collective-permute-start | bytes 2359304 | tf_op jit(solution)/shard_map/ppermute | solution.py:237
  82.4 0.8 fusion.2
  83.2 0.3 fusion
  83.5 0.1 convert_element_type.30
  83.6 0.1 convert_element_type.31
  83.7 0.9 collective-permute-done.3.other_ref
  84.6 0.0 copy-start.3
  84.6 1.0 copy-done.3
  85.6 2.2 %shard_map.81 = bf16[2,256,512]{2,1,0:T(8,128)(2,1)S(1)} custom-call(s32[1]{0:T(128)} %bitcast.8.slot_ref, bf16[4,256,384]{2,1,0:T(8,128)(2,1)S(1)} %bitcast.15, bf16[4,256,384]{2,1,0:T(8,128)(2,1)S(1)} %collective-permute-done.3.other_ref, bf16[4,1,320]{2,1,0:T(2,128)(2,1)S(1)} %pad_maximum_fusion.drop_ref, bf16[320,512]{1,0:T(8,128)(2,1)S(1)} %get-tuple-element.10.down0, ...), custom_call_target="tpu_custom_call" | custom-call | flops 671088640 | bytes 1048576 | tf_op jit(solution)/shard_map/pallas_call | solution.py:255
  87.8 24.3 %all_to_all.35.shares_ref = bf16[16,32,512]{2,1,0:T(8,128)(2,1)S(1)} all-to-all(bf16[16,32,512]{2,1,0:T(8,128)(2,1)S(1)} %bitcast.17), channel_id=1, replica_groups={{0,2,4,6,16,18,20,22,32,34,36,38,48,50,52,54},{1,3,5,7,17,19,21,23,33,3..., dimensions={0} | all-to-all | bytes 1048576 | tf_op jit(solution)/shard_map/all_to_all | solution.py:264
  112.1 0.9 shard_map.82
  113.0 8.0 %all-to-all-start.4 = ((bf16[16,32,512]{2,1,0:T(8,128)(2,1)}), bf16[16,32,512]{2,1,0:T(8,128)(2,1)S(1)}, u32[]{:S(2)}, u32[]{:S(2)}) async-start(bf16[16,32,512]{2,1,0:T(8,128)(2,1)} %shard_map.82), calls=%async_computation.4 | async-start | bytes 1048576 | tf_op jit(solution)/shard_map/all_to_all | solution.py:266
  121.0 0.2 copy.11.names_ref
  121.2 0.9 shard_map.80.chosen_ref
  122.2 15.2 %all-to-all-done.4 = bf16[16,32,512]{2,1,0:T(8,128)(2,1)S(1)} async-done(((bf16[16,32,512]{2,1,0:T(8,128)(2,1)}), bf16[16,32,512]{2,1,0:T(8,128)(2,1)S(1)}, u32[]{:S(2)}, u32[]{:S(2)}) %all-to-all-start.4) | async-done | bytes 524320 | tf_op jit(solution)/shard_map/all_to_all | solution.py:266
  137.3 0.5 shard_map.83
  137.8 18.0 %all_to_all.36.in_ref = bf16[4,176,512]{2,1,0:T(8,128)(2,1)S(1)} all-to-all(bf16[4,176,512]{2,1,0:T(8,128)(2,1)S(1)} %shard_map.83), channel_id=1, replica_groups={{0,1,8,9},{2,3,10,11},{4,5,12,13},{6,7,14,15},{16,17,24,25},{18,19,26,2..., dimensions={0} | all-to-all | bytes 1441792 | tf_op jit(solution)/shard_map/all_to_all | solution.py:283
  155.8 0.9 shard_map.84
  156.7 8.4 %all_to_all.37 = f32[4,8,128]{2,1,0:T(8,128)S(1)} all-to-all(f32[4,8,128]{2,1,0:T(8,128)S(1)} %get-tuple-element.14), channel_id=1, replica_groups=mesh['var'=2,'tok'=4,'wide'=64] {'tok'}, dimensions={0} | all-to-all | bytes 32768 | tf_op jit(solution)/shard_map/all_to_all | solution.py:294
  165.1 0.6 reduce_sum.9
  (4 shorter events, 0.0 us)
Async XLA Ops:
  0.7 0.8 copy-start.4
  3.1 47.1 %all-to-all-start = ((bf16[64,8,1024]{2,1,0:T(8,128)(2,1)}), bf16[64,8,1024]{2,1,0:T(8,128)(2,1)S(1)}, u32[]{:S(2)}, u32[]{:S(2)}) async-start(bf16[64,8,1024]{2,1,0:T(8,128)(2,1)} %shard_map.77), calls=%async_computation | async-start | bytes 2097152 | tf_op jit(solution)/shard_map/all_to_all | solution.py:205
  19.8 30.5 %copy-start = (bf16[2048,320]{0,1:T(8,128)(2,1)S(1)}, bf16[2048,320]{0,1:T(8,128)(2,1)}, u32[]{:S(2)}) copy-start(bf16[2048,320]{0,1:T(8,128)(2,1)} %param.8) | copy-start | bytes 3932164
  19.8 30.4 %copy-start.5 = (f32[2048]{0:T(1024)S(1)}, f32[2048]{0:T(1024)}, u32[]{:S(2)}) copy-start(f32[2048]{0:T(1024)} %param.7) | copy-start | bytes 24580
  22.2 36.7 %collective-permute-start = (bf16[320,512]{1,0:T(8,128)(2,1)}, bf16[320,512]{1,0:T(8,128)(2,1)S(1)}, u32[]{:S(2)}, u32[]{:S(2)}) collective-permute-start(bf16[320,512]{1,0:T(8,128)(2,1)} %get-tuple-element.21), channel_id=1, source_target_pairs={{0,1},{1,0},{2,3},{3,2},{4,5},{5,4},{6,7},{7,6},{8,9},{9,8},{10,11... | collective-permute-start | bytes 983048 | tf_op jit(solution)/shard_map/ppermute | solution.py:211
  25.6 33.4 %collective-permute-start.1 = (bf16[320,512]{1,0:T(8,128)(2,1)}, bf16[320,512]{1,0:T(8,128)(2,1)S(1)}, u32[]{:S(2)}, u32[]{:S(2)}) collective-permute-start(bf16[320,512]{1,0:T(8,128)(2,1)} %get-tuple-element.23), channel_id=1, source_target_pairs={{0,8},{1,9},{2,10},{3,11},{4,12},{5,13},{6,14},{7,15},{8,0},{9,1},... | collective-permute-start | bytes 983048 | tf_op jit(solution)/shard_map/ppermute | solution.py:211
  28.0 30.9 %collective-permute-start.2 = (bf16[320,512]{1,0:T(8,128)(2,1)}, bf16[320,512]{1,0:T(8,128)(2,1)}, u32[]{:S(2)}, u32[]{:S(2)}) collective-permute-start(bf16[320,512]{1,0:T(8,128)(2,1)} %get-tuple-element.20), channel_id=1, source_target_pairs={{0,9},{1,8},{2,11},{3,10},{4,13},{5,12},{6,15},{7,14},{8,1},{9,0},... | collective-permute-start | bytes 983048 | tf_op jit(solution)/shard_map/ppermute | solution.py:211
  50.2 1.3 copy-start.1
  53.7 11.7 %all-to-all-start.1 = ((bf16[4,64,768]{2,1,0:T(8,128)(2,1)}), bf16[4,64,768]{2,1,0:T(8,128)(2,1)S(1)}, u32[]{:S(2)}, u32[]{:S(2)}) async-start(bf16[4,64,768]{2,1,0:T(8,128)(2,1)} %bitcast.6), calls=%async_computation.1 | async-start | bytes 786432 | tf_op jit(solution)/shard_map/all_to_all | solution.py:224
  58.9 7.6 %copy-start.2 = (bf16[320,512]{1,0:T(8,128)(2,1)}, bf16[320,512]{1,0:T(8,128)(2,1)S(1)}, u32[]{:S(2)}) copy-start(bf16[320,512]{1,0:T(8,128)(2,1)S(1)} %collective-permute-done.1.down2) | copy-start | bytes 983044
  66.5 14.0 %all-to-all-start.2 = ((bf16[16,64,384]{2,1,0:T(8,128)(2,1)}), bf16[16,64,384]{2,1,0:T(8,128)(2,1)S(1)}, u32[]{:S(2)}, u32[]{:S(2)}) async-start(bf16[16,64,384]{2,1,0:T(8,128)(2,1)} %shard_map.79), calls=%async_computation.2 | async-start | bytes 1572864 | tf_op jit(solution)/shard_map/all_to_all | solution.py:235
  80.5 4.2 %collective-permute-start.3 = (bf16[4,256,384]{2,1,0:T(8,128)(2,1)S(1)}, bf16[4,256,384]{2,1,0:T(8,128)(2,1)S(1)}, u32[]{:S(2)}, u32[]{:S(2)}) collective-permute-start(bf16[4,256,384]{2,1,0:T(8,128)(2,1)S(1)} %bitcast.14), channel_id=1, source_target_pairs={{0,256},{256,0},{1,257},{257,1},{2,258},{258,2},{3,259},{259,3},{4... | collective-permute-start | bytes 2359304 | tf_op jit(solution)/shard_map/ppermute | solution.py:237
  84.6 1.0 copy-start.3
  113.0 24.3 %all-to-all-start.4 = ((bf16[16,32,512]{2,1,0:T(8,128)(2,1)}), bf16[16,32,512]{2,1,0:T(8,128)(2,1)S(1)}, u32[]{:S(2)}, u32[]{:S(2)}) async-start(bf16[16,32,512]{2,1,0:T(8,128)(2,1)} %shard_map.82), calls=%async_computation.4 | async-start | bytes 1048576 | tf_op jit(solution)/shard_map/all_to_all | solution.py:266

commit v7 on v6

--- a/solution.py
+++ b/solution.py
@@ -30,6 +30,7 @@
 
 VMEM = pl.BlockSpec(memory_space=pltpu.VMEM)
 SMEM = pl.BlockSpec(memory_space=pltpu.SMEM)
+HBM = pl.BlockSpec(memory_space=pltpu.HBM)
 
 
 def call(kernel, out_shape, in_specs, flops, size, scratch=()):
@@ -60,7 +61,13 @@
         out_ref[i] = piece
 
 
-def parent_kernel(tokens_ref, gain_ref, gate_ref, up_ref, out_ref, rows_ref):
+def parent_kernel(tokens_ref, gain_ref, gate_hbm, up_hbm, out_ref, rows_ref, gate_ref, up_ref, sems):
+    copies = [
+        pltpu.make_async_copy(src, dst, sems.at[i])
+        for i, (src, dst) in enumerate(((gate_hbm, gate_ref), (up_hbm, up_ref)))
+    ]
+    for copy in copies:
+        copy.start()
     n_shards, _, width = tokens_ref.shape
     local = gate_ref.shape[0]
     lanes = out_ref.shape[1] // 2
@@ -81,7 +88,9 @@
     squares = jnp.concatenate(squares, axis=0)
     hi = squares.astype(jnp.bfloat16).astype(jnp.float32)
     contract = (((1,), (1,)), ((), ()))
+    copies[0].wait()
     gate = lax.dot_general(rows_ref[...], gate_ref[...], contract, preferred_element_type=jnp.float32)
+    copies[1].wait()
     up = lax.dot_general(rows_ref[...], up_ref[...], contract, preferred_element_type=jnp.float32)
     lane = lax.broadcasted_iota(jnp.int32, (squares.shape[0], lanes - local), 1)
     extra = jnp.where(lane == 0, hi, jnp.where(lane == 1, squares - hi, 0.0))
@@ -91,39 +100,48 @@
     out_ref[:, lanes + local :] = jnp.zeros_like(extra).astype(out_ref.dtype)
 
 
-def residual_kernel(slot_ref, own_ref, other_ref, drop_ref, down0, down1, down2, down3, out_ref):
+def residual_kernel(slot_ref, own_hbm, other_hbm, drop_ref, down0, down1, down2, down3, out_ref, own_ref, other_ref, down_ref, sems):
     slot = slot_ref[0]
-    downs = (down0, down1, down2, down3)
-    local = down0.shape[0]
+    local = down_ref.shape[1]
+    copies = [pltpu.make_async_copy(own_hbm, own_ref, sems.at[0])]
+    for k, down in enumerate((down0, down1, down2, down3)):
+        copies.append(pltpu.make_async_copy(down, down_ref.at[k], sems.at[1 + k]))
+    copies.append(pltpu.make_async_copy(other_hbm, other_ref, sems.at[5]))
+    for copy in copies:
+        copy.start()
+    copies[0].wait()
+    for half, hidden_ref in enumerate((own_ref, other_ref)):
+        if half == 1:
+            copies[5].wait()
+        total = None
+        for k in range(4):
+            if half == 0:
+                copies[1 + k].wait()
+            index = slot ^ k
+            units = hidden_ref[index][:, :local] * drop_ref[index]
+            term = jnp.dot(units, down_ref[k], preferred_element_type=jnp.float32)
+            total = term if total is None else total + term
+        out_ref[half] = (-total).astype(out_ref.dtype)
+
+
+def select_kernel(pair, names_ref, own_ref, other_ref, out_ref):
+    rows = own_ref.shape[1]
+    count = names_ref.shape[0]
+    local = count
+    names = names_ref[...]
     for half, hidden_ref in enumerate((own_ref, other_ref)):
         total = None
-        for k in range(4):
-            index = slot ^ k
-            units = hidden_ref[index][:, :local] * drop_ref[index]
-            term = jnp.dot(units, downs[k][...], preferred_element_type=jnp.float32)
+        for i in range(2):
+            units = lax.broadcasted_iota(jnp.int32, (count, local), 1) + i * local
+            picker = jnp.where(units == names, 1.0, 0.0).astype(jnp.bfloat16)
+            term = lax.dot_general(
+                picker,
+                hidden_ref[2 * pair + i][:, :local],
+                (((1,), (1,)), ((), ())),
+                preferred_element_type=jnp.float32,
+            )
             total = term if total is None else total + term
-        out_ref[half] = (-total).astype(out_ref.dtype)
-
-
-def select_kernel(names_ref, own_ref, other_ref, out_ref):
-    rows = own_ref.shape[1]
-    count = names_ref.shape[1]
-    local = count
-    for pair in range(2):
-        names = names_ref[pair]
-        for half, hidden_ref in enumerate((own_ref, other_ref)):
-            total = None
-            for i in range(2):
-                units = lax.broadcasted_iota(jnp.int32, (count, local), 1) + i * local
-                picker = jnp.where(units == names, 1.0, 0.0).astype(jnp.bfloat16)
-                term = lax.dot_general(
-                    picker,
-                    hidden_ref[2 * pair + i][:, :local],
-                    (((1,), (1,)), ((), ())),
-                    preferred_element_type=jnp.float32,
-                )
-                total = term if total is None else total + term
-            out_ref[pair, :, half * rows : (half + 1) * rows] = total.astype(out_ref.dtype)
+        out_ref[:, half * rows : (half + 1) * rows] = total.astype(out_ref.dtype)
 
 
 def hidden_kernel(local, sums_ref, out_ref):
@@ -149,38 +167,25 @@
         out_ref[i] = piece
 
 
-def gradient_kernel(factor, chosen_ref, rounded_ref, out_ref):
+def gradient_kernel(factor, first_ref, second_ref, rounded_ref, out_ref, error_ref):
     rounded = rounded_ref[...]
-    block = chosen_ref.shape[1] // 2
-    for pair in range(2):
-        product = jnp.dot(chosen_ref[pair], rounded, preferred_element_type=jnp.float32) * factor
+    block = out_ref.shape[1]
+    for pair, chosen_ref in enumerate((first_ref, second_ref)):
+        product = jnp.dot(chosen_ref[...], rounded, preferred_element_type=jnp.float32) * factor
         for i in range(2):
-            out_ref[2 * pair + i, :block] = product[i * block : (i + 1) * block].astype(out_ref.dtype)
+            out_ref[2 * pair + i] = product[i * block : (i + 1) * block].astype(out_ref.dtype)
     errors = rounded.astype(jnp.float32)
     columns = jnp.sum(errors * errors, axis=0, keepdims=True)
-    hi = columns.astype(out_ref.dtype).astype(jnp.float32)
-    line = lax.broadcasted_iota(jnp.int32, (16, columns.shape[1]), 0)
-    extra = jnp.where(line == 0, hi, jnp.where(line == 1, columns - hi, 0.0)).astype(out_ref.dtype)
-    for i in range(4):
-        out_ref[i, block:] = extra
-
-
-def interleave_kernel(in_ref, out_ref, error_ref):
-    block = out_ref.shape[0]
+    lanes = columns[:, :128]
+    for i in range(1, columns.shape[1] // 128):
+        lanes = lanes + columns[:, i * 128 : (i + 1) * 128]
+    error_ref[...] = lanes
+
+
+def interleave_kernel(in_ref, out_ref):
     width = in_ref.shape[2]
-    total = None
     for i in range(in_ref.shape[0]):
-        out_ref[:, i * width : (i + 1) * width] = in_ref[i, :block]
-        term = in_ref[i, block:].astype(jnp.float32)
-        total = term if total is None else total + term
-    columns = jnp.sum(total, axis=0, keepdims=True)
-    lanes = columns[:, :128]
-    for i in range(1, width // 128):
-        lanes = lanes + columns[:, i * 128 : (i + 1) * 128]
-    line = lax.broadcasted_iota(jnp.int32, (8, 128), 0)
-    lanes = jnp.where(line == 0, lanes, 0.0)
-    for i in range(error_ref.shape[0]):
-        error_ref[i] = lanes
+        out_ref[:, i * width : (i + 1) * width] = in_ref[i]
 
 
 def per_device(tokens, norm_gain, gate_parent, up_parent, down_parent, kept):
@@ -214,10 +219,15 @@
     partial = call(
         parent_kernel,
         jax.ShapeDtypeStruct((n_wide * half, 2 * (local + pad)), jnp.bfloat16),
-        [VMEM] * 4,
+        [VMEM] * 2 + [HBM] * 2,
         4 * n_wide * half * width * local,
         8 * width * local,
-        [pltpu.VMEM((n_wide * half, width), jnp.bfloat16)],
+        [
+            pltpu.VMEM((n_wide * half, width), jnp.bfloat16),
+            pltpu.VMEM((local, width), jnp.bfloat16),
+            pltpu.VMEM((local, width), jnp.bfloat16),
+            pltpu.SemaphoreType.DMA((2,)),
+        ],
     )(gathered, norm_gain.reshape(1, width), gate_parent.T, up_parent.T)
     rows = n_wide * half // n_tok
 
@@ -233,10 +243,6 @@
 
     groups = [[t * n_wide + w for w in block for t in range(n_tok)] for block in blocks]
     hidden = lax.all_to_all(hidden, ("tok", "wide"), 0, 0, axis_index_groups=groups)
-    hidden = hidden.reshape(4, n_tok * rows, local + pad)
-    other = lax.ppermute(hidden, "var", [(0, 1), (1, 0)])
-    total_rows = 2 * n_tok * rows
-
     var_kept = kept[0]
     block = var_kept.shape[0] // n_wide
     names = []
@@ -247,51 +253,70 @@
         names.append(name)
         matches = jnp.arange(2 * local, dtype=jnp.int32)[:, None] == name[None, :]
         drops.append(jnp.where(jnp.any(matches, axis=1), 0.0, 1.0).astype(jnp.bfloat16))
-    names = jnp.stack(names)[:, :, None]
+    names = [name[:, None] for name in names]
     drop = jnp.concatenate(drops).reshape(4, 1, local)
+    hidden, drop, *names = lax.optimization_barrier((hidden, drop, *names))
+    hidden = hidden.reshape(4, n_tok * rows, local + pad)
+    other = lax.ppermute(hidden, "var", [(0, 1), (1, 0)])
+    total_rows = 2 * n_tok * rows
 
     n_blocks = n_wide // 4
     product_flops = 2 * total_rows * 4 * local * quarter
     shares = call(
         residual_kernel,
         jax.ShapeDtypeStruct((2, total_rows // 2, quarter), jnp.bfloat16),
-        [SMEM] + [VMEM] * 7,
+        [SMEM, HBM, HBM, VMEM] + [HBM] * 4,
         product_flops,
         4 * total_rows * quarter,
+        [
+            pltpu.VMEM(hidden.shape, jnp.bfloat16),
+            pltpu.VMEM(hidden.shape, jnp.bfloat16),
+            pltpu.VMEM((4, local, quarter), jnp.bfloat16),
+            pltpu.SemaphoreType.DMA((6,)),
+        ],
     )(slot.reshape(1), hidden, other, drop, *downs)
     shares = shares.reshape(n_blocks, total_rows // n_blocks, quarter)
     strides = stride_groups()
+    chosen = [
+        call(
+            functools.partial(select_kernel, pair),
+            jax.ShapeDtypeStruct((2 * block, total_rows), jnp.bfloat16),
+            [VMEM] * 3,
+            2 * total_rows * local * 4 * block,
+            2 * total_rows * local,
+        )(names[pair], hidden, other)
+        for pair in range(2)
+    ]
     shares = lax.all_to_all(shares, "wide", 0, 0, axis_index_groups=strides)
+    shares, chosen[0] = lax.optimization_barrier((shares, chosen[0]))
     pieces = call(piece_kernel, jax.ShapeDtypeStruct(shares.shape, jnp.bfloat16), [VMEM], 0, 4 * total_rows * quarter)(shares)
     rounded = lax.all_to_all(pieces, "wide", 0, 0, axis_index_groups=strides).reshape(total_rows, quarter)
 
-    chosen = call(
-        select_kernel,
-        jax.ShapeDtypeStruct((2, 2 * block, total_rows), jnp.bfloat16),
+    factor = 1.0 / math.sqrt(total_rows)
+    grad, errors = call(
+        functools.partial(gradient_kernel, factor),
+        (
+            jax.ShapeDtypeStruct((4, block, quarter), jnp.bfloat16),
+            jax.ShapeDtypeStruct((1, 128), jnp.float32),
+        ),
         [VMEM] * 3,
-        4 * total_rows * local * 4 * block,
-        4 * total_rows * local,
-    )(names, hidden, other)
-    factor = 1.0 / math.sqrt(total_rows)
-    grad = call(
-        functools.partial(gradient_kernel, factor),
-        jax.ShapeDtypeStruct((4, block + 16, quarter), jnp.bfloat16),
-        [VMEM] * 2,
         2 * total_rows * 4 * block * quarter,
         4 * total_rows * quarter,
-    )(chosen, rounded)
+    )(*chosen, rounded)
+
+    errors = lax.psum(errors, "tok")
+    errors = jnp.broadcast_to(errors, (4, 8, 128))
     swapped = lax.all_to_all(grad, "wide", 0, 0, axis_index_groups=blocks)
-    grad, errors = call(
+    swapped, errors = lax.optimization_barrier((swapped, errors))
+    errors = lax.all_to_all(errors, "wide", 0, 0, axis_index_groups=blocks)
+    loss = jnp.sum(errors[:, 0]) / (total_rows * D)
+    grad = call(
         interleave_kernel,
-        (
-            jax.ShapeDtypeStruct((block, 4 * quarter), jnp.bfloat16),
-            jax.ShapeDtypeStruct((n_tok, 8, 128), jnp.float32),
-        ),
+        jax.ShapeDtypeStruct((block, 4 * quarter), jnp.bfloat16),
         [VMEM],
         0,
         4 * block * quarter,
     )(swapped)
-    loss = jnp.sum(lax.all_to_all(errors, "tok", 0, 0)) / (total_rows * D)
     return (loss.reshape(1), grad[None])
 
 

time: 168 us -> 171 us (1.018)
  blocking collectives: 50.7 us -> 9.72 us
  starting transfers between devices: 44.1 us -> 64.9 us
  waiting for transfers between devices: 52.2 us -> 71.1 us
  Pallas kernels: 10.3 us -> 13.1 us
    all_to_all x3 -> x0, blocking collectives: 50.7 us -> none  [the longest x1 24.3 us: per_device(): shares = lax.all_to_all(shares, 'wide', 0, 0, axis_index_groups=strides)]
    all_to_all x0 -> x3, starting transfers between devices: none -> 20.9 us  [the longest x1 9.63 us: per_device(): swapped = lax.all_to_all(grad, 'wide', 0, 0, axis_index_groups=blocks)]
    all_to_all x0 -> x3, waiting for transfers between devices: none -> 18.4 us  [the longest x1 16 us: per_device(): shares = lax.all_to_all(shares, 'wide', 0, 0, axis_index_groups=strides)]
    psum x0 -> x1, blocking collectives: none -> 9.72 us  [per_device(): errors = lax.psum(errors, 'tok')]
  transfers between devices with their start and end apart: 8 -> 11, of which waited for: 6 -> 8; matrix products, arithmetic and copies ran while one was open for 2% -> 2% of each run, Pallas kernels for 2% -> 3%
where the time goes in v7:
time: 171 us; the launch traced here: 170 us
  waiting for transfers between devices  71.1 us (42%)
  starting transfers between devices  64.9 us (38%)
  Pallas kernels  13.1 us (8%)
  blocking collectives  9.72 us (6%)
  local copies, waits for them, and re-layouts  6.48 us (4%)
  between operations  2.65 us (2%)
  other arithmetic  1.79 us (1%)
    all_to_all x1, waiting for transfers between devices, per_device(): gathered = lax.all_to_all(pieces, 'wide', 0, 0)  18.8 us
    all_to_all x1, starting transfers between devices, per_device(): gathered = lax.all_to_all(pieces, 'wide', 0, 0)  16.6 us
    all_to_all x1, waiting for transfers between devices, per_device(): shares = lax.all_to_all(shares, 'wide', 0, 0, axis_index_groups=strides)  16 us
    all_to_all x1, waiting for transfers between devices, per_device(): lax.all_to_all(pieces, 'wide', 0, 0, axis_index_groups=strides)  15.7 us
    psum x1, blocking collectives, per_device(): errors = lax.psum(errors, 'tok')  9.72 us
    all_to_all x1, starting transfers between devices, per_device(): swapped = lax.all_to_all(grad, 'wide', 0, 0, axis_index_groups=blocks)  9.63 us
    ppermute x3, starting transfers between devices, per_device(): downs[k] = lax.ppermute(downs[k], 'wide', perm)  9.2 us
    all_to_all x1, waiting for transfers between devices, per_device(): lax.all_to_all(hidden, ('tok', 'wide'), 0, 0, axis_index_groups=groups)  8.56 us
  transfers between devices with their start and end apart: 11, of which 8 were waited for; matrix products, arithmetic and copies ran while one was open for 2% of the time, Pallas kernels for 3%

profile of v7, /device:TPU:8, one launch (start us, length us, event | category | flops | bytes accessed | tf_op | source)
XLA Modules:
  0.0 169.8 jit_solution(10516226824788846810)
XLA Ops:
  0.6 0.1 pad_add_fusion.place_ref
  0.7 0.0 copy-start.4
  0.7 0.8 copy-done.4
  1.5 1.7 shard_map.77
  3.1 16.6 %all-to-all-start = ((bf16[64,8,1024]{2,1,0:T(8,128)(2,1)}), bf16[64,8,1024]{2,1,0:T(8,128)(2,1)S(1)}, u32[]{:S(2)}, u32[]{:S(2)}) async-start(bf16[64,8,1024]{2,1,0:T(8,128)(2,1)} %shard_map.77), calls=%async_computation | async-start | bytes 2097152 | tf_op jit(solution)/shard_map/all_to_all | solution.py:210
  19.8 0.0 copy-start
  19.8 0.0 copy-start.5
  19.8 2.4 %constant_dynamic-slice_fusion = (bf16[320,512]{1,0:T(8,128)(2,1)}, bf16[320,512]{1,0:T(8,128)(2,1)}, bf16[320,512]{1,0:T(8,128)(2,1)S(1)}, bf16[320,512]{1,0:T(8,128)(2,1)}) fusion(bf16[320,2048]{1,0:T(8,128)(2,1)} %param.10, s32[]{:T(128)S(6)} %select_n.80, s32[]{:T(128)S(6)} %select_n.78, s32[]{:T(128)S(6)} %select_n.77, s32[]{:T(128)S(6)} %select_n.79), kind=kLoop, calls=%fused_computation.9 | loop fusion | bytes 2621456 | tf_op jit(solution)/shard_map/dynamic_slice | solution.py:213
  22.2 3.4 %collective-permute-start = (bf16[320,512]{1,0:T(8,128)(2,1)}, bf16[320,512]{1,0:T(8,128)(2,1)S(1)}, u32[]{:S(2)}, u32[]{:S(2)}) collective-permute-start(bf16[320,512]{1,0:T(8,128)(2,1)} %get-tuple-element.35), channel_id=1, source_target_pairs={{0,1},{1,0},{2,3},{3,2},{4,5},{5,4},{6,7},{7,6},{8,9},{9,8},{10,11... | collective-permute-start | bytes 983048 | tf_op jit(solution)/shard_map/ppermute | solution.py:216
  25.6 2.5 %collective-permute-start.1 = (bf16[320,512]{1,0:T(8,128)(2,1)}, bf16[320,512]{1,0:T(8,128)(2,1)S(1)}, u32[]{:S(2)}, u32[]{:S(2)}) collective-permute-start(bf16[320,512]{1,0:T(8,128)(2,1)} %get-tuple-element.37), channel_id=1, source_target_pairs={{0,8},{1,9},{2,10},{3,11},{4,12},{5,13},{6,14},{7,15},{8,0},{9,1},... | collective-permute-start | bytes 983048 | tf_op jit(solution)/shard_map/ppermute | solution.py:216
  28.0 3.4 %collective-permute-start.2 = (bf16[320,512]{1,0:T(8,128)(2,1)}, bf16[320,512]{1,0:T(8,128)(2,1)}, u32[]{:S(2)}, u32[]{:S(2)}) collective-permute-start(bf16[320,512]{1,0:T(8,128)(2,1)} %get-tuple-element.34), channel_id=1, source_target_pairs={{0,9},{1,8},{2,11},{3,10},{4,13},{5,12},{6,15},{7,14},{8,1},{9,0},... | collective-permute-start | bytes 983048 | tf_op jit(solution)/shard_map/ppermute | solution.py:216
  31.4 18.8 %all-to-all-done.tokens_ref = bf16[64,8,1024]{2,1,0:T(8,128)(2,1)S(1)} async-done(((bf16[64,8,1024]{2,1,0:T(8,128)(2,1)}), bf16[64,8,1024]{2,1,0:T(8,128)(2,1)S(1)}, u32[]{:S(2)}, u32[]{:S(2)}) %all-to-all-start) | async-done | bytes 1048608 | tf_op jit(solution)/shard_map/all_to_all | solution.py:210
  50.3 0.0 copy-done
  50.3 0.0 copy-done.5
  50.3 0.0 copy-start.1
  50.3 1.3 copy-done.1
  51.6 2.9 %shard_map.78 = bf16[256,768]{1,0:T(8,128)(2,1)} custom-call(bf16[64,8,1024]{2,1,0:T(8,128)(2,1)S(1)} %all-to-all-done.tokens_ref, f32[1,2048]{1,0:T(1,128)S(1)} %bitcast.25, bf16[320,2048]{1,0:T(8,128)(2,1)S(1)} %bitcast.22, bf16[320,2048]{1,0:T(8,128)(2,1)S(1)} %bitcast.23), custom_call_target="tpu_custom_call" | custom-call | flops 671088640 | bytes 5242880 | tf_op jit(solution)/shard_map/pallas_call | solution.py:219
  54.5 4.3 %all-to-all-start.1 = ((bf16[4,64,768]{2,1,0:T(8,128)(2,1)}), bf16[4,64,768]{2,1,0:T(8,128)(2,1)S(1)}, u32[]{:S(2)}, u32[]{:S(2)}) async-start(bf16[4,64,768]{2,1,0:T(8,128)(2,1)} %bitcast.6), calls=%async_computation.1 | async-start | bytes 786432 | tf_op jit(solution)/shard_map/all_to_all | solution.py:234
  58.8 0.2 collective-permute-done.down1
  58.9 0.0 collective-permute-done.1.down2
  58.9 0.0 copy-start.2
  58.9 0.0 collective-permute-done.2.down3
  58.9 7.2 %all-to-all-done.1.sums_ref = bf16[4,64,768]{2,1,0:T(8,128)(2,1)S(1)} async-done(((bf16[4,64,768]{2,1,0:T(8,128)(2,1)}), bf16[4,64,768]{2,1,0:T(8,128)(2,1)S(1)}, u32[]{:S(2)}, u32[]{:S(2)}) %all-to-all-start.1) | async-done | bytes 393248 | tf_op jit(solution)/shard_map/all_to_all | solution.py:234
  66.1 1.2 shard_map.79
  67.3 0.0 copy-done.2
  67.3 4.1 %all-to-all-start.2 = ((bf16[16,64,384]{2,1,0:T(8,128)(2,1)}), bf16[16,64,384]{2,1,0:T(8,128)(2,1)S(1)}, u32[]{:S(2)}, u32[]{:S(2)}) async-start(bf16[16,64,384]{2,1,0:T(8,128)(2,1)} %shard_map.79), calls=%async_computation.2 | async-start | bytes 1572864 | tf_op jit(solution)/shard_map/all_to_all | solution.py:245
  71.4 0.8 fusion.4
  72.2 0.3 fusion
  72.5 0.1 convert_element_type.31
  72.6 0.1 convert_element_type.30
  72.7 8.6 %all-to-all-done.2 = bf16[16,64,384]{2,1,0:T(8,128)(2,1)S(1)} async-done(((bf16[16,64,384]{2,1,0:T(8,128)(2,1)}), bf16[16,64,384]{2,1,0:T(8,128)(2,1)S(1)}, u32[]{:S(2)}, u32[]{:S(2)}) %all-to-all-start.2) | async-done | bytes 786464 | tf_op jit(solution)/shard_map/all_to_all | solution.py:245
  81.3 1.9 %collective-permute-start.3 = (bf16[4,256,384]{2,1,0:T(8,128)(2,1)S(1)}, bf16[4,256,384]{2,1,0:T(8,128)(2,1)S(1)}, u32[]{:S(2)}, u32[]{:S(2)}) collective-permute-start(bf16[4,256,384]{2,1,0:T(8,128)(2,1)S(1)} %bitcast.18), channel_id=1, source_target_pairs={{0,256},{256,0},{1,257},{257,1},{2,258},{258,2},{3,259},{259,3},{4... | collective-permute-start | bytes 2359304 | tf_op jit(solution)/shard_map/ppermute | solution.py:260
  83.2 2.3 %collective-permute-done.3.other_hbm.other_ref = bf16[4,256,384]{2,1,0:T(8,128)(2,1)S(1)} collective-permute-done((bf16[4,256,384]{2,1,0:T(8,128)(2,1)S(1)}, bf16[4,256,384]{2,1,0:T(8,128)(2,1)S(1)}, u32[]{:S(2)}, u32[]{:S(2)}) %collective-permute-start.3) | collective-permute-done | bytes 786464 | tf_op jit(solution)/shard_map/ppermute | solution.py:260
  85.5 0.0 copy-start.3
  85.5 1.0 copy-done.3
  86.4 3.2 %shard_map.80 = bf16[2,256,512]{2,1,0:T(8,128)(2,1)} custom-call(s32[1]{0:T(128)} %bitcast.slot_ref, bf16[4,256,384]{2,1,0:T(8,128)(2,1)S(1)} %bitcast.19, bf16[4,256,384]{2,1,0:T(8,128)(2,1)S(1)} %collective-permute-done.3.other_hbm.other_ref, bf16[4,1,320]{2,1,0:T(2,128)(2,1)S(1)} %pad_maximum_fusion.drop_ref, ...), custom_call_target="tpu_custom_call" | custom-call | flops 671088640 | bytes 1048576 | tf_op jit(solution)/shard_map/pallas_call | solution.py:265
  89.6 7.1 %all-to-all-start.3 = ((bf16[16,32,512]{2,1,0:T(8,128)(2,1)}), bf16[16,32,512]{2,1,0:T(8,128)(2,1)S(1)}, u32[]{:S(2)}, u32[]{:S(2)}) async-start(bf16[16,32,512]{2,1,0:T(8,128)(2,1)} %bitcast.10), calls=%async_computation.3 | async-start | bytes 1048576 | tf_op jit(solution)/shard_map/all_to_all | solution.py:290
  96.7 0.1 copy.18.names_ref
  96.9 0.6 shard_map.81.first_ref
  97.4 16.0 %all-to-all-done.3.shares_ref = bf16[16,32,512]{2,1,0:T(8,128)(2,1)S(1)} async-done(((bf16[16,32,512]{2,1,0:T(8,128)(2,1)}), bf16[16,32,512]{2,1,0:T(8,128)(2,1)S(1)}, u32[]{:S(2)}, u32[]{:S(2)}) %all-to-all-start.3) | async-done | bytes 524320 | tf_op jit(solution)/shard_map/all_to_all | solution.py:290
  113.4 0.9 shard_map.83
  114.3 7.9 %all-to-all-start.4 = ((bf16[16,32,512]{2,1,0:T(8,128)(2,1)}), bf16[16,32,512]{2,1,0:T(8,128)(2,1)S(1)}, u32[]{:S(2)}, u32[]{:S(2)}) async-start(bf16[16,32,512]{2,1,0:T(8,128)(2,1)} %shard_map.83), calls=%async_computation.4 | async-start | bytes 1048576 | tf_op jit(solution)/shard_map/all_to_all | solution.py:293
  122.2 0.1 copy.19.names_ref
  122.4 0.6 shard_map.82.second_ref
  122.9 15.7 %all-to-all-done.4 = bf16[16,32,512]{2,1,0:T(8,128)(2,1)S(1)} async-done(((bf16[16,32,512]{2,1,0:T(8,128)(2,1)}), bf16[16,32,512]{2,1,0:T(8,128)(2,1)S(1)}, u32[]{:S(2)}, u32[]{:S(2)}) %all-to-all-start.4) | async-done | bytes 524320 | tf_op jit(solution)/shard_map/all_to_all | solution.py:293
  138.6 1.3 shard_map.84
  140.0 9.6 %all-to-all-start.5 = ((bf16[4,160,512]{2,1,0:T(8,128)(2,1)}), bf16[4,160,512]{2,1,0:T(8,128)(2,1)S(1)}, u32[]{:S(2)}, u32[]{:S(2)}) async-start(bf16[4,160,512]{2,1,0:T(8,128)(2,1)} %get-tuple-element.28), calls=%async_computation.5 | async-start | bytes 1310720 | tf_op jit(solution)/shard_map/all_to_all | solution.py:309
  149.6 9.7 %psum.10 = f32[128]{0:T(128)S(1)} all-reduce(f32[128]{0:T(128)S(1)} %bitcast.26), channel_id=1, replica_groups=mesh['var'=2,'tok'=4,'wide'=64] {'tok'}, use_global_device_ids=true, to_apply=%region_2.3 | all-reduce | flops 128 | bytes 1024 | tf_op jit(solution)/shard_map/psum | solution.py:307
  159.3 0.0 all-to-all-done.5.in_ref
  159.3 0.6 broadcast_in_dim.26
  159.9 4.2 %all-to-all-start.6 = ((f32[4,8,128]{2,1,0:T(8,128)}), f32[4,8,128]{2,1,0:T(8,128)S(1)}, u32[]{:S(2)}, u32[]{:S(2)}) async-start(f32[4,8,128]{2,1,0:T(8,128)} %broadcast_in_dim.26), calls=%async_computation.6 | async-start | bytes 32768 | tf_op jit(solution)/shard_map/all_to_all | solution.py:311
  164.1 0.9 shard_map.85
  165.0 2.4 %all-to-all-done.6 = f32[4,8,128]{2,1,0:T(8,128)S(1)} async-done(((f32[4,8,128]{2,1,0:T(8,128)}), f32[4,8,128]{2,1,0:T(8,128)S(1)}, u32[]{:S(2)}, u32[]{:S(2)}) %all-to-all-start.6) | async-done | bytes 16416 | tf_op jit(solution)/shard_map/all_to_all | solution.py:311
  167.4 0.6 reduce_sum.9
  (4 shorter events, 0.0 us)
Async XLA Ops:
  0.7 0.8 copy-start.4
  3.1 47.1 %all-to-all-start = ((bf16[64,8,1024]{2,1,0:T(8,128)(2,1)}), bf16[64,8,1024]{2,1,0:T(8,128)(2,1)S(1)}, u32[]{:S(2)}, u32[]{:S(2)}) async-start(bf16[64,8,1024]{2,1,0:T(8,128)(2,1)} %shard_map.77), calls=%async_computation | async-start | bytes 2097152 | tf_op jit(solution)/shard_map/all_to_all | solution.py:210
  19.8 30.5 %copy-start = (bf16[2048,320]{0,1:T(8,128)(2,1)S(1)}, bf16[2048,320]{0,1:T(8,128)(2,1)}, u32[]{:S(2)}) copy-start(bf16[2048,320]{0,1:T(8,128)(2,1)} %param.8) | copy-start | bytes 3932164
  19.8 30.4 %copy-start.5 = (f32[2048]{0:T(1024)S(1)}, f32[2048]{0:T(1024)}, u32[]{:S(2)}) copy-start(f32[2048]{0:T(1024)} %param.7) | copy-start | bytes 24580
  22.2 36.7 %collective-permute-start = (bf16[320,512]{1,0:T(8,128)(2,1)}, bf16[320,512]{1,0:T(8,128)(2,1)S(1)}, u32[]{:S(2)}, u32[]{:S(2)}) collective-permute-start(bf16[320,512]{1,0:T(8,128)(2,1)} %get-tuple-element.35), channel_id=1, source_target_pairs={{0,1},{1,0},{2,3},{3,2},{4,5},{5,4},{6,7},{7,6},{8,9},{9,8},{10,11... | collective-permute-start | bytes 983048 | tf_op jit(solution)/shard_map/ppermute | solution.py:216
  25.6 33.4 %collective-permute-start.1 = (bf16[320,512]{1,0:T(8,128)(2,1)}, bf16[320,512]{1,0:T(8,128)(2,1)S(1)}, u32[]{:S(2)}, u32[]{:S(2)}) collective-permute-start(bf16[320,512]{1,0:T(8,128)(2,1)} %get-tuple-element.37), channel_id=1, source_target_pairs={{0,8},{1,9},{2,10},{3,11},{4,12},{5,13},{6,14},{7,15},{8,0},{9,1},... | collective-permute-start | bytes 983048 | tf_op jit(solution)/shard_map/ppermute | solution.py:216
  28.0 30.9 %collective-permute-start.2 = (bf16[320,512]{1,0:T(8,128)(2,1)}, bf16[320,512]{1,0:T(8,128)(2,1)}, u32[]{:S(2)}, u32[]{:S(2)}) collective-permute-start(bf16[320,512]{1,0:T(8,128)(2,1)} %get-tuple-element.34), channel_id=1, source_target_pairs={{0,9},{1,8},{2,11},{3,10},{4,13},{5,12},{6,15},{7,14},{8,1},{9,0},... | collective-permute-start | bytes 983048 | tf_op jit(solution)/shard_map/ppermute | solution.py:216
  50.3 1.3 copy-start.1
  54.5 11.7 %all-to-all-start.1 = ((bf16[4,64,768]{2,1,0:T(8,128)(2,1)}), bf16[4,64,768]{2,1,0:T(8,128)(2,1)S(1)}, u32[]{:S(2)}, u32[]{:S(2)}) async-start(bf16[4,64,768]{2,1,0:T(8,128)(2,1)} %bitcast.6), calls=%async_computation.1 | async-start | bytes 786432 | tf_op jit(solution)/shard_map/all_to_all | solution.py:234
  58.9 8.4 %copy-start.2 = (bf16[320,512]{1,0:T(8,128)(2,1)}, bf16[320,512]{1,0:T(8,128)(2,1)S(1)}, u32[]{:S(2)}) copy-start(bf16[320,512]{1,0:T(8,128)(2,1)S(1)} %collective-permute-done.1.down2) | copy-start | bytes 983044
  67.3 14.0 %all-to-all-start.2 = ((bf16[16,64,384]{2,1,0:T(8,128)(2,1)}), bf16[16,64,384]{2,1,0:T(8,128)(2,1)S(1)}, u32[]{:S(2)}, u32[]{:S(2)}) async-start(bf16[16,64,384]{2,1,0:T(8,128)(2,1)} %shard_map.79), calls=%async_computation.2 | async-start | bytes 1572864 | tf_op jit(solution)/shard_map/all_to_all | solution.py:245
  81.3 4.2 %collective-permute-start.3 = (bf16[4,256,384]{2,1,0:T(8,128)(2,1)S(1)}, bf16[4,256,384]{2,1,0:T(8,128)(2,1)S(1)}, u32[]{:S(2)}, u32[]{:S(2)}) collective-permute-start(bf16[4,256,384]{2,1,0:T(8,128)(2,1)S(1)} %bitcast.18), channel_id=1, source_target_pairs={{0,256},{256,0},{1,257},{257,1},{2,258},{258,2},{3,259},{259,3},{4... | collective-permute-start | bytes 2359304 | tf_op jit(solution)/shard_map/ppermute | solution.py:260
  85.5 1.0 copy-start.3
  89.6 23.8 %all-to-all-start.3 = ((bf16[16,32,512]{2,1,0:T(8,128)(2,1)}), bf16[16,32,512]{2,1,0:T(8,128)(2,1)S(1)}, u32[]{:S(2)}, u32[]{:S(2)}) async-start(bf16[16,32,512]{2,1,0:T(8,128)(2,1)} %bitcast.10), calls=%async_computation.3 | async-start | bytes 1048576 | tf_op jit(solution)/shard_map/all_to_all | solution.py:290
  114.3 24.3 %all-to-all-start.4 = ((bf16[16,32,512]{2,1,0:T(8,128)(2,1)}), bf16[16,32,512]{2,1,0:T(8,128)(2,1)S(1)}, u32[]{:S(2)}, u32[]{:S(2)}) async-start(bf16[16,32,512]{2,1,0:T(8,128)(2,1)} %shard_map.83), calls=%async_computation.4 | async-start | bytes 1048576 | tf_op jit(solution)/shard_map/all_to_all | solution.py:293
  140.0 19.3 %all-to-all-start.5 = ((bf16[4,160,512]{2,1,0:T(8,128)(2,1)}), bf16[4,160,512]{2,1,0:T(8,128)(2,1)S(1)}, u32[]{:S(2)}, u32[]{:S(2)}) async-start(bf16[4,160,512]{2,1,0:T(8,128)(2,1)} %get-tuple-element.28), calls=%async_computation.5 | async-start | bytes 1310720 | tf_op jit(solution)/shard_map/all_to_all | solution.py:309
  159.9 7.5 %all-to-all-start.6 = ((f32[4,8,128]{2,1,0:T(8,128)}), f32[4,8,128]{2,1,0:T(8,128)S(1)}, u32[]{:S(2)}, u32[]{:S(2)}) async-start(f32[4,8,128]{2,1,0:T(8,128)} %broadcast_in_dim.26), calls=%async_computation.6 | async-start | bytes 32768 | tf_op jit(solution)/shard_map/all_to_all | solution.py:311

commit v8 on v6

--- a/solution.py
+++ b/solution.py
@@ -60,9 +60,9 @@
         out_ref[i] = piece
 
 
-def parent_kernel(tokens_ref, gain_ref, gate_ref, up_ref, out_ref, rows_ref):
+def parent_kernel(tokens_ref, gain_ref, weights_ref, out_ref, rows_ref):
     n_shards, _, width = tokens_ref.shape
-    local = gate_ref.shape[0]
+    local = weights_ref.shape[0] // 2
     lanes = out_ref.shape[1] // 2
     step = 16
     squares = []
@@ -81,8 +81,8 @@
     squares = jnp.concatenate(squares, axis=0)
     hi = squares.astype(jnp.bfloat16).astype(jnp.float32)
     contract = (((1,), (1,)), ((), ()))
-    gate = lax.dot_general(rows_ref[...], gate_ref[...], contract, preferred_element_type=jnp.float32)
-    up = lax.dot_general(rows_ref[...], up_ref[...], contract, preferred_element_type=jnp.float32)
+    gate = lax.dot_general(rows_ref[...], weights_ref[:local], contract, preferred_element_type=jnp.float32)
+    up = lax.dot_general(rows_ref[...], weights_ref[local:], contract, preferred_element_type=jnp.float32)
     lane = lax.broadcasted_iota(jnp.int32, (squares.shape[0], lanes - local), 1)
     extra = jnp.where(lane == 0, hi, jnp.where(lane == 1, squares - hi, 0.0))
     out_ref[:, :local] = gate.astype(out_ref.dtype)
@@ -149,38 +149,33 @@
         out_ref[i] = piece
 
 
-def gradient_kernel(factor, chosen_ref, rounded_ref, out_ref):
+def gradient_kernel(factor, slot_ref, chosen_ref, rounded_ref, out0, out1, out2, out3, error_ref, rows_ref):
+    slot = slot_ref[0]
     rounded = rounded_ref[...]
-    block = chosen_ref.shape[1] // 2
+    block = out0.shape[0]
     for pair in range(2):
         product = jnp.dot(chosen_ref[pair], rounded, preferred_element_type=jnp.float32) * factor
         for i in range(2):
-            out_ref[2 * pair + i, :block] = product[i * block : (i + 1) * block].astype(out_ref.dtype)
+            rows_ref[2 * pair + i] = product[i * block : (i + 1) * block].astype(rows_ref.dtype)
+    for k, out_ref in enumerate((out0, out1, out2, out3)):
+        out_ref[...] = rows_ref[slot ^ k]
     errors = rounded.astype(jnp.float32)
     columns = jnp.sum(errors * errors, axis=0, keepdims=True)
-    hi = columns.astype(out_ref.dtype).astype(jnp.float32)
-    line = lax.broadcasted_iota(jnp.int32, (16, columns.shape[1]), 0)
-    extra = jnp.where(line == 0, hi, jnp.where(line == 1, columns - hi, 0.0)).astype(out_ref.dtype)
-    for i in range(4):
-        out_ref[i, block:] = extra
-
-
-def interleave_kernel(in_ref, out_ref, error_ref):
-    block = out_ref.shape[0]
-    width = in_ref.shape[2]
-    total = None
-    for i in range(in_ref.shape[0]):
-        out_ref[:, i * width : (i + 1) * width] = in_ref[i, :block]
-        term = in_ref[i, block:].astype(jnp.float32)
-        total = term if total is None else total + term
-    columns = jnp.sum(total, axis=0, keepdims=True)
     lanes = columns[:, :128]
-    for i in range(1, width // 128):
+    for i in range(1, columns.shape[1] // 128):
         lanes = lanes + columns[:, i * 128 : (i + 1) * 128]
     line = lax.broadcasted_iota(jnp.int32, (8, 128), 0)
     lanes = jnp.where(line == 0, lanes, 0.0)
     for i in range(error_ref.shape[0]):
         error_ref[i] = lanes
+
+
+def interleave_kernel(slot_ref, in0, in1, in2, in3, out_ref):
+    slot = slot_ref[0]
+    width = in0.shape[1]
+    for k, in_ref in enumerate((in0, in1, in2, in3)):
+        start = pl.multiple_of((slot ^ k) * width, 128)
+        out_ref[:, pl.ds(start, width)] = in_ref[...]
 
 
 def per_device(tokens, norm_gain, gate_parent, up_parent, down_parent, kept):
@@ -210,15 +205,17 @@
         perm = [(w, w ^ ((k // 2) * SIDE + k % 2)) for w in range(n_wide)]
         downs[k] = lax.ppermute(downs[k], "wide", perm)
 
+    weights = jnp.concatenate([gate_parent.T, up_parent.T], axis=0)
+    gathered, weights = lax.optimization_barrier((gathered, weights))
     pad = (-local) % 128
     partial = call(
         parent_kernel,
         jax.ShapeDtypeStruct((n_wide * half, 2 * (local + pad)), jnp.bfloat16),
-        [VMEM] * 4,
+        [VMEM] * 3,
         4 * n_wide * half * width * local,
         8 * width * local,
         [pltpu.VMEM((n_wide * half, width), jnp.bfloat16)],
-    )(gathered, norm_gain.reshape(1, width), gate_parent.T, up_parent.T)
+    )(gathered, norm_gain.reshape(1, width), weights)
     rows = n_wide * half // n_tok
 
     scattered = lax.all_to_all(partial.reshape(n_tok, rows, 2 * (local + pad)), "tok", 0, 0)
@@ -273,25 +270,29 @@
         4 * total_rows * local,
     )(names, hidden, other)
     factor = 1.0 / math.sqrt(total_rows)
-    grad = call(
+    *grads, errors = call(
         functools.partial(gradient_kernel, factor),
-        jax.ShapeDtypeStruct((4, block + 16, quarter), jnp.bfloat16),
-        [VMEM] * 2,
+        (
+            *[jax.ShapeDtypeStruct((block, quarter), jnp.bfloat16)] * 4,
+            jax.ShapeDtypeStruct((4 * n_tok, 8, 128), jnp.float32),
+        ),
+        [SMEM, VMEM, VMEM],
         2 * total_rows * 4 * block * quarter,
         4 * total_rows * quarter,
-    )(chosen, rounded)
-    swapped = lax.all_to_all(grad, "wide", 0, 0, axis_index_groups=blocks)
-    grad, errors = call(
+        [pltpu.VMEM((4, block, quarter), jnp.bfloat16)],
+    )(slot.reshape(1), chosen, rounded)
+    errors = lax.all_to_all(errors, ("tok", "wide"), 0, 0, axis_index_groups=groups)
+    loss = jnp.sum(errors) / (total_rows * D)
+    for k in range(1, 4):
+        perm = [(w, w ^ ((k // 2) * SIDE + k % 2)) for w in range(n_wide)]
+        grads[k] = lax.ppermute(grads[k], "wide", perm)
+    grad = call(
         interleave_kernel,
-        (
-            jax.ShapeDtypeStruct((block, 4 * quarter), jnp.bfloat16),
-            jax.ShapeDtypeStruct((n_tok, 8, 128), jnp.float32),
-        ),
-        [VMEM],
+        jax.ShapeDtypeStruct((block, 4 * quarter), jnp.bfloat16),
+        [SMEM] + [VMEM] * 4,
         0,
         4 * block * quarter,
-    )(swapped)
-    loss = jnp.sum(lax.all_to_all(errors, "tok", 0, 0)) / (total_rows * D)
+    )(slot.reshape(1), *grads)
     return (loss.reshape(1), grad[None])
 
 

time: 168 us -> 166 us (0.988)
  the two profiles are of different devices: /device:TPU:8 before, /device:TPU:2 now
where the time goes in v8:
time: 166 us; the launch traced here: 165 us
  waiting for transfers between devices  54.3 us (33%)
  starting transfers between devices  52.2 us (31%)
  blocking collectives  38.4 us (23%)
  Pallas kernels  11.7 us (7%)
  other arithmetic  3.71 us (2%)
  between operations  2.69 us (2%)
  local copies, waits for them, and re-layouts  2.13 us (1%)
    all_to_all x1, blocking collectives, per_device(): shares = lax.all_to_all(shares, 'wide', 0, 0, axis_index_groups=strides)  29.3 us
    all_to_all x1, waiting for transfers between devices, per_device(): lax.all_to_all(pieces, 'wide', 0, 0, axis_index_groups=strides)  20.4 us
    all_to_all x1, waiting for transfers between devices, per_device(): gathered = lax.all_to_all(pieces, 'wide', 0, 0)  17.1 us
    all_to_all x1, starting transfers between devices, per_device(): gathered = lax.all_to_all(pieces, 'wide', 0, 0)  16.9 us
    all_to_all x1, waiting for transfers between devices, per_device(): lax.all_to_all(hidden, ('tok', 'wide'), 0, 0, axis_index_groups=groups)  9.87 us
    ppermute x3, starting transfers between devices, per_device(): grads[k] = lax.ppermute(grads[k], 'wide', perm)  9.21 us
    ppermute x3, starting transfers between devices, per_device(): downs[k] = lax.ppermute(downs[k], 'wide', perm)  9.2 us
    all_to_all x1, blocking collectives, per_device(): lax.all_to_all(errors, ('tok', 'wide'), 0, 0, axis_index_groups=groups)  9.07 us
  transfers between devices with their start and end apart: 11, of which 6 were waited for; matrix products, arithmetic and copies ran while one was open for 3% of the time, Pallas kernels for 3%

profile of v8, /device:TPU:2, one launch (start us, length us, event | category | flops | bytes accessed | tf_op | source)
XLA Modules:
  0.0 165.2 jit_solution(14559582900441167185)
XLA Ops:
  0.6 0.1 pad_add_fusion.place_ref
  0.7 0.0 copy-start
  0.7 0.8 copy-done
  1.5 0.0 copy-start.2
  1.5 1.7 %shard_map.77 = bf16[64,8,1024]{2,1,0:T(8,128)(2,1)} custom-call(s32[2]{0:T(128)S(1)} %pad_add_fusion.place_ref, bf16[8,2048]{1,0:T(8,128)(2,1)S(1)} %copy-done), custom_call_target="tpu_custom_call" | custom-call | bytes 1048576 | tf_op jit(solution)/shard_map/pallas_call | solution.py:193
  3.2 16.9 %all-to-all-start = ((bf16[64,8,1024]{2,1,0:T(8,128)(2,1)}), bf16[64,8,1024]{2,1,0:T(8,128)(2,1)}, u32[]{:S(2)}, u32[]{:S(2)}) async-start(bf16[64,8,1024]{2,1,0:T(8,128)(2,1)} %shard_map.77), calls=%async_computation | async-start | bytes 2097152 | tf_op jit(solution)/shard_map/all_to_all | solution.py:200
  20.1 0.0 copy-done.2
  20.1 1.0 constant_dynamic-slice_fusion
  21.2 3.4 %collective-permute-start = (bf16[320,512]{1,0:T(8,128)(2,1)}, bf16[320,512]{1,0:T(8,128)(2,1)S(1)}, u32[]{:S(2)}, u32[]{:S(2)}) collective-permute-start(bf16[320,512]{1,0:T(8,128)(2,1)} %get-tuple-element.31), channel_id=1, source_target_pairs={{0,1},{1,0},{2,3},{3,2},{4,5},{5,4},{6,7},{7,6},{8,9},{9,8},{10,11... | collective-permute-start | bytes 983048 | tf_op jit(solution)/shard_map/ppermute | solution.py:206
  24.6 3.4 %collective-permute-start.1 = (bf16[320,512]{1,0:T(8,128)(2,1)}, bf16[320,512]{1,0:T(8,128)(2,1)}, u32[]{:S(2)}, u32[]{:S(2)}) collective-permute-start(bf16[320,512]{1,0:T(8,128)(2,1)} %get-tuple-element.33), channel_id=1, source_target_pairs={{0,8},{1,9},{2,10},{3,11},{4,12},{5,13},{6,14},{7,15},{8,0},{9,1},... | collective-permute-start | bytes 983048 | tf_op jit(solution)/shard_map/ppermute | solution.py:206
  27.9 2.4 %collective-permute-start.2 = (bf16[320,512]{1,0:T(8,128)(2,1)}, bf16[320,512]{1,0:T(8,128)(2,1)}, u32[]{:S(2)}, u32[]{:S(2)}) collective-permute-start(bf16[320,512]{1,0:T(8,128)(2,1)} %get-tuple-element.30), channel_id=1, source_target_pairs={{0,9},{1,8},{2,11},{3,10},{4,13},{5,12},{6,15},{7,14},{8,1},{9,0},... | collective-permute-start | bytes 983048 | tf_op jit(solution)/shard_map/ppermute | solution.py:206
  30.4 0.0 copy-start.1
  30.4 1.9 %pad_maximum_fusion.weights_ref = bf16[640,2048]{1,0:T(8,128)(2,1)S(1)} fusion(bf16[320,2048]{1,0:T(8,128)(2,1)} %bitcast.20, bf16[320,2048]{1,0:T(8,128)(2,1)} %bitcast.21), kind=kLoop, calls=%fused_computation | loop fusion | flops 5242880 | bytes 5242880 | tf_op jit(solution)/shard_map/concatenate | solution.py:208
  32.3 17.1 %all-to-all-done.tokens_ref = bf16[64,8,1024]{2,1,0:T(8,128)(2,1)} async-done(((bf16[64,8,1024]{2,1,0:T(8,128)(2,1)}), bf16[64,8,1024]{2,1,0:T(8,128)(2,1)}, u32[]{:S(2)}, u32[]{:S(2)}) %all-to-all-start) | async-done | bytes 1048608 | tf_op jit(solution)/shard_map/all_to_all | solution.py:200
  49.4 0.0 copy-done.1
  49.4 3.3 %shard_map.78 = bf16[256,768]{1,0:T(8,128)(2,1)} custom-call(bf16[64,8,1024]{2,1,0:T(8,128)(2,1)} %all-to-all-done.tokens_ref, f32[1,2048]{1,0:T(1,128)S(1)} %bitcast.19, bf16[640,2048]{1,0:T(8,128)(2,1)S(1)} %pad_maximum_fusion.weights_ref), custom_call_target="tpu_custom_call" | custom-call | flops 671088640 | bytes 5242880 | tf_op jit(solution)/shard_map/pallas_call | solution.py:211
  52.7 4.8 %all-to-all-start.1 = ((bf16[4,64,768]{2,1,0:T(8,128)(2,1)}), bf16[4,64,768]{2,1,0:T(8,128)(2,1)S(1)}, u32[]{:S(2)}, u32[]{:S(2)}) async-start(bf16[4,64,768]{2,1,0:T(8,128)(2,1)} %bitcast.7), calls=%async_computation.1 | async-start | bytes 786432 | tf_op jit(solution)/shard_map/all_to_all | solution.py:221
  57.6 0.0 collective-permute-done.down1
  57.6 0.0 collective-permute-done.1.down2
  57.6 1.3 collective-permute-done.2.down3
  58.9 4.6 %all-to-all-done.1.sums_ref = bf16[4,64,768]{2,1,0:T(8,128)(2,1)S(1)} async-done(((bf16[4,64,768]{2,1,0:T(8,128)(2,1)}), bf16[4,64,768]{2,1,0:T(8,128)(2,1)S(1)}, u32[]{:S(2)}, u32[]{:S(2)}) %all-to-all-start.1) | async-done | bytes 393248 | tf_op jit(solution)/shard_map/all_to_all | solution.py:221
  63.5 1.2 shard_map.79
  64.7 6.1 %all-to-all-start.2 = ((bf16[16,64,384]{2,1,0:T(8,128)(2,1)}), bf16[16,64,384]{2,1,0:T(8,128)(2,1)S(1)}, u32[]{:S(2)}, u32[]{:S(2)}) async-start(bf16[16,64,384]{2,1,0:T(8,128)(2,1)} %shard_map.79), calls=%async_computation.2 | async-start | bytes 1572864 | tf_op jit(solution)/shard_map/all_to_all | solution.py:232
  70.8 9.9 %all-to-all-done.2 = bf16[16,64,384]{2,1,0:T(8,128)(2,1)S(1)} async-done(((bf16[16,64,384]{2,1,0:T(8,128)(2,1)}), bf16[16,64,384]{2,1,0:T(8,128)(2,1)S(1)}, u32[]{:S(2)}, u32[]{:S(2)}) %all-to-all-start.2) | async-done | bytes 786464 | tf_op jit(solution)/shard_map/all_to_all | solution.py:232
  80.6 1.9 %collective-permute-start.3 = (bf16[4,256,384]{2,1,0:T(8,128)(2,1)S(1)}, bf16[4,256,384]{2,1,0:T(8,128)(2,1)S(1)}, u32[]{:S(2)}, u32[]{:S(2)}) collective-permute-start(bf16[4,256,384]{2,1,0:T(8,128)(2,1)S(1)} %bitcast.14), channel_id=1, source_target_pairs={{0,256},{256,0},{1,257},{257,1},{2,258},{258,2},{3,259},{259,3},{4... | collective-permute-start | bytes 2359304 | tf_op jit(solution)/shard_map/ppermute | solution.py:234
  82.5 0.8 fusion.2
  83.3 0.3 fusion
  83.7 0.1 convert_element_type.30
  83.7 0.1 convert_element_type.31
  83.9 0.9 collective-permute-done.3.other_ref
  84.8 2.3 %shard_map.81 = bf16[2,256,512]{2,1,0:T(8,128)(2,1)S(1)} custom-call(s32[1]{0:T(128)} %bitcast.slot_ref, bf16[4,256,384]{2,1,0:T(8,128)(2,1)S(1)} %bitcast.15, bf16[4,256,384]{2,1,0:T(8,128)(2,1)S(1)} %collective-permute-done.3.other_ref, bf16[4,1,320]{2,1,0:T(2,128)(2,1)S(1)} %pad_maximum_fusion.1.drop_ref, bf16[320,512]{1,0:T(8,128)(2,1)S(1)} %get-tuple-element.17.down0, ...), custom_call_target="tpu_custom_call" | custom-call | flops 671088640 | bytes 1048576 | tf_op jit(solution)/shard_map/pallas_call | solution.py:252
  87.1 29.3 %all_to_all.30.shares_ref = bf16[16,32,512]{2,1,0:T(8,128)(2,1)S(1)} all-to-all(bf16[16,32,512]{2,1,0:T(8,128)(2,1)S(1)} %bitcast.17), channel_id=1, replica_groups={{0,2,4,6,16,18,20,22,32,34,36,38,48,50,52,54},{1,3,5,7,17,19,21,23,33,3..., dimensions={0} | all-to-all | bytes 1048576 | tf_op jit(solution)/shard_map/all_to_all | solution.py:261
  116.5 0.9 shard_map.82
  117.3 4.1 %all-to-all-start.4 = ((bf16[16,32,512]{2,1,0:T(8,128)(2,1)}), bf16[16,32,512]{2,1,0:T(8,128)(2,1)S(1)}, u32[]{:S(2)}, u32[]{:S(2)}) async-start(bf16[16,32,512]{2,1,0:T(8,128)(2,1)} %shard_map.82), calls=%async_computation.4 | async-start | bytes 1048576 | tf_op jit(solution)/shard_map/all_to_all | solution.py:263
  121.5 0.2 copy.11.names_ref
  121.6 0.9 shard_map.80.chosen_ref
  122.6 20.4 %all-to-all-done.4 = bf16[16,32,512]{2,1,0:T(8,128)(2,1)S(1)} async-done(((bf16[16,32,512]{2,1,0:T(8,128)(2,1)}), bf16[16,32,512]{2,1,0:T(8,128)(2,1)S(1)}, u32[]{:S(2)}, u32[]{:S(2)}) %all-to-all-start.4) | async-done | bytes 524320 | tf_op jit(solution)/shard_map/all_to_all | solution.py:263
  143.0 0.5 shard_map.83
  143.6 1.9 %collective-permute-start.4 = (bf16[160,512]{1,0:T(8,128)(2,1)S(1)}, bf16[160,512]{1,0:T(8,128)(2,1)S(1)}, u32[]{:S(2)}, u32[]{:S(2)}) collective-permute-start(bf16[160,512]{1,0:T(8,128)(2,1)S(1)} %get-tuple-element.23), channel_id=1, source_target_pairs={{0,1},{1,0},{2,3},{3,2},{4,5},{5,4},{6,7},{7,6},{8,9},{9,8},{10,11... | collective-permute-start | bytes 491528 | tf_op jit(solution)/shard_map/ppermute | solution.py:288
  145.5 1.9 %collective-permute-start.5 = (bf16[160,512]{1,0:T(8,128)(2,1)S(1)}, bf16[160,512]{1,0:T(8,128)(2,1)S(1)}, u32[]{:S(2)}, u32[]{:S(2)}) collective-permute-start(bf16[160,512]{1,0:T(8,128)(2,1)S(1)} %get-tuple-element.24), channel_id=1, source_target_pairs={{0,8},{1,9},{2,10},{3,11},{4,12},{5,13},{6,14},{7,15},{8,0},{9,1},... | collective-permute-start | bytes 491528 | tf_op jit(solution)/shard_map/ppermute | solution.py:288
  147.4 5.4 %collective-permute-start.6 = (bf16[160,512]{1,0:T(8,128)(2,1)S(1)}, bf16[160,512]{1,0:T(8,128)(2,1)S(1)}, u32[]{:S(2)}, u32[]{:S(2)}) collective-permute-start(bf16[160,512]{1,0:T(8,128)(2,1)S(1)} %get-tuple-element.25), channel_id=1, source_target_pairs={{0,9},{1,8},{2,11},{3,10},{4,13},{5,12},{6,15},{7,14},{8,1},{9,0},... | collective-permute-start | bytes 491528 | tf_op jit(solution)/shard_map/ppermute | solution.py:288
  152.8 9.1 %all_to_all.31 = f32[16,8,128]{2,1,0:T(8,128)S(1)} all-to-all(f32[16,8,128]{2,1,0:T(8,128)S(1)} %get-tuple-element.21), channel_id=1, replica_groups={{0,64,128,192,1,65,129,193,8,72,136,200,9,73,137,201},{2,66,130,194,3,6..., dimensions={0} | all-to-all | bytes 131072 | tf_op jit(solution)/shard_map/all_to_all | solution.py:284
  161.9 0.6 reduce_sum.9
  163.1 0.0 collective-permute-done.4.in1
  163.2 0.0 collective-permute-done.5.in2
  163.2 0.0 collective-permute-done.6.in3
  163.2 0.9 shard_map.84
  (4 shorter events, 0.0 us)
Async XLA Ops:
  0.7 0.8 copy-start
  1.5 18.7 %copy-start.2 = (bf16[320,2048]{1,0:T(8,128)(2,1)S(1)}, bf16[320,2048]{1,0:T(8,128)(2,1)}, u32[]{:S(2)}) copy-start(bf16[320,2048]{1,0:T(8,128)(2,1)} %param.10) | copy-start | bytes 3932164
  3.2 46.3 %all-to-all-start = ((bf16[64,8,1024]{2,1,0:T(8,128)(2,1)}), bf16[64,8,1024]{2,1,0:T(8,128)(2,1)}, u32[]{:S(2)}, u32[]{:S(2)}) async-start(bf16[64,8,1024]{2,1,0:T(8,128)(2,1)} %shard_map.77), calls=%async_computation | async-start | bytes 2097152 | tf_op jit(solution)/shard_map/all_to_all | solution.py:200
  21.2 36.4 %collective-permute-start = (bf16[320,512]{1,0:T(8,128)(2,1)}, bf16[320,512]{1,0:T(8,128)(2,1)S(1)}, u32[]{:S(2)}, u32[]{:S(2)}) collective-permute-start(bf16[320,512]{1,0:T(8,128)(2,1)} %get-tuple-element.31), channel_id=1, source_target_pairs={{0,1},{1,0},{2,3},{3,2},{4,5},{5,4},{6,7},{7,6},{8,9},{9,8},{10,11... | collective-permute-start | bytes 983048 | tf_op jit(solution)/shard_map/ppermute | solution.py:206
  24.6 33.0 %collective-permute-start.1 = (bf16[320,512]{1,0:T(8,128)(2,1)}, bf16[320,512]{1,0:T(8,128)(2,1)}, u32[]{:S(2)}, u32[]{:S(2)}) collective-permute-start(bf16[320,512]{1,0:T(8,128)(2,1)} %get-tuple-element.33), channel_id=1, source_target_pairs={{0,8},{1,9},{2,10},{3,11},{4,12},{5,13},{6,14},{7,15},{8,0},{9,1},... | collective-permute-start | bytes 983048 | tf_op jit(solution)/shard_map/ppermute | solution.py:206
  27.9 31.0 %collective-permute-start.2 = (bf16[320,512]{1,0:T(8,128)(2,1)}, bf16[320,512]{1,0:T(8,128)(2,1)}, u32[]{:S(2)}, u32[]{:S(2)}) collective-permute-start(bf16[320,512]{1,0:T(8,128)(2,1)} %get-tuple-element.30), channel_id=1, source_target_pairs={{0,9},{1,8},{2,11},{3,10},{4,13},{5,12},{6,15},{7,14},{8,1},{9,0},... | collective-permute-start | bytes 983048 | tf_op jit(solution)/shard_map/ppermute | solution.py:206
  30.4 19.1 %copy-start.1 = (f32[2048]{0:T(1024)S(1)}, f32[2048]{0:T(1024)}, u32[]{:S(2)}) copy-start(f32[2048]{0:T(1024)} %param.7) | copy-start | bytes 24580
  52.7 10.8 %all-to-all-start.1 = ((bf16[4,64,768]{2,1,0:T(8,128)(2,1)}), bf16[4,64,768]{2,1,0:T(8,128)(2,1)S(1)}, u32[]{:S(2)}, u32[]{:S(2)}) async-start(bf16[4,64,768]{2,1,0:T(8,128)(2,1)} %bitcast.7), calls=%async_computation.1 | async-start | bytes 786432 | tf_op jit(solution)/shard_map/all_to_all | solution.py:221
  64.7 16.0 %all-to-all-start.2 = ((bf16[16,64,384]{2,1,0:T(8,128)(2,1)}), bf16[16,64,384]{2,1,0:T(8,128)(2,1)S(1)}, u32[]{:S(2)}, u32[]{:S(2)}) async-start(bf16[16,64,384]{2,1,0:T(8,128)(2,1)} %shard_map.79), calls=%async_computation.2 | async-start | bytes 1572864 | tf_op jit(solution)/shard_map/all_to_all | solution.py:232
  80.6 4.2 %collective-permute-start.3 = (bf16[4,256,384]{2,1,0:T(8,128)(2,1)S(1)}, bf16[4,256,384]{2,1,0:T(8,128)(2,1)S(1)}, u32[]{:S(2)}, u32[]{:S(2)}) collective-permute-start(bf16[4,256,384]{2,1,0:T(8,128)(2,1)S(1)} %bitcast.14), channel_id=1, source_target_pairs={{0,256},{256,0},{1,257},{257,1},{2,258},{258,2},{3,259},{259,3},{4... | collective-permute-start | bytes 2359304 | tf_op jit(solution)/shard_map/ppermute | solution.py:234
  117.3 25.7 %all-to-all-start.4 = ((bf16[16,32,512]{2,1,0:T(8,128)(2,1)}), bf16[16,32,512]{2,1,0:T(8,128)(2,1)S(1)}, u32[]{:S(2)}, u32[]{:S(2)}) async-start(bf16[16,32,512]{2,1,0:T(8,128)(2,1)} %shard_map.82), calls=%async_computation.4 | async-start | bytes 1048576 | tf_op jit(solution)/shard_map/all_to_all | solution.py:263
  143.6 19.6 %collective-permute-start.4 = (bf16[160,512]{1,0:T(8,128)(2,1)S(1)}, bf16[160,512]{1,0:T(8,128)(2,1)S(1)}, u32[]{:S(2)}, u32[]{:S(2)}) collective-permute-start(bf16[160,512]{1,0:T(8,128)(2,1)S(1)} %get-tuple-element.23), channel_id=1, source_target_pairs={{0,1},{1,0},{2,3},{3,2},{4,5},{5,4},{6,7},{7,6},{8,9},{9,8},{10,11... | collective-permute-start | bytes 491528 | tf_op jit(solution)/shard_map/ppermute | solution.py:288
  145.5 17.7 %collective-permute-start.5 = (bf16[160,512]{1,0:T(8,128)(2,1)S(1)}, bf16[160,512]{1,0:T(8,128)(2,1)S(1)}, u32[]{:S(2)}, u32[]{:S(2)}) collective-permute-start(bf16[160,512]{1,0:T(8,128)(2,1)S(1)} %get-tuple-element.24), channel_id=1, source_target_pairs={{0,8},{1,9},{2,10},{3,11},{4,12},{5,13},{6,14},{7,15},{8,0},{9,1},... | collective-permute-start | bytes 491528 | tf_op jit(solution)/shard_map/ppermute | solution.py:288
  147.4 15.7 %collective-permute-start.6 = (bf16[160,512]{1,0:T(8,128)(2,1)S(1)}, bf16[160,512]{1,0:T(8,128)(2,1)S(1)}, u32[]{:S(2)}, u32[]{:S(2)}) collective-permute-start(bf16[160,512]{1,0:T(8,128)(2,1)S(1)} %get-tuple-element.25), channel_id=1, source_target_pairs={{0,9},{1,8},{2,11},{3,10},{4,13},{5,12},{6,15},{7,14},{8,1},{9,0},... | collective-permute-start | bytes 491528 | tf_op jit(solution)/shard_map/ppermute | solution.py:288

commit v9 on v8

--- a/solution.py
+++ b/solution.py
@@ -30,10 +30,12 @@
 
 VMEM = pl.BlockSpec(memory_space=pltpu.VMEM)
 SMEM = pl.BlockSpec(memory_space=pltpu.SMEM)
-
-
-def call(kernel, out_shape, in_specs, flops, size, scratch=()):
-    out_specs = jax.tree.map(lambda _: VMEM, out_shape)
+ANY = pl.BlockSpec(memory_space=pl.ANY)
+COPIES = 8
+
+
+def call(kernel, out_shape, in_specs, flops, size, scratch=(), out_spec=None):
+    out_specs = jax.tree.map(lambda _: out_spec or VMEM, out_shape)
     return pl.pallas_call(
         kernel,
         out_shape=out_shape,
@@ -45,7 +47,31 @@
     )
 
 
-def spread_kernel(place_ref, tokens_ref, out_ref):
+def repeat(piece, out_ref, held_ref, sems):
+    count = held_ref.shape[0]
+    for i in range(count):
+        held_ref[i] = piece
+    copies = [
+        pltpu.make_async_copy(held_ref, out_ref.at[pl.ds(i * count, count)], sems.at[i])
+        for i in range(COPIES)
+    ]
+    for copy in copies:
+        copy.start()
+    for copy in copies:
+        copy.wait()
+
+
+def repeated(kernel, out_shape, in_specs):
+    count = out_shape.shape[0] // COPIES
+    size = 4 * math.prod(out_shape.shape)
+    scratch = [
+        pltpu.VMEM((count,) + out_shape.shape[1:], out_shape.dtype),
+        pltpu.SemaphoreType.DMA((COPIES,)),
+    ]
+    return call(kernel, out_shape, in_specs, 0, size, scratch, ANY)
+
+
+def spread_kernel(place_ref, tokens_ref, out_ref, held_ref, sems):
     width = out_ref.shape[2]
     tokens = tokens_ref[...].astype(jnp.float32)
     left, right = tokens[:, :width], tokens[:, width:]
@@ -56,8 +82,7 @@
     low = jnp.where(upper, first, pltpu.roll(second, 4, 0))
     high = jnp.where(upper, pltpu.roll(first, 4, 0), second)
     piece = jnp.where(place_ref[0] == 0, low, high).astype(out_ref.dtype)
-    for i in range(out_ref.shape[0]):
-        out_ref[i] = piece
+    repeat(piece, out_ref, held_ref, sems)
 
 
 def parent_kernel(tokens_ref, gain_ref, weights_ref, out_ref, rows_ref):
@@ -126,7 +151,7 @@
             out_ref[pair, :, half * rows : (half + 1) * rows] = total.astype(out_ref.dtype)
 
 
-def hidden_kernel(local, sums_ref, out_ref):
+def hidden_kernel(local, sums_ref, out_ref, held_ref, sems):
     total = sums_ref[0].astype(jnp.float32)
     for i in range(1, sums_ref.shape[0]):
         total = total + sums_ref[i].astype(jnp.float32)
@@ -136,17 +161,14 @@
     gate = total[:, :half] * scale
     up = total[:, half:] * scale
     hidden = (gate / (1.0 + jnp.exp(-gate)) * up).astype(out_ref.dtype)
-    for i in range(out_ref.shape[0]):
-        out_ref[i] = hidden
-
-
-def piece_kernel(shares_ref, out_ref):
+    repeat(hidden, out_ref, held_ref, sems)
+
+
+def piece_kernel(shares_ref, out_ref, held_ref, sems):
     total = shares_ref[0].astype(jnp.float32)
     for i in range(1, shares_ref.shape[0]):
         total = total + shares_ref[i].astype(jnp.float32)
-    piece = total.astype(out_ref.dtype)
-    for i in range(out_ref.shape[0]):
-        out_ref[i] = piece
+    repeat(total.astype(out_ref.dtype), out_ref, held_ref, sems)
 
 
 def gradient_kernel(factor, slot_ref, chosen_ref, rounded_ref, out0, out1, out2, out3, error_ref, rows_ref):
@@ -160,12 +182,10 @@
     for k, out_ref in enumerate((out0, out1, out2, out3)):
         out_ref[...] = rows_ref[slot ^ k]
     errors = rounded.astype(jnp.float32)
-    columns = jnp.sum(errors * errors, axis=0, keepdims=True)
+    columns = jnp.sum((errors * errors).reshape(-1, 16, errors.shape[1]), axis=0)
     lanes = columns[:, :128]
     for i in range(1, columns.shape[1] // 128):
         lanes = lanes + columns[:, i * 128 : (i + 1) * 128]
-    line = lax.broadcasted_iota(jnp.int32, (8, 128), 0)
-    lanes = jnp.where(line == 0, lanes, 0.0)
     for i in range(error_ref.shape[0]):
         error_ref[i] = lanes
 
@@ -190,12 +210,10 @@
     blocks = block_groups()
 
     half = tokens.shape[0] // 2
-    pieces = call(
+    pieces = repeated(
         spread_kernel,
         jax.ShapeDtypeStruct((n_wide, 2 * half, width // 2), jnp.bfloat16),
         [SMEM, VMEM],
-        0,
-        2 * n_wide * half * width,
     )(jnp.stack([core, wide % 2]), tokens)
     gathered = lax.all_to_all(pieces, "wide", 0, 0)
 
@@ -220,12 +238,10 @@
 
     scattered = lax.all_to_all(partial.reshape(n_tok, rows, 2 * (local + pad)), "tok", 0, 0)
     scattered, *downs = lax.optimization_barrier((scattered, *downs))
-    hidden = call(
+    hidden = repeated(
         functools.partial(hidden_kernel, local),
         jax.ShapeDtypeStruct((4 * n_tok, rows, local + pad), jnp.bfloat16),
         [VMEM],
-        0,
-        16 * rows * local,
     )(scattered)
 
     groups = [[t * n_wide + w for w in block for t in range(n_tok)] for block in blocks]
@@ -259,7 +275,7 @@
     shares = shares.reshape(n_blocks, total_rows // n_blocks, quarter)
     strides = stride_groups()
     shares = lax.all_to_all(shares, "wide", 0, 0, axis_index_groups=strides)
-    pieces = call(piece_kernel, jax.ShapeDtypeStruct(shares.shape, jnp.bfloat16), [VMEM], 0, 4 * total_rows * quarter)(shares)
+    pieces = repeated(piece_kernel, jax.ShapeDtypeStruct(shares.shape, jnp.bfloat16), [VMEM])(shares)
     rounded = lax.all_to_all(pieces, "wide", 0, 0, axis_index_groups=strides).reshape(total_rows, quarter)
 
     chosen = call(
@@ -274,7 +290,7 @@
         functools.partial(gradient_kernel, factor),
         (
             *[jax.ShapeDtypeStruct((block, quarter), jnp.bfloat16)] * 4,
-            jax.ShapeDtypeStruct((4 * n_tok, 8, 128), jnp.float32),
+            jax.ShapeDtypeStruct((4 * n_tok, 16, 128), jnp.float32),
         ),
         [SMEM, VMEM, VMEM],
         2 * total_rows * 4 * block * quarter,

time: 166 us -> 166 us (level)
  blocking collectives: 38.4 us -> 29.3 us
  waiting for transfers between devices: 54.3 us -> 59.8 us
  starting transfers between devices: 52.2 us -> 55.6 us
    all_to_all x1 -> x0, blocking collectives: 9.07 us -> none  [per_device(): lax.all_to_all(errors, ('tok', 'wide'), 0, 0, axis_index_groups=groups)]
    ppermute x3, waiting for transfers between devices: 0.01 us -> 5.56 us  [per_device(): grads[k] = lax.ppermute(grads[k], 'wide', perm)]
    all_to_all x0 -> x1, starting transfers between devices: none -> 3.41 us  [per_device(): lax.all_to_all(errors, ('tok', 'wide'), 0, 0, axis_index_groups=groups)]
  transfers between devices with their start and end apart: 11 -> 12, of which waited for: 6 -> 8; matrix products, arithmetic and copies ran while one was open for 3% -> 3% of each run, Pallas kernels for 3% -> 3%
where the time goes in v9:
time: 166 us
  waiting for transfers between devices  59.8 us (36%)
  starting transfers between devices  55.6 us (33%)
  blocking collectives  29.3 us (18%)
  Pallas kernels  12.3 us (7%)
  other arithmetic  3.73 us (2%)
  between operations  2.69 us (2%)
  local copies, waits for them, and re-layouts  2.12 us (1%)
    all_to_all x1, blocking collectives, per_device(): shares = lax.all_to_all(shares, 'wide', 0, 0, axis_index_groups=strides)  29.3 us
    all_to_all x1, waiting for transfers between devices, per_device(): lax.all_to_all(pieces, 'wide', 0, 0, axis_index_groups=strides)  20.3 us
    all_to_all x1, waiting for transfers between devices, per_device(): gathered = lax.all_to_all(pieces, 'wide', 0, 0)  17.2 us
    all_to_all x1, starting transfers between devices, per_device(): gathered = lax.all_to_all(pieces, 'wide', 0, 0)  16.9 us
    all_to_all x1, waiting for transfers between devices, per_device(): lax.all_to_all(hidden, ('tok', 'wide'), 0, 0, axis_index_groups=groups)  9.87 us
    ppermute x3, starting transfers between devices, per_device(): grads[k] = lax.ppermute(grads[k], 'wide', perm)  9.21 us
    ppermute x3, starting transfers between devices, per_device(): downs[k] = lax.ppermute(downs[k], 'wide', perm)  9.2 us
    all_to_all x1, starting transfers between devices, per_device(): lax.all_to_all(hidden, ('tok', 'wide'), 0, 0, axis_index_groups=groups)  6.12 us
  transfers between devices with their start and end apart: 12, of which 8 were waited for; matrix products, arithmetic and copies ran while one was open for 3% of the time, Pallas kernels for 3%

profile of v9, /device:TPU:2, one launch (start us, length us, event | category | flops | bytes accessed | tf_op | source)
XLA Modules:
  0.0 165.5 jit_solution(16243602944940996608)
XLA Ops:
  0.6 0.1 pad_add_fusion.place_ref
  0.7 0.0 copy-start
  0.7 0.8 copy-done
  1.5 0.0 copy-start.2
  1.5 1.6 shard_map.77
  3.1 16.9 %all-to-all-start = ((bf16[64,8,1024]{2,1,0:T(8,128)(2,1)}), bf16[64,8,1024]{2,1,0:T(8,128)(2,1)}, u32[]{:S(2)}, u32[]{:S(2)}) async-start(bf16[64,8,1024]{2,1,0:T(8,128)(2,1)} %shard_map.77), calls=%async_computation | async-start | bytes 2097152 | tf_op jit(solution)/shard_map/all_to_all | solution.py:218
  20.1 0.0 copy-done.2
  20.1 1.0 constant_dynamic-slice_fusion
  21.1 3.4 %collective-permute-start = (bf16[320,512]{1,0:T(8,128)(2,1)}, bf16[320,512]{1,0:T(8,128)(2,1)S(1)}, u32[]{:S(2)}, u32[]{:S(2)}) collective-permute-start(bf16[320,512]{1,0:T(8,128)(2,1)} %get-tuple-element.31), channel_id=1, source_target_pairs={{0,1},{1,0},{2,3},{3,2},{4,5},{5,4},{6,7},{7,6},{8,9},{9,8},{10,11... | collective-permute-start | bytes 983048 | tf_op jit(solution)/shard_map/ppermute | solution.py:224
  24.5 3.4 %collective-permute-start.1 = (bf16[320,512]{1,0:T(8,128)(2,1)}, bf16[320,512]{1,0:T(8,128)(2,1)}, u32[]{:S(2)}, u32[]{:S(2)}) collective-permute-start(bf16[320,512]{1,0:T(8,128)(2,1)} %get-tuple-element.33), channel_id=1, source_target_pairs={{0,8},{1,9},{2,10},{3,11},{4,12},{5,13},{6,14},{7,15},{8,0},{9,1},... | collective-permute-start | bytes 983048 | tf_op jit(solution)/shard_map/ppermute | solution.py:224
  27.9 2.4 %collective-permute-start.2 = (bf16[320,512]{1,0:T(8,128)(2,1)}, bf16[320,512]{1,0:T(8,128)(2,1)}, u32[]{:S(2)}, u32[]{:S(2)}) collective-permute-start(bf16[320,512]{1,0:T(8,128)(2,1)} %get-tuple-element.30), channel_id=1, source_target_pairs={{0,9},{1,8},{2,11},{3,10},{4,13},{5,12},{6,15},{7,14},{8,1},{9,0},... | collective-permute-start | bytes 983048 | tf_op jit(solution)/shard_map/ppermute | solution.py:224
  30.3 0.0 copy-start.1
  30.4 1.9 %pad_maximum_fusion.weights_ref = bf16[640,2048]{1,0:T(8,128)(2,1)S(1)} fusion(bf16[320,2048]{1,0:T(8,128)(2,1)} %bitcast.20, bf16[320,2048]{1,0:T(8,128)(2,1)} %bitcast.21), kind=kLoop, calls=%fused_computation | loop fusion | flops 5242880 | bytes 5242880 | tf_op jit(solution)/shard_map/concatenate | solution.py:226
  32.2 17.2 %all-to-all-done.tokens_ref = bf16[64,8,1024]{2,1,0:T(8,128)(2,1)} async-done(((bf16[64,8,1024]{2,1,0:T(8,128)(2,1)}), bf16[64,8,1024]{2,1,0:T(8,128)(2,1)}, u32[]{:S(2)}, u32[]{:S(2)}) %all-to-all-start) | async-done | bytes 1048608 | tf_op jit(solution)/shard_map/all_to_all | solution.py:218
  49.4 0.0 copy-done.1
  49.4 3.3 %shard_map.78 = bf16[256,768]{1,0:T(8,128)(2,1)} custom-call(bf16[64,8,1024]{2,1,0:T(8,128)(2,1)} %all-to-all-done.tokens_ref, f32[1,2048]{1,0:T(1,128)S(1)} %bitcast.19, bf16[640,2048]{1,0:T(8,128)(2,1)S(1)} %pad_maximum_fusion.weights_ref), custom_call_target="tpu_custom_call" | custom-call | flops 671088640 | bytes 5242880 | tf_op jit(solution)/shard_map/pallas_call | solution.py:229
  52.7 4.8 %all-to-all-start.1 = ((bf16[4,64,768]{2,1,0:T(8,128)(2,1)}), bf16[4,64,768]{2,1,0:T(8,128)(2,1)S(1)}, u32[]{:S(2)}, u32[]{:S(2)}) async-start(bf16[4,64,768]{2,1,0:T(8,128)(2,1)} %bitcast.7), calls=%async_computation.1 | async-start | bytes 786432 | tf_op jit(solution)/shard_map/all_to_all | solution.py:239
  57.5 0.0 collective-permute-done.down1
  57.5 0.0 collective-permute-done.1.down2
  57.5 1.3 collective-permute-done.2.down3
  58.9 4.6 %all-to-all-done.1.sums_ref = bf16[4,64,768]{2,1,0:T(8,128)(2,1)S(1)} async-done(((bf16[4,64,768]{2,1,0:T(8,128)(2,1)}), bf16[4,64,768]{2,1,0:T(8,128)(2,1)S(1)}, u32[]{:S(2)}, u32[]{:S(2)}) %all-to-all-start.1) | async-done | bytes 393248 | tf_op jit(solution)/shard_map/all_to_all | solution.py:239
  63.5 1.1 shard_map.79
  64.6 6.1 %all-to-all-start.2 = ((bf16[16,64,384]{2,1,0:T(8,128)(2,1)}), bf16[16,64,384]{2,1,0:T(8,128)(2,1)S(1)}, u32[]{:S(2)}, u32[]{:S(2)}) async-start(bf16[16,64,384]{2,1,0:T(8,128)(2,1)} %shard_map.79), calls=%async_computation.2 | async-start | bytes 1572864 | tf_op jit(solution)/shard_map/all_to_all | solution.py:248
  70.7 9.9 %all-to-all-done.2 = bf16[16,64,384]{2,1,0:T(8,128)(2,1)S(1)} async-done(((bf16[16,64,384]{2,1,0:T(8,128)(2,1)}), bf16[16,64,384]{2,1,0:T(8,128)(2,1)S(1)}, u32[]{:S(2)}, u32[]{:S(2)}) %all-to-all-start.2) | async-done | bytes 786464 | tf_op jit(solution)/shard_map/all_to_all | solution.py:248
  80.6 1.9 %collective-permute-start.3 = (bf16[4,256,384]{2,1,0:T(8,128)(2,1)S(1)}, bf16[4,256,384]{2,1,0:T(8,128)(2,1)S(1)}, u32[]{:S(2)}, u32[]{:S(2)}) collective-permute-start(bf16[4,256,384]{2,1,0:T(8,128)(2,1)S(1)} %bitcast.14), channel_id=1, source_target_pairs={{0,256},{256,0},{1,257},{257,1},{2,258},{258,2},{3,259},{259,3},{4... | collective-permute-start | bytes 2359304 | tf_op jit(solution)/shard_map/ppermute | solution.py:250
  82.5 0.8 fusion.2
  83.3 0.3 fusion
  83.6 0.1 convert_element_type.30
  83.7 0.1 convert_element_type.31
  83.8 0.9 collective-permute-done.3.other_ref
  84.8 2.3 %shard_map.81 = bf16[2,256,512]{2,1,0:T(8,128)(2,1)S(1)} custom-call(s32[1]{0:T(128)} %bitcast.slot_ref, bf16[4,256,384]{2,1,0:T(8,128)(2,1)S(1)} %bitcast.15, bf16[4,256,384]{2,1,0:T(8,128)(2,1)S(1)} %collective-permute-done.3.other_ref, bf16[4,1,320]{2,1,0:T(2,128)(2,1)S(1)} %pad_maximum_fusion.1.drop_ref, bf16[320,512]{1,0:T(8,128)(2,1)S(1)} %get-tuple-element.17.down0, ...), custom_call_target="tpu_custom_call" | custom-call | flops 671088640 | bytes 1048576 | tf_op jit(solution)/shard_map/pallas_call | solution.py:268
  87.1 29.3 %all_to_all.30.shares_ref = bf16[16,32,512]{2,1,0:T(8,128)(2,1)S(1)} all-to-all(bf16[16,32,512]{2,1,0:T(8,128)(2,1)S(1)} %bitcast.17), channel_id=1, replica_groups={{0,2,4,6,16,18,20,22,32,34,36,38,48,50,52,54},{1,3,5,7,17,19,21,23,33,3..., dimensions={0} | all-to-all | bytes 1048576 | tf_op jit(solution)/shard_map/all_to_all | solution.py:277
  116.4 0.9 shard_map.82
  117.3 4.1 %all-to-all-start.4 = ((bf16[16,32,512]{2,1,0:T(8,128)(2,1)}), bf16[16,32,512]{2,1,0:T(8,128)(2,1)S(1)}, u32[]{:S(2)}, u32[]{:S(2)}) async-start(bf16[16,32,512]{2,1,0:T(8,128)(2,1)} %shard_map.82), calls=%async_computation.4 | async-start | bytes 1048576 | tf_op jit(solution)/shard_map/all_to_all | solution.py:279
  121.4 0.2 copy.11.names_ref
  121.6 0.9 shard_map.80.chosen_ref
  122.5 20.3 %all-to-all-done.4 = bf16[16,32,512]{2,1,0:T(8,128)(2,1)S(1)} async-done(((bf16[16,32,512]{2,1,0:T(8,128)(2,1)}), bf16[16,32,512]{2,1,0:T(8,128)(2,1)S(1)}, u32[]{:S(2)}, u32[]{:S(2)}) %all-to-all-start.4) | async-done | bytes 524320 | tf_op jit(solution)/shard_map/all_to_all | solution.py:279
  142.9 1.1 shard_map.83
  144.0 3.4 %all-to-all-start.5 = ((f32[16,16,128]{2,1,0:T(8,128)}), f32[16,16,128]{2,1,0:T(8,128)S(1)}, u32[]{:S(2)}, u32[]{:S(2)}) async-start(f32[16,16,128]{2,1,0:T(8,128)} %get-tuple-element.21), calls=%async_computation.5 | async-start | bytes 262144 | tf_op jit(solution)/shard_map/all_to_all | solution.py:300
  147.4 3.3 %collective-permute-start.4 = (bf16[160,512]{1,0:T(8,128)(2,1)S(1)}, bf16[160,512]{1,0:T(8,128)(2,1)S(1)}, u32[]{:S(2)}, u32[]{:S(2)}) collective-permute-start(bf16[160,512]{1,0:T(8,128)(2,1)S(1)} %get-tuple-element.23), channel_id=1, source_target_pairs={{0,1},{1,0},{2,3},{3,2},{4,5},{5,4},{6,7},{7,6},{8,9},{9,8},{10,11... | collective-permute-start | bytes 491528 | tf_op jit(solution)/shard_map/ppermute | solution.py:304
  150.7 3.4 %collective-permute-start.5 = (bf16[160,512]{1,0:T(8,128)(2,1)S(1)}, bf16[160,512]{1,0:T(8,128)(2,1)S(1)}, u32[]{:S(2)}, u32[]{:S(2)}) collective-permute-start(bf16[160,512]{1,0:T(8,128)(2,1)S(1)} %get-tuple-element.24), channel_id=1, source_target_pairs={{0,8},{1,9},{2,10},{3,11},{4,12},{5,13},{6,14},{7,15},{8,0},{9,1},... | collective-permute-start | bytes 491528 | tf_op jit(solution)/shard_map/ppermute | solution.py:304
  154.1 2.5 %collective-permute-start.6 = (bf16[160,512]{1,0:T(8,128)(2,1)S(1)}, bf16[160,512]{1,0:T(8,128)(2,1)S(1)}, u32[]{:S(2)}, u32[]{:S(2)}) collective-permute-start(bf16[160,512]{1,0:T(8,128)(2,1)S(1)} %get-tuple-element.25), channel_id=1, source_target_pairs={{0,9},{1,8},{2,11},{3,10},{4,13},{5,12},{6,15},{7,14},{8,1},{9,0},... | collective-permute-start | bytes 491528 | tf_op jit(solution)/shard_map/ppermute | solution.py:304
  156.6 0.0 collective-permute-done.4.in1
  156.6 2.1 %collective-permute-done.5.in2 = bf16[160,512]{1,0:T(8,128)(2,1)S(1)} collective-permute-done((bf16[160,512]{1,0:T(8,128)(2,1)S(1)}, bf16[160,512]{1,0:T(8,128)(2,1)S(1)}, u32[]{:S(2)}, u32[]{:S(2)}) %collective-permute-start.5) | collective-permute-done | bytes 163872 | tf_op jit(solution)/shard_map/ppermute | solution.py:304
  158.7 3.5 %collective-permute-done.6.in3 = bf16[160,512]{1,0:T(8,128)(2,1)S(1)} collective-permute-done((bf16[160,512]{1,0:T(8,128)(2,1)S(1)}, bf16[160,512]{1,0:T(8,128)(2,1)S(1)}, u32[]{:S(2)}, u32[]{:S(2)}) %collective-permute-start.6) | collective-permute-done | bytes 163872 | tf_op jit(solution)/shard_map/ppermute | solution.py:304
  162.2 0.9 shard_map.84
  163.1 0.0 all-to-all-done.5
  163.1 0.6 reduce_sum.9
  (4 shorter events, 0.0 us)
Async XLA Ops:
  0.7 0.8 copy-start
  1.5 18.6 %copy-start.2 = (bf16[320,2048]{1,0:T(8,128)(2,1)S(1)}, bf16[320,2048]{1,0:T(8,128)(2,1)}, u32[]{:S(2)}) copy-start(bf16[320,2048]{1,0:T(8,128)(2,1)} %param.10) | copy-start | bytes 3932164
  3.1 46.3 %all-to-all-start = ((bf16[64,8,1024]{2,1,0:T(8,128)(2,1)}), bf16[64,8,1024]{2,1,0:T(8,128)(2,1)}, u32[]{:S(2)}, u32[]{:S(2)}) async-start(bf16[64,8,1024]{2,1,0:T(8,128)(2,1)} %shard_map.77), calls=%async_computation | async-start | bytes 2097152 | tf_op jit(solution)/shard_map/all_to_all | solution.py:218
  21.1 36.4 %collective-permute-start = (bf16[320,512]{1,0:T(8,128)(2,1)}, bf16[320,512]{1,0:T(8,128)(2,1)S(1)}, u32[]{:S(2)}, u32[]{:S(2)}) collective-permute-start(bf16[320,512]{1,0:T(8,128)(2,1)} %get-tuple-element.31), channel_id=1, source_target_pairs={{0,1},{1,0},{2,3},{3,2},{4,5},{5,4},{6,7},{7,6},{8,9},{9,8},{10,11... | collective-permute-start | bytes 983048 | tf_op jit(solution)/shard_map/ppermute | solution.py:224
  24.5 33.0 %collective-permute-start.1 = (bf16[320,512]{1,0:T(8,128)(2,1)}, bf16[320,512]{1,0:T(8,128)(2,1)}, u32[]{:S(2)}, u32[]{:S(2)}) collective-permute-start(bf16[320,512]{1,0:T(8,128)(2,1)} %get-tuple-element.33), channel_id=1, source_target_pairs={{0,8},{1,9},{2,10},{3,11},{4,12},{5,13},{6,14},{7,15},{8,0},{9,1},... | collective-permute-start | bytes 983048 | tf_op jit(solution)/shard_map/ppermute | solution.py:224
  27.9 31.0 %collective-permute-start.2 = (bf16[320,512]{1,0:T(8,128)(2,1)}, bf16[320,512]{1,0:T(8,128)(2,1)}, u32[]{:S(2)}, u32[]{:S(2)}) collective-permute-start(bf16[320,512]{1,0:T(8,128)(2,1)} %get-tuple-element.30), channel_id=1, source_target_pairs={{0,9},{1,8},{2,11},{3,10},{4,13},{5,12},{6,15},{7,14},{8,1},{9,0},... | collective-permute-start | bytes 983048 | tf_op jit(solution)/shard_map/ppermute | solution.py:224
  30.3 19.1 %copy-start.1 = (f32[2048]{0:T(1024)S(1)}, f32[2048]{0:T(1024)}, u32[]{:S(2)}) copy-start(f32[2048]{0:T(1024)} %param.7) | copy-start | bytes 24580
  52.7 10.7 %all-to-all-start.1 = ((bf16[4,64,768]{2,1,0:T(8,128)(2,1)}), bf16[4,64,768]{2,1,0:T(8,128)(2,1)S(1)}, u32[]{:S(2)}, u32[]{:S(2)}) async-start(bf16[4,64,768]{2,1,0:T(8,128)(2,1)} %bitcast.7), calls=%async_computation.1 | async-start | bytes 786432 | tf_op jit(solution)/shard_map/all_to_all | solution.py:239
  64.6 16.0 %all-to-all-start.2 = ((bf16[16,64,384]{2,1,0:T(8,128)(2,1)}), bf16[16,64,384]{2,1,0:T(8,128)(2,1)S(1)}, u32[]{:S(2)}, u32[]{:S(2)}) async-start(bf16[16,64,384]{2,1,0:T(8,128)(2,1)} %shard_map.79), calls=%async_computation.2 | async-start | bytes 1572864 | tf_op jit(solution)/shard_map/all_to_all | solution.py:248
  80.6 4.2 %collective-permute-start.3 = (bf16[4,256,384]{2,1,0:T(8,128)(2,1)S(1)}, bf16[4,256,384]{2,1,0:T(8,128)(2,1)S(1)}, u32[]{:S(2)}, u32[]{:S(2)}) collective-permute-start(bf16[4,256,384]{2,1,0:T(8,128)(2,1)S(1)} %bitcast.14), channel_id=1, source_target_pairs={{0,256},{256,0},{1,257},{257,1},{2,258},{258,2},{3,259},{259,3},{4... | collective-permute-start | bytes 2359304 | tf_op jit(solution)/shard_map/ppermute | solution.py:250
  117.3 25.5 %all-to-all-start.4 = ((bf16[16,32,512]{2,1,0:T(8,128)(2,1)}), bf16[16,32,512]{2,1,0:T(8,128)(2,1)S(1)}, u32[]{:S(2)}, u32[]{:S(2)}) async-start(bf16[16,32,512]{2,1,0:T(8,128)(2,1)} %shard_map.82), calls=%async_computation.4 | async-start | bytes 1048576 | tf_op jit(solution)/shard_map/all_to_all | solution.py:279
  144.0 19.1 %all-to-all-start.5 = ((f32[16,16,128]{2,1,0:T(8,128)}), f32[16,16,128]{2,1,0:T(8,128)S(1)}, u32[]{:S(2)}, u32[]{:S(2)}) async-start(f32[16,16,128]{2,1,0:T(8,128)} %get-tuple-element.21), calls=%async_computation.5 | async-start | bytes 262144 | tf_op jit(solution)/shard_map/all_to_all | solution.py:300
  147.4 9.2 %collective-permute-start.4 = (bf16[160,512]{1,0:T(8,128)(2,1)S(1)}, bf16[160,512]{1,0:T(8,128)(2,1)S(1)}, u32[]{:S(2)}, u32[]{:S(2)}) collective-permute-start(bf16[160,512]{1,0:T(8,128)(2,1)S(1)} %get-tuple-element.23), channel_id=1, source_target_pairs={{0,1},{1,0},{2,3},{3,2},{4,5},{5,4},{6,7},{7,6},{8,9},{9,8},{10,11... | collective-permute-start | bytes 491528 | tf_op jit(solution)/shard_map/ppermute | solution.py:304
  150.7 8.0 %collective-permute-start.5 = (bf16[160,512]{1,0:T(8,128)(2,1)S(1)}, bf16[160,512]{1,0:T(8,128)(2,1)S(1)}, u32[]{:S(2)}, u32[]{:S(2)}) collective-permute-start(bf16[160,512]{1,0:T(8,128)(2,1)S(1)} %get-tuple-element.24), channel_id=1, source_target_pairs={{0,8},{1,9},{2,10},{3,11},{4,12},{5,13},{6,14},{7,15},{8,0},{9,1},... | collective-permute-start | bytes 491528 | tf_op jit(solution)/shard_map/ppermute | solution.py:304
  154.1 8.1 %collective-permute-start.6 = (bf16[160,512]{1,0:T(8,128)(2,1)S(1)}, bf16[160,512]{1,0:T(8,128)(2,1)S(1)}, u32[]{:S(2)}, u32[]{:S(2)}) collective-permute-start(bf16[160,512]{1,0:T(8,128)(2,1)S(1)} %get-tuple-element.25), channel_id=1, source_target_pairs={{0,9},{1,8},{2,11},{3,10},{4,13},{5,12},{6,15},{7,14},{8,1},{9,0},... | collective-permute-start | bytes 491528 | tf_op jit(solution)/shard_map/ppermute | solution.py:304

commit v10 on v9

--- a/solution.py
+++ b/solution.py
@@ -29,7 +29,6 @@
 
 
 VMEM = pl.BlockSpec(memory_space=pltpu.VMEM)
-SMEM = pl.BlockSpec(memory_space=pltpu.SMEM)
 ANY = pl.BlockSpec(memory_space=pl.ANY)
 COPIES = 8
 
@@ -47,6 +46,11 @@
     )
 
 
+def block_slot():
+    wide = lax.axis_index("wide")
+    return wide // SIDE % 2 * 2 + wide % 2
+
+
 def repeat(piece, out_ref, held_ref, sems):
     count = held_ref.shape[0]
     for i in range(count):
@@ -71,23 +75,28 @@
     return call(kernel, out_shape, in_specs, 0, size, scratch, ANY)
 
 
-def spread_kernel(place_ref, tokens_ref, out_ref, held_ref, sems):
+def spread_kernel(tokens_ref, out_ref, held_ref, sems):
     width = out_ref.shape[2]
     tokens = tokens_ref[...].astype(jnp.float32)
     left, right = tokens[:, :width], tokens[:, width:]
-    odd = place_ref[1] == 1
+    odd = lax.axis_index("wide") % 2 == 1
     first = jnp.where(odd, right, left)
     second = jnp.where(odd, left, right)
     upper = lax.broadcasted_iota(jnp.int32, first.shape, 0) < 4
     low = jnp.where(upper, first, pltpu.roll(second, 4, 0))
     high = jnp.where(upper, pltpu.roll(first, 4, 0), second)
-    piece = jnp.where(place_ref[0] == 0, low, high).astype(out_ref.dtype)
+    piece = jnp.where(lax.axis_index("var") == 0, low, high).astype(out_ref.dtype)
     repeat(piece, out_ref, held_ref, sems)
 
 
-def parent_kernel(tokens_ref, gain_ref, weights_ref, out_ref, rows_ref):
+def parent_kernel(tokens_ref, gain_ref, weights_any, out_ref, rows_ref, weights_ref, sems):
     n_shards, _, width = tokens_ref.shape
-    local = weights_ref.shape[0] // 2
+    local = weights_ref.shape[1]
+    copies = [
+        pltpu.make_async_copy(weights_any.at[pl.ds(i * local, local)], weights_ref.at[i], sems.at[i]) for i in range(2)
+    ]
+    for copy in copies:
+        copy.start()
     lanes = out_ref.shape[1] // 2
     step = 16
     squares = []
@@ -106,8 +115,10 @@
     squares = jnp.concatenate(squares, axis=0)
     hi = squares.astype(jnp.bfloat16).astype(jnp.float32)
     contract = (((1,), (1,)), ((), ()))
-    gate = lax.dot_general(rows_ref[...], weights_ref[:local], contract, preferred_element_type=jnp.float32)
-    up = lax.dot_general(rows_ref[...], weights_ref[local:], contract, preferred_element_type=jnp.float32)
+    copies[0].wait()
+    gate = lax.dot_general(rows_ref[...], weights_ref[0], contract, preferred_element_type=jnp.float32)
+    copies[1].wait()
+    up = lax.dot_general(rows_ref[...], weights_ref[1], contract, preferred_element_type=jnp.float32)
     lane = lax.broadcasted_iota(jnp.int32, (squares.shape[0], lanes - local), 1)
     extra = jnp.where(lane == 0, hi, jnp.where(lane == 1, squares - hi, 0.0))
     out_ref[:, :local] = gate.astype(out_ref.dtype)
@@ -116,8 +127,8 @@
     out_ref[:, lanes + local :] = jnp.zeros_like(extra).astype(out_ref.dtype)
 
 
-def residual_kernel(slot_ref, own_ref, other_ref, drop_ref, down0, down1, down2, down3, out_ref):
-    slot = slot_ref[0]
+def residual_kernel(own_ref, other_ref, drop_ref, down0, down1, down2, down3, out_ref):
+    slot = block_slot()
     downs = (down0, down1, down2, down3)
     local = down0.shape[0]
     for half, hidden_ref in enumerate((own_ref, other_ref)):
@@ -171,8 +182,8 @@
     repeat(total.astype(out_ref.dtype), out_ref, held_ref, sems)
 
 
-def gradient_kernel(factor, slot_ref, chosen_ref, rounded_ref, out0, out1, out2, out3, error_ref, rows_ref):
-    slot = slot_ref[0]
+def gradient_kernel(factor, chosen_ref, rounded_ref, out0, out1, out2, out3, error_ref, rows_ref):
+    slot = block_slot()
     rounded = rounded_ref[...]
     block = out0.shape[0]
     for pair in range(2):
@@ -190,8 +201,8 @@
         error_ref[i] = lanes
 
 
-def interleave_kernel(slot_ref, in0, in1, in2, in3, out_ref):
-    slot = slot_ref[0]
+def interleave_kernel(in0, in1, in2, in3, out_ref):
+    slot = block_slot()
     width = in0.shape[1]
     for k, in_ref in enumerate((in0, in1, in2, in3)):
         start = pl.multiple_of((slot ^ k) * width, 128)
@@ -213,8 +224,8 @@
     pieces = repeated(
         spread_kernel,
         jax.ShapeDtypeStruct((n_wide, 2 * half, width // 2), jnp.bfloat16),
-        [SMEM, VMEM],
-    )(jnp.stack([core, wide % 2]), tokens)
+        [VMEM],
+    )(tokens)
     gathered = lax.all_to_all(pieces, "wide", 0, 0)
 
     quarter = down_parent.shape[1] // 4
@@ -229,10 +240,14 @@
     partial = call(
         parent_kernel,
         jax.ShapeDtypeStruct((n_wide * half, 2 * (local + pad)), jnp.bfloat16),
-        [VMEM] * 3,
+        [VMEM, VMEM, ANY],
         4 * n_wide * half * width * local,
         8 * width * local,
-        [pltpu.VMEM((n_wide * half, width), jnp.bfloat16)],
+        [
+            pltpu.VMEM((n_wide * half, width), jnp.bfloat16),
+            pltpu.VMEM((2, local, width), jnp.bfloat16),
+            pltpu.SemaphoreType.DMA((2,)),
+        ],
     )(gathered, norm_gain.reshape(1, width), weights)
     rows = n_wide * half // n_tok
 
@@ -268,10 +283,10 @@
     shares = call(
         residual_kernel,
         jax.ShapeDtypeStruct((2, total_rows // 2, quarter), jnp.bfloat16),
-        [SMEM] + [VMEM] * 7,
+        [VMEM] * 7,
         product_flops,
         4 * total_rows * quarter,
-    )(slot.reshape(1), hidden, other, drop, *downs)
+    )(hidden, other, drop, *downs)
     shares = shares.reshape(n_blocks, total_rows // n_blocks, quarter)
     strides = stride_groups()
     shares = lax.all_to_all(shares, "wide", 0, 0, axis_index_groups=strides)
@@ -292,11 +307,11 @@
             *[jax.ShapeDtypeStruct((block, quarter), jnp.bfloat16)] * 4,
             jax.ShapeDtypeStruct((4 * n_tok, 16, 128), jnp.float32),
         ),
-        [SMEM, VMEM, VMEM],
+        [VMEM, VMEM],
         2 * total_rows * 4 * block * quarter,
         4 * total_rows * quarter,
         [pltpu.VMEM((4, block, quarter), jnp.bfloat16)],
-    )(slot.reshape(1), chosen, rounded)
+    )(chosen, rounded)
     errors = lax.all_to_all(errors, ("tok", "wide"), 0, 0, axis_index_groups=groups)
     loss = jnp.sum(errors) / (total_rows * D)
     for k in range(1, 4):
@@ -305,10 +320,10 @@
     grad = call(
         interleave_kernel,
         jax.ShapeDtypeStruct((block, 4 * quarter), jnp.bfloat16),
-        [SMEM] + [VMEM] * 4,
+        [VMEM] * 4,
         0,
         4 * block * quarter,
-    )(slot.reshape(1), *grads)
+    )(*grads)
     return (loss.reshape(1), grad[None])
 
 

time: 166 us -> 166 us (level)
  transfers between devices with their start and end apart: 12 -> 12, of which waited for: 8 -> 8; matrix products, arithmetic and copies ran while one was open for 3% -> 3% of each run, Pallas kernels for 3% -> 4%
where the time goes in v10:
time: 166 us; the launch traced here: 165 us
  waiting for transfers between devices  59.8 us (36%)
  starting transfers between devices  55.7 us (34%)
  blocking collectives  28.5 us (17%)
  Pallas kernels  12.5 us (8%)
  other arithmetic  3.65 us (2%)
  between operations  2.68 us (2%)
  local copies, waits for them, and re-layouts  2.11 us (1%)
    all_to_all x1, blocking collectives, per_device(): shares = lax.all_to_all(shares, 'wide', 0, 0, axis_index_groups=strides)  28.5 us
    all_to_all x1, waiting for transfers between devices, per_device(): lax.all_to_all(pieces, 'wide', 0, 0, axis_index_groups=strides)  20.2 us
    all_to_all x1, waiting for transfers between devices, per_device(): gathered = lax.all_to_all(pieces, 'wide', 0, 0)  17.2 us
    all_to_all x1, starting transfers between devices, per_device(): gathered = lax.all_to_all(pieces, 'wide', 0, 0)  16.9 us
    all_to_all x1, waiting for transfers between devices, per_device(): lax.all_to_all(hidden, ('tok', 'wide'), 0, 0, axis_index_groups=groups)  9.87 us
    ppermute x3, starting transfers between devices, per_device(): downs[k] = lax.ppermute(downs[k], 'wide', perm)  9.2 us
    ppermute x3, starting transfers between devices, per_device(): grads[k] = lax.ppermute(grads[k], 'wide', perm)  9.2 us
    all_to_all x1, starting transfers between devices, per_device(): lax.all_to_all(hidden, ('tok', 'wide'), 0, 0, axis_index_groups=groups)  6.11 us
  transfers between devices with their start and end apart: 12, of which 8 were waited for; matrix products, arithmetic and copies ran while one was open for 3% of the time, Pallas kernels for 4%

profile of v10, /device:TPU:2, one launch (start us, length us, event | category | flops | bytes accessed | tf_op | source)
XLA Modules:
  0.0 165.1 jit_solution(16334353324787870113)
XLA Ops:
  0.6 0.0 copy-start
  0.6 0.7 copy-done
  1.4 0.0 copy-start.2
  1.4 1.1 shard_map.77
  2.5 16.9 %all-to-all-start = ((bf16[64,8,1024]{2,1,0:T(8,128)(2,1)}), bf16[64,8,1024]{2,1,0:T(8,128)(2,1)}, u32[]{:S(2)}, u32[]{:S(2)}) async-start(bf16[64,8,1024]{2,1,0:T(8,128)(2,1)} %shard_map.77), calls=%async_computation | async-start | bytes 2097152 | tf_op jit(solution)/shard_map/all_to_all | solution.py:229
  19.5 0.0 copy-done.2
  19.5 1.0 constant_dynamic-slice_fusion
  20.5 3.4 %collective-permute-start = (bf16[320,512]{1,0:T(8,128)(2,1)}, bf16[320,512]{1,0:T(8,128)(2,1)S(1)}, u32[]{:S(2)}, u32[]{:S(2)}) collective-permute-start(bf16[320,512]{1,0:T(8,128)(2,1)} %get-tuple-element.31), channel_id=1, source_target_pairs={{0,1},{1,0},{2,3},{3,2},{4,5},{5,4},{6,7},{7,6},{8,9},{9,8},{10,11... | collective-permute-start | bytes 983048 | tf_op jit(solution)/shard_map/ppermute | solution.py:235
  23.9 3.4 %collective-permute-start.1 = (bf16[320,512]{1,0:T(8,128)(2,1)}, bf16[320,512]{1,0:T(8,128)(2,1)}, u32[]{:S(2)}, u32[]{:S(2)}) collective-permute-start(bf16[320,512]{1,0:T(8,128)(2,1)} %get-tuple-element.33), channel_id=1, source_target_pairs={{0,8},{1,9},{2,10},{3,11},{4,12},{5,13},{6,14},{7,15},{8,0},{9,1},... | collective-permute-start | bytes 983048 | tf_op jit(solution)/shard_map/ppermute | solution.py:235
  27.3 2.4 %collective-permute-start.2 = (bf16[320,512]{1,0:T(8,128)(2,1)}, bf16[320,512]{1,0:T(8,128)(2,1)}, u32[]{:S(2)}, u32[]{:S(2)}) collective-permute-start(bf16[320,512]{1,0:T(8,128)(2,1)} %get-tuple-element.30), channel_id=1, source_target_pairs={{0,9},{1,8},{2,11},{3,10},{4,13},{5,12},{6,15},{7,14},{8,1},{9,0},... | collective-permute-start | bytes 983048 | tf_op jit(solution)/shard_map/ppermute | solution.py:235
  29.7 0.0 copy-start.1
  29.7 1.9 %pad_maximum_fusion.weights_any = bf16[640,2048]{1,0:T(8,128)(2,1)S(1)} fusion(bf16[320,2048]{1,0:T(8,128)(2,1)} %bitcast.17, bf16[320,2048]{1,0:T(8,128)(2,1)} %bitcast.18), kind=kLoop, calls=%fused_computation | loop fusion | flops 5242880 | bytes 5242880 | tf_op jit(solution)/shard_map/concatenate | solution.py:237
  31.6 17.2 %all-to-all-done.tokens_ref = bf16[64,8,1024]{2,1,0:T(8,128)(2,1)} async-done(((bf16[64,8,1024]{2,1,0:T(8,128)(2,1)}), bf16[64,8,1024]{2,1,0:T(8,128)(2,1)}, u32[]{:S(2)}, u32[]{:S(2)}) %all-to-all-start) | async-done | bytes 1048608 | tf_op jit(solution)/shard_map/all_to_all | solution.py:229
  48.8 0.0 copy-done.1
  48.8 4.1 %shard_map.78 = bf16[256,768]{1,0:T(8,128)(2,1)} custom-call(bf16[64,8,1024]{2,1,0:T(8,128)(2,1)} %all-to-all-done.tokens_ref, f32[1,2048]{1,0:T(1,128)S(1)} %bitcast.16, bf16[640,2048]{1,0:T(8,128)(2,1)S(1)} %pad_maximum_fusion.weights_any), custom_call_target="tpu_custom_call" | custom-call | flops 671088640 | bytes 5242880 | tf_op jit(solution)/shard_map/pallas_call | solution.py:240
  52.9 4.8 %all-to-all-start.1 = ((bf16[4,64,768]{2,1,0:T(8,128)(2,1)}), bf16[4,64,768]{2,1,0:T(8,128)(2,1)S(1)}, u32[]{:S(2)}, u32[]{:S(2)}) async-start(bf16[4,64,768]{2,1,0:T(8,128)(2,1)} %bitcast.4), calls=%async_computation.1 | async-start | bytes 786432 | tf_op jit(solution)/shard_map/all_to_all | solution.py:254
  57.7 0.0 collective-permute-done.down1
  57.7 0.0 collective-permute-done.1.down2
  57.7 0.5 collective-permute-done.2.down3
  58.3 5.4 %all-to-all-done.1.sums_ref = bf16[4,64,768]{2,1,0:T(8,128)(2,1)S(1)} async-done(((bf16[4,64,768]{2,1,0:T(8,128)(2,1)}), bf16[4,64,768]{2,1,0:T(8,128)(2,1)S(1)}, u32[]{:S(2)}, u32[]{:S(2)}) %all-to-all-start.1) | async-done | bytes 393248 | tf_op jit(solution)/shard_map/all_to_all | solution.py:254
  63.6 1.1 shard_map.79
  64.8 6.1 %all-to-all-start.2 = ((bf16[16,64,384]{2,1,0:T(8,128)(2,1)}), bf16[16,64,384]{2,1,0:T(8,128)(2,1)S(1)}, u32[]{:S(2)}, u32[]{:S(2)}) async-start(bf16[16,64,384]{2,1,0:T(8,128)(2,1)} %shard_map.79), calls=%async_computation.2 | async-start | bytes 1572864 | tf_op jit(solution)/shard_map/all_to_all | solution.py:263
  70.9 9.9 %all-to-all-done.2 = bf16[16,64,384]{2,1,0:T(8,128)(2,1)S(1)} async-done(((bf16[16,64,384]{2,1,0:T(8,128)(2,1)}), bf16[16,64,384]{2,1,0:T(8,128)(2,1)S(1)}, u32[]{:S(2)}, u32[]{:S(2)}) %all-to-all-start.2) | async-done | bytes 786464 | tf_op jit(solution)/shard_map/all_to_all | solution.py:263
  80.8 1.9 %collective-permute-start.3 = (bf16[4,256,384]{2,1,0:T(8,128)(2,1)S(1)}, bf16[4,256,384]{2,1,0:T(8,128)(2,1)S(1)}, u32[]{:S(2)}, u32[]{:S(2)}) collective-permute-start(bf16[4,256,384]{2,1,0:T(8,128)(2,1)S(1)} %bitcast.11), channel_id=1, source_target_pairs={{0,256},{256,0},{1,257},{257,1},{2,258},{258,2},{3,259},{259,3},{4... | collective-permute-start | bytes 2359304 | tf_op jit(solution)/shard_map/ppermute | solution.py:265
  82.7 0.8 fusion.2
  83.5 0.3 fusion
  83.8 0.1 convert_element_type.31
  83.9 0.1 convert_element_type.30
  84.0 0.9 collective-permute-done.3.other_ref
  85.0 2.3 %shard_map.81 = bf16[2,256,512]{2,1,0:T(8,128)(2,1)S(1)} custom-call(bf16[4,256,384]{2,1,0:T(8,128)(2,1)S(1)} %bitcast.12, bf16[4,256,384]{2,1,0:T(8,128)(2,1)S(1)} %collective-permute-done.3.other_ref, bf16[4,1,320]{2,1,0:T(2,128)(2,1)S(1)} %pad_maximum_fusion.1.drop_ref, bf16[320,512]{1,0:T(8,128)(2,1)S(1)} %get-tuple-element.17.down0, ...), custom_call_target="tpu_custom_call" | custom-call | flops 671088640 | bytes 1048576 | tf_op jit(solution)/shard_map/pallas_call | solution.py:283
  87.3 28.5 %all_to_all.30.shares_ref = bf16[16,32,512]{2,1,0:T(8,128)(2,1)S(1)} all-to-all(bf16[16,32,512]{2,1,0:T(8,128)(2,1)S(1)} %bitcast.14), channel_id=1, replica_groups={{0,2,4,6,16,18,20,22,32,34,36,38,48,50,52,54},{1,3,5,7,17,19,21,23,33,3..., dimensions={0} | all-to-all | bytes 1048576 | tf_op jit(solution)/shard_map/all_to_all | solution.py:292
  115.8 0.9 shard_map.82
  116.7 4.1 %all-to-all-start.4 = ((bf16[16,32,512]{2,1,0:T(8,128)(2,1)}), bf16[16,32,512]{2,1,0:T(8,128)(2,1)S(1)}, u32[]{:S(2)}, u32[]{:S(2)}) async-start(bf16[16,32,512]{2,1,0:T(8,128)(2,1)} %shard_map.82), calls=%async_computation.4 | async-start | bytes 1048576 | tf_op jit(solution)/shard_map/all_to_all | solution.py:294
  120.8 0.2 copy.11.names_ref
  121.0 0.9 shard_map.80.chosen_ref
  121.9 20.2 %all-to-all-done.4 = bf16[16,32,512]{2,1,0:T(8,128)(2,1)S(1)} async-done(((bf16[16,32,512]{2,1,0:T(8,128)(2,1)}), bf16[16,32,512]{2,1,0:T(8,128)(2,1)S(1)}, u32[]{:S(2)}, u32[]{:S(2)}) %all-to-all-start.4) | async-done | bytes 524320 | tf_op jit(solution)/shard_map/all_to_all | solution.py:294
  142.2 1.1 shard_map.83
  143.3 3.5 %all-to-all-start.5 = ((f32[16,16,128]{2,1,0:T(8,128)}), f32[16,16,128]{2,1,0:T(8,128)S(1)}, u32[]{:S(2)}, u32[]{:S(2)}) async-start(f32[16,16,128]{2,1,0:T(8,128)} %get-tuple-element.21), calls=%async_computation.5 | async-start | bytes 262144 | tf_op jit(solution)/shard_map/all_to_all | solution.py:315
  146.8 3.4 %collective-permute-start.4 = (bf16[160,512]{1,0:T(8,128)(2,1)S(1)}, bf16[160,512]{1,0:T(8,128)(2,1)S(1)}, u32[]{:S(2)}, u32[]{:S(2)}) collective-permute-start(bf16[160,512]{1,0:T(8,128)(2,1)S(1)} %get-tuple-element.23), channel_id=1, source_target_pairs={{0,1},{1,0},{2,3},{3,2},{4,5},{5,4},{6,7},{7,6},{8,9},{9,8},{10,11... | collective-permute-start | bytes 491528 | tf_op jit(solution)/shard_map/ppermute | solution.py:319
  150.2 3.4 %collective-permute-start.5 = (bf16[160,512]{1,0:T(8,128)(2,1)S(1)}, bf16[160,512]{1,0:T(8,128)(2,1)S(1)}, u32[]{:S(2)}, u32[]{:S(2)}) collective-permute-start(bf16[160,512]{1,0:T(8,128)(2,1)S(1)} %get-tuple-element.24), channel_id=1, source_target_pairs={{0,8},{1,9},{2,10},{3,11},{4,12},{5,13},{6,14},{7,15},{8,0},{9,1},... | collective-permute-start | bytes 491528 | tf_op jit(solution)/shard_map/ppermute | solution.py:319
  153.6 2.4 %collective-permute-start.6 = (bf16[160,512]{1,0:T(8,128)(2,1)S(1)}, bf16[160,512]{1,0:T(8,128)(2,1)S(1)}, u32[]{:S(2)}, u32[]{:S(2)}) collective-permute-start(bf16[160,512]{1,0:T(8,128)(2,1)S(1)} %get-tuple-element.25), channel_id=1, source_target_pairs={{0,9},{1,8},{2,11},{3,10},{4,13},{5,12},{6,15},{7,14},{8,1},{9,0},... | collective-permute-start | bytes 491528 | tf_op jit(solution)/shard_map/ppermute | solution.py:319
  156.0 0.0 collective-permute-done.4.in1
  156.1 2.1 %collective-permute-done.5.in2 = bf16[160,512]{1,0:T(8,128)(2,1)S(1)} collective-permute-done((bf16[160,512]{1,0:T(8,128)(2,1)S(1)}, bf16[160,512]{1,0:T(8,128)(2,1)S(1)}, u32[]{:S(2)}, u32[]{:S(2)}) %collective-permute-start.5) | collective-permute-done | bytes 163872 | tf_op jit(solution)/shard_map/ppermute | solution.py:319
  158.1 3.7 %collective-permute-done.6.in3 = bf16[160,512]{1,0:T(8,128)(2,1)S(1)} collective-permute-done((bf16[160,512]{1,0:T(8,128)(2,1)S(1)}, bf16[160,512]{1,0:T(8,128)(2,1)S(1)}, u32[]{:S(2)}, u32[]{:S(2)}) %collective-permute-start.6) | collective-permute-done | bytes 163872 | tf_op jit(solution)/shard_map/ppermute | solution.py:319
  161.8 0.9 shard_map.84
  162.7 0.0 all-to-all-done.5
  162.7 0.6 reduce_sum.9
  (4 shorter events, 0.0 us)
Async XLA Ops:
  0.6 0.8 copy-start
  1.4 18.1 %copy-start.2 = (bf16[320,2048]{1,0:T(8,128)(2,1)S(1)}, bf16[320,2048]{1,0:T(8,128)(2,1)}, u32[]{:S(2)}) copy-start(bf16[320,2048]{1,0:T(8,128)(2,1)} %param.10) | copy-start | bytes 3932164
  2.5 46.3 %all-to-all-start = ((bf16[64,8,1024]{2,1,0:T(8,128)(2,1)}), bf16[64,8,1024]{2,1,0:T(8,128)(2,1)}, u32[]{:S(2)}, u32[]{:S(2)}) async-start(bf16[64,8,1024]{2,1,0:T(8,128)(2,1)} %shard_map.77), calls=%async_computation | async-start | bytes 2097152 | tf_op jit(solution)/shard_map/all_to_all | solution.py:229
  20.5 37.2 %collective-permute-start = (bf16[320,512]{1,0:T(8,128)(2,1)}, bf16[320,512]{1,0:T(8,128)(2,1)S(1)}, u32[]{:S(2)}, u32[]{:S(2)}) collective-permute-start(bf16[320,512]{1,0:T(8,128)(2,1)} %get-tuple-element.31), channel_id=1, source_target_pairs={{0,1},{1,0},{2,3},{3,2},{4,5},{5,4},{6,7},{7,6},{8,9},{9,8},{10,11... | collective-permute-start | bytes 983048 | tf_op jit(solution)/shard_map/ppermute | solution.py:235
  23.9 33.8 %collective-permute-start.1 = (bf16[320,512]{1,0:T(8,128)(2,1)}, bf16[320,512]{1,0:T(8,128)(2,1)}, u32[]{:S(2)}, u32[]{:S(2)}) collective-permute-start(bf16[320,512]{1,0:T(8,128)(2,1)} %get-tuple-element.33), channel_id=1, source_target_pairs={{0,8},{1,9},{2,10},{3,11},{4,12},{5,13},{6,14},{7,15},{8,0},{9,1},... | collective-permute-start | bytes 983048 | tf_op jit(solution)/shard_map/ppermute | solution.py:235
  27.3 31.0 %collective-permute-start.2 = (bf16[320,512]{1,0:T(8,128)(2,1)}, bf16[320,512]{1,0:T(8,128)(2,1)}, u32[]{:S(2)}, u32[]{:S(2)}) collective-permute-start(bf16[320,512]{1,0:T(8,128)(2,1)} %get-tuple-element.30), channel_id=1, source_target_pairs={{0,9},{1,8},{2,11},{3,10},{4,13},{5,12},{6,15},{7,14},{8,1},{9,0},... | collective-permute-start | bytes 983048 | tf_op jit(solution)/shard_map/ppermute | solution.py:235
  29.7 19.1 %copy-start.1 = (f32[2048]{0:T(1024)S(1)}, f32[2048]{0:T(1024)}, u32[]{:S(2)}) copy-start(f32[2048]{0:T(1024)} %param.7) | copy-start | bytes 24580
  52.9 10.8 %all-to-all-start.1 = ((bf16[4,64,768]{2,1,0:T(8,128)(2,1)}), bf16[4,64,768]{2,1,0:T(8,128)(2,1)S(1)}, u32[]{:S(2)}, u32[]{:S(2)}) async-start(bf16[4,64,768]{2,1,0:T(8,128)(2,1)} %bitcast.4), calls=%async_computation.1 | async-start | bytes 786432 | tf_op jit(solution)/shard_map/all_to_all | solution.py:254
  64.8 16.0 %all-to-all-start.2 = ((bf16[16,64,384]{2,1,0:T(8,128)(2,1)}), bf16[16,64,384]{2,1,0:T(8,128)(2,1)S(1)}, u32[]{:S(2)}, u32[]{:S(2)}) async-start(bf16[16,64,384]{2,1,0:T(8,128)(2,1)} %shard_map.79), calls=%async_computation.2 | async-start | bytes 1572864 | tf_op jit(solution)/shard_map/all_to_all | solution.py:263
  80.8 4.2 %collective-permute-start.3 = (bf16[4,256,384]{2,1,0:T(8,128)(2,1)S(1)}, bf16[4,256,384]{2,1,0:T(8,128)(2,1)S(1)}, u32[]{:S(2)}, u32[]{:S(2)}) collective-permute-start(bf16[4,256,384]{2,1,0:T(8,128)(2,1)S(1)} %bitcast.11), channel_id=1, source_target_pairs={{0,256},{256,0},{1,257},{257,1},{2,258},{258,2},{3,259},{259,3},{4... | collective-permute-start | bytes 2359304 | tf_op jit(solution)/shard_map/ppermute | solution.py:265
  116.7 25.4 %all-to-all-start.4 = ((bf16[16,32,512]{2,1,0:T(8,128)(2,1)}), bf16[16,32,512]{2,1,0:T(8,128)(2,1)S(1)}, u32[]{:S(2)}, u32[]{:S(2)}) async-start(bf16[16,32,512]{2,1,0:T(8,128)(2,1)} %shard_map.82), calls=%async_computation.4 | async-start | bytes 1048576 | tf_op jit(solution)/shard_map/all_to_all | solution.py:294
  143.3 19.4 %all-to-all-start.5 = ((f32[16,16,128]{2,1,0:T(8,128)}), f32[16,16,128]{2,1,0:T(8,128)S(1)}, u32[]{:S(2)}, u32[]{:S(2)}) async-start(f32[16,16,128]{2,1,0:T(8,128)} %get-tuple-element.21), calls=%async_computation.5 | async-start | bytes 262144 | tf_op jit(solution)/shard_map/all_to_all | solution.py:315
  146.8 9.2 %collective-permute-start.4 = (bf16[160,512]{1,0:T(8,128)(2,1)S(1)}, bf16[160,512]{1,0:T(8,128)(2,1)S(1)}, u32[]{:S(2)}, u32[]{:S(2)}) collective-permute-start(bf16[160,512]{1,0:T(8,128)(2,1)S(1)} %get-tuple-element.23), channel_id=1, source_target_pairs={{0,1},{1,0},{2,3},{3,2},{4,5},{5,4},{6,7},{7,6},{8,9},{9,8},{10,11... | collective-permute-start | bytes 491528 | tf_op jit(solution)/shard_map/ppermute | solution.py:319
  150.2 7.9 %collective-permute-start.5 = (bf16[160,512]{1,0:T(8,128)(2,1)S(1)}, bf16[160,512]{1,0:T(8,128)(2,1)S(1)}, u32[]{:S(2)}, u32[]{:S(2)}) collective-permute-start(bf16[160,512]{1,0:T(8,128)(2,1)S(1)} %get-tuple-element.24), channel_id=1, source_target_pairs={{0,8},{1,9},{2,10},{3,11},{4,12},{5,13},{6,14},{7,15},{8,0},{9,1},... | collective-permute-start | bytes 491528 | tf_op jit(solution)/shard_map/ppermute | solution.py:319
  153.6 8.1 %collective-permute-start.6 = (bf16[160,512]{1,0:T(8,128)(2,1)S(1)}, bf16[160,512]{1,0:T(8,128)(2,1)S(1)}, u32[]{:S(2)}, u32[]{:S(2)}) collective-permute-start(bf16[160,512]{1,0:T(8,128)(2,1)S(1)} %get-tuple-element.25), channel_id=1, source_target_pairs={{0,9},{1,8},{2,11},{3,10},{4,13},{5,12},{6,15},{7,14},{8,1},{9,0},... | collective-permute-start | bytes 491528 | tf_op jit(solution)/shard_map/ppermute | solution.py:319

commit v11 on v10

--- a/solution.py
+++ b/solution.py
@@ -89,14 +89,9 @@
     repeat(piece, out_ref, held_ref, sems)
 
 
-def parent_kernel(tokens_ref, gain_ref, weights_any, out_ref, rows_ref, weights_ref, sems):
+def parent_kernel(tokens_ref, gain_ref, weights_ref, out_ref, rows_ref):
     n_shards, _, width = tokens_ref.shape
-    local = weights_ref.shape[1]
-    copies = [
-        pltpu.make_async_copy(weights_any.at[pl.ds(i * local, local)], weights_ref.at[i], sems.at[i]) for i in range(2)
-    ]
-    for copy in copies:
-        copy.start()
+    local = weights_ref.shape[0] // 2
     lanes = out_ref.shape[1] // 2
     step = 16
     squares = []
@@ -115,10 +110,8 @@
     squares = jnp.concatenate(squares, axis=0)
     hi = squares.astype(jnp.bfloat16).astype(jnp.float32)
     contract = (((1,), (1,)), ((), ()))
-    copies[0].wait()
-    gate = lax.dot_general(rows_ref[...], weights_ref[0], contract, preferred_element_type=jnp.float32)
-    copies[1].wait()
-    up = lax.dot_general(rows_ref[...], weights_ref[1], contract, preferred_element_type=jnp.float32)
+    gate = lax.dot_general(rows_ref[...], weights_ref[:local], contract, preferred_element_type=jnp.float32)
+    up = lax.dot_general(rows_ref[...], weights_ref[local:], contract, preferred_element_type=jnp.float32)
     lane = lax.broadcasted_iota(jnp.int32, (squares.shape[0], lanes - local), 1)
     extra = jnp.where(lane == 0, hi, jnp.where(lane == 1, squares - hi, 0.0))
     out_ref[:, :local] = gate.astype(out_ref.dtype)
@@ -240,13 +233,11 @@
     partial = call(
         parent_kernel,
         jax.ShapeDtypeStruct((n_wide * half, 2 * (local + pad)), jnp.bfloat16),
-        [VMEM, VMEM, ANY],
+        [VMEM] * 3,
         4 * n_wide * half * width * local,
         8 * width * local,
         [
             pltpu.VMEM((n_wide * half, width), jnp.bfloat16),
-            pltpu.VMEM((2, local, width), jnp.bfloat16),
-            pltpu.SemaphoreType.DMA((2,)),
         ],
     )(gathered, norm_gain.reshape(1, width), weights)
     rows = n_wide * half // n_tok

time: 166 us -> 166 us (level)
  transfers between devices with their start and end apart: 12 -> 12, of which waited for: 8 -> 8; matrix products, arithmetic and copies ran while one was open for 3% -> 3% of each run, Pallas kernels for 4% -> 3%
where the time goes in v11:
time: 166 us; the launch traced here: 165 us
  waiting for transfers between devices  59.8 us (36%)
  starting transfers between devices  55.7 us (34%)
  blocking collectives  29.3 us (18%)
  Pallas kernels  11.8 us (7%)
  other arithmetic  3.65 us (2%)
  between operations  2.67 us (2%)
  local copies, waits for them, and re-layouts  2.11 us (1%)
    all_to_all x1, blocking collectives, per_device(): shares = lax.all_to_all(shares, 'wide', 0, 0, axis_index_groups=strides)  29.3 us
    all_to_all x1, waiting for transfers between devices, per_device(): lax.all_to_all(pieces, 'wide', 0, 0, axis_index_groups=strides)  20.2 us
    all_to_all x1, waiting for transfers between devices, per_device(): gathered = lax.all_to_all(pieces, 'wide', 0, 0)  17.2 us
    all_to_all x1, starting transfers between devices, per_device(): gathered = lax.all_to_all(pieces, 'wide', 0, 0)  16.9 us
    all_to_all x1, waiting for transfers between devices, per_device(): lax.all_to_all(hidden, ('tok', 'wide'), 0, 0, axis_index_groups=groups)  9.87 us
    ppermute x3, starting transfers between devices, per_device(): downs[k] = lax.ppermute(downs[k], 'wide', perm)  9.2 us
    ppermute x3, starting transfers between devices, per_device(): grads[k] = lax.ppermute(grads[k], 'wide', perm)  9.2 us
    all_to_all x1, starting transfers between devices, per_device(): lax.all_to_all(hidden, ('tok', 'wide'), 0, 0, axis_index_groups=groups)  6.11 us
  transfers between devices with their start and end apart: 12, of which 8 were waited for; matrix products, arithmetic and copies ran while one was open for 3% of the time, Pallas kernels for 3%

profile of v11, /device:TPU:2, one launch (start us, length us, event | category | flops | bytes accessed | tf_op | source)
XLA Modules:
  0.0 165.1 jit_solution(11488274513214670114)
XLA Ops:
  0.6 0.0 copy-start
  0.6 0.7 copy-done
  1.4 0.0 copy-start.2
  1.4 1.1 shard_map.77
  2.5 16.9 %all-to-all-start = ((bf16[64,8,1024]{2,1,0:T(8,128)(2,1)}), bf16[64,8,1024]{2,1,0:T(8,128)(2,1)}, u32[]{:S(2)}, u32[]{:S(2)}) async-start(bf16[64,8,1024]{2,1,0:T(8,128)(2,1)} %shard_map.77), calls=%async_computation | async-start | bytes 2097152 | tf_op jit(solution)/shard_map/all_to_all | solution.py:222
  19.5 0.0 copy-done.2
  19.5 1.0 constant_dynamic-slice_fusion
  20.5 3.4 %collective-permute-start = (bf16[320,512]{1,0:T(8,128)(2,1)}, bf16[320,512]{1,0:T(8,128)(2,1)S(1)}, u32[]{:S(2)}, u32[]{:S(2)}) collective-permute-start(bf16[320,512]{1,0:T(8,128)(2,1)} %get-tuple-element.31), channel_id=1, source_target_pairs={{0,1},{1,0},{2,3},{3,2},{4,5},{5,4},{6,7},{7,6},{8,9},{9,8},{10,11... | collective-permute-start | bytes 983048 | tf_op jit(solution)/shard_map/ppermute | solution.py:228
  23.9 3.4 %collective-permute-start.1 = (bf16[320,512]{1,0:T(8,128)(2,1)}, bf16[320,512]{1,0:T(8,128)(2,1)}, u32[]{:S(2)}, u32[]{:S(2)}) collective-permute-start(bf16[320,512]{1,0:T(8,128)(2,1)} %get-tuple-element.33), channel_id=1, source_target_pairs={{0,8},{1,9},{2,10},{3,11},{4,12},{5,13},{6,14},{7,15},{8,0},{9,1},... | collective-permute-start | bytes 983048 | tf_op jit(solution)/shard_map/ppermute | solution.py:228
  27.3 2.4 %collective-permute-start.2 = (bf16[320,512]{1,0:T(8,128)(2,1)}, bf16[320,512]{1,0:T(8,128)(2,1)}, u32[]{:S(2)}, u32[]{:S(2)}) collective-permute-start(bf16[320,512]{1,0:T(8,128)(2,1)} %get-tuple-element.30), channel_id=1, source_target_pairs={{0,9},{1,8},{2,11},{3,10},{4,13},{5,12},{6,15},{7,14},{8,1},{9,0},... | collective-permute-start | bytes 983048 | tf_op jit(solution)/shard_map/ppermute | solution.py:228
  29.7 0.0 copy-start.1
  29.7 1.9 %pad_maximum_fusion.weights_ref = bf16[640,2048]{1,0:T(8,128)(2,1)S(1)} fusion(bf16[320,2048]{1,0:T(8,128)(2,1)} %bitcast.17, bf16[320,2048]{1,0:T(8,128)(2,1)} %bitcast.18), kind=kLoop, calls=%fused_computation | loop fusion | flops 5242880 | bytes 5242880 | tf_op jit(solution)/shard_map/concatenate | solution.py:230
  31.6 17.2 %all-to-all-done.tokens_ref = bf16[64,8,1024]{2,1,0:T(8,128)(2,1)} async-done(((bf16[64,8,1024]{2,1,0:T(8,128)(2,1)}), bf16[64,8,1024]{2,1,0:T(8,128)(2,1)}, u32[]{:S(2)}, u32[]{:S(2)}) %all-to-all-start) | async-done | bytes 1048608 | tf_op jit(solution)/shard_map/all_to_all | solution.py:222
  48.8 0.0 copy-done.1
  48.8 3.3 %shard_map.78 = bf16[256,768]{1,0:T(8,128)(2,1)} custom-call(bf16[64,8,1024]{2,1,0:T(8,128)(2,1)} %all-to-all-done.tokens_ref, f32[1,2048]{1,0:T(1,128)S(1)} %bitcast.16, bf16[640,2048]{1,0:T(8,128)(2,1)S(1)} %pad_maximum_fusion.weights_ref), custom_call_target="tpu_custom_call" | custom-call | flops 671088640 | bytes 5242880 | tf_op jit(solution)/shard_map/pallas_call | solution.py:233
  52.1 4.8 %all-to-all-start.1 = ((bf16[4,64,768]{2,1,0:T(8,128)(2,1)}), bf16[4,64,768]{2,1,0:T(8,128)(2,1)S(1)}, u32[]{:S(2)}, u32[]{:S(2)}) async-start(bf16[4,64,768]{2,1,0:T(8,128)(2,1)} %bitcast.4), calls=%async_computation.1 | async-start | bytes 786432 | tf_op jit(solution)/shard_map/all_to_all | solution.py:245
  56.9 0.0 collective-permute-done.down1
  56.9 0.0 collective-permute-done.1.down2
  56.9 1.3 collective-permute-done.2.down3
  58.3 4.6 %all-to-all-done.1.sums_ref = bf16[4,64,768]{2,1,0:T(8,128)(2,1)S(1)} async-done(((bf16[4,64,768]{2,1,0:T(8,128)(2,1)}), bf16[4,64,768]{2,1,0:T(8,128)(2,1)S(1)}, u32[]{:S(2)}, u32[]{:S(2)}) %all-to-all-start.1) | async-done | bytes 393248 | tf_op jit(solution)/shard_map/all_to_all | solution.py:245
  62.8 1.1 shard_map.79
  64.0 6.1 %all-to-all-start.2 = ((bf16[16,64,384]{2,1,0:T(8,128)(2,1)}), bf16[16,64,384]{2,1,0:T(8,128)(2,1)S(1)}, u32[]{:S(2)}, u32[]{:S(2)}) async-start(bf16[16,64,384]{2,1,0:T(8,128)(2,1)} %shard_map.79), calls=%async_computation.2 | async-start | bytes 1572864 | tf_op jit(solution)/shard_map/all_to_all | solution.py:254
  70.1 9.9 %all-to-all-done.2 = bf16[16,64,384]{2,1,0:T(8,128)(2,1)S(1)} async-done(((bf16[16,64,384]{2,1,0:T(8,128)(2,1)}), bf16[16,64,384]{2,1,0:T(8,128)(2,1)S(1)}, u32[]{:S(2)}, u32[]{:S(2)}) %all-to-all-start.2) | async-done | bytes 786464 | tf_op jit(solution)/shard_map/all_to_all | solution.py:254
  80.0 1.9 %collective-permute-start.3 = (bf16[4,256,384]{2,1,0:T(8,128)(2,1)S(1)}, bf16[4,256,384]{2,1,0:T(8,128)(2,1)S(1)}, u32[]{:S(2)}, u32[]{:S(2)}) collective-permute-start(bf16[4,256,384]{2,1,0:T(8,128)(2,1)S(1)} %bitcast.11), channel_id=1, source_target_pairs={{0,256},{256,0},{1,257},{257,1},{2,258},{258,2},{3,259},{259,3},{4... | collective-permute-start | bytes 2359304 | tf_op jit(solution)/shard_map/ppermute | solution.py:256
  81.9 0.8 fusion.2
  82.7 0.3 fusion
  83.0 0.1 convert_element_type.31
  83.1 0.1 convert_element_type.30
  83.2 0.9 collective-permute-done.3.other_ref
  84.2 2.3 %shard_map.81 = bf16[2,256,512]{2,1,0:T(8,128)(2,1)S(1)} custom-call(bf16[4,256,384]{2,1,0:T(8,128)(2,1)S(1)} %bitcast.12, bf16[4,256,384]{2,1,0:T(8,128)(2,1)S(1)} %collective-permute-done.3.other_ref, bf16[4,1,320]{2,1,0:T(2,128)(2,1)S(1)} %pad_maximum_fusion.1.drop_ref, bf16[320,512]{1,0:T(8,128)(2,1)S(1)} %get-tuple-element.17.down0, ...), custom_call_target="tpu_custom_call" | custom-call | flops 671088640 | bytes 1048576 | tf_op jit(solution)/shard_map/pallas_call | solution.py:274
  86.5 29.3 %all_to_all.30.shares_ref = bf16[16,32,512]{2,1,0:T(8,128)(2,1)S(1)} all-to-all(bf16[16,32,512]{2,1,0:T(8,128)(2,1)S(1)} %bitcast.14), channel_id=1, replica_groups={{0,2,4,6,16,18,20,22,32,34,36,38,48,50,52,54},{1,3,5,7,17,19,21,23,33,3..., dimensions={0} | all-to-all | bytes 1048576 | tf_op jit(solution)/shard_map/all_to_all | solution.py:283
  115.8 0.9 shard_map.82
  116.7 4.1 %all-to-all-start.4 = ((bf16[16,32,512]{2,1,0:T(8,128)(2,1)}), bf16[16,32,512]{2,1,0:T(8,128)(2,1)S(1)}, u32[]{:S(2)}, u32[]{:S(2)}) async-start(bf16[16,32,512]{2,1,0:T(8,128)(2,1)} %shard_map.82), calls=%async_computation.4 | async-start | bytes 1048576 | tf_op jit(solution)/shard_map/all_to_all | solution.py:285
  120.8 0.2 copy.11.names_ref
  121.0 0.9 shard_map.80.chosen_ref
  121.9 20.2 %all-to-all-done.4 = bf16[16,32,512]{2,1,0:T(8,128)(2,1)S(1)} async-done(((bf16[16,32,512]{2,1,0:T(8,128)(2,1)}), bf16[16,32,512]{2,1,0:T(8,128)(2,1)S(1)}, u32[]{:S(2)}, u32[]{:S(2)}) %all-to-all-start.4) | async-done | bytes 524320 | tf_op jit(solution)/shard_map/all_to_all | solution.py:285
  142.2 1.1 shard_map.83
  143.3 3.5 %all-to-all-start.5 = ((f32[16,16,128]{2,1,0:T(8,128)}), f32[16,16,128]{2,1,0:T(8,128)S(1)}, u32[]{:S(2)}, u32[]{:S(2)}) async-start(f32[16,16,128]{2,1,0:T(8,128)} %get-tuple-element.21), calls=%async_computation.5 | async-start | bytes 262144 | tf_op jit(solution)/shard_map/all_to_all | solution.py:306
  146.8 3.4 %collective-permute-start.4 = (bf16[160,512]{1,0:T(8,128)(2,1)S(1)}, bf16[160,512]{1,0:T(8,128)(2,1)S(1)}, u32[]{:S(2)}, u32[]{:S(2)}) collective-permute-start(bf16[160,512]{1,0:T(8,128)(2,1)S(1)} %get-tuple-element.23), channel_id=1, source_target_pairs={{0,1},{1,0},{2,3},{3,2},{4,5},{5,4},{6,7},{7,6},{8,9},{9,8},{10,11... | collective-permute-start | bytes 491528 | tf_op jit(solution)/shard_map/ppermute | solution.py:310
  150.2 3.4 %collective-permute-start.5 = (bf16[160,512]{1,0:T(8,128)(2,1)S(1)}, bf16[160,512]{1,0:T(8,128)(2,1)S(1)}, u32[]{:S(2)}, u32[]{:S(2)}) collective-permute-start(bf16[160,512]{1,0:T(8,128)(2,1)S(1)} %get-tuple-element.24), channel_id=1, source_target_pairs={{0,8},{1,9},{2,10},{3,11},{4,12},{5,13},{6,14},{7,15},{8,0},{9,1},... | collective-permute-start | bytes 491528 | tf_op jit(solution)/shard_map/ppermute | solution.py:310
  153.6 2.4 %collective-permute-start.6 = (bf16[160,512]{1,0:T(8,128)(2,1)S(1)}, bf16[160,512]{1,0:T(8,128)(2,1)S(1)}, u32[]{:S(2)}, u32[]{:S(2)}) collective-permute-start(bf16[160,512]{1,0:T(8,128)(2,1)S(1)} %get-tuple-element.25), channel_id=1, source_target_pairs={{0,9},{1,8},{2,11},{3,10},{4,13},{5,12},{6,15},{7,14},{8,1},{9,0},... | collective-permute-start | bytes 491528 | tf_op jit(solution)/shard_map/ppermute | solution.py:310
  156.0 0.0 collective-permute-done.4.in1
  156.1 2.1 %collective-permute-done.5.in2 = bf16[160,512]{1,0:T(8,128)(2,1)S(1)} collective-permute-done((bf16[160,512]{1,0:T(8,128)(2,1)S(1)}, bf16[160,512]{1,0:T(8,128)(2,1)S(1)}, u32[]{:S(2)}, u32[]{:S(2)}) %collective-permute-start.5) | collective-permute-done | bytes 163872 | tf_op jit(solution)/shard_map/ppermute | solution.py:310
  158.1 3.7 %collective-permute-done.6.in3 = bf16[160,512]{1,0:T(8,128)(2,1)S(1)} collective-permute-done((bf16[160,512]{1,0:T(8,128)(2,1)S(1)}, bf16[160,512]{1,0:T(8,128)(2,1)S(1)}, u32[]{:S(2)}, u32[]{:S(2)}) %collective-permute-start.6) | collective-permute-done | bytes 163872 | tf_op jit(solution)/shard_map/ppermute | solution.py:310
  161.8 0.9 shard_map.84
  162.7 0.0 all-to-all-done.5
  162.7 0.6 reduce_sum.9
  (4 shorter events, 0.0 us)
Async XLA Ops:
  0.6 0.8 copy-start
  1.4 18.1 %copy-start.2 = (bf16[320,2048]{1,0:T(8,128)(2,1)S(1)}, bf16[320,2048]{1,0:T(8,128)(2,1)}, u32[]{:S(2)}) copy-start(bf16[320,2048]{1,0:T(8,128)(2,1)} %param.10) | copy-start | bytes 3932164
  2.5 46.3 %all-to-all-start = ((bf16[64,8,1024]{2,1,0:T(8,128)(2,1)}), bf16[64,8,1024]{2,1,0:T(8,128)(2,1)}, u32[]{:S(2)}, u32[]{:S(2)}) async-start(bf16[64,8,1024]{2,1,0:T(8,128)(2,1)} %shard_map.77), calls=%async_computation | async-start | bytes 2097152 | tf_op jit(solution)/shard_map/all_to_all | solution.py:222
  20.5 36.4 %collective-permute-start = (bf16[320,512]{1,0:T(8,128)(2,1)}, bf16[320,512]{1,0:T(8,128)(2,1)S(1)}, u32[]{:S(2)}, u32[]{:S(2)}) collective-permute-start(bf16[320,512]{1,0:T(8,128)(2,1)} %get-tuple-element.31), channel_id=1, source_target_pairs={{0,1},{1,0},{2,3},{3,2},{4,5},{5,4},{6,7},{7,6},{8,9},{9,8},{10,11... | collective-permute-start | bytes 983048 | tf_op jit(solution)/shard_map/ppermute | solution.py:228
  23.9 33.0 %collective-permute-start.1 = (bf16[320,512]{1,0:T(8,128)(2,1)}, bf16[320,512]{1,0:T(8,128)(2,1)}, u32[]{:S(2)}, u32[]{:S(2)}) collective-permute-start(bf16[320,512]{1,0:T(8,128)(2,1)} %get-tuple-element.33), channel_id=1, source_target_pairs={{0,8},{1,9},{2,10},{3,11},{4,12},{5,13},{6,14},{7,15},{8,0},{9,1},... | collective-permute-start | bytes 983048 | tf_op jit(solution)/shard_map/ppermute | solution.py:228
  27.3 31.0 %collective-permute-start.2 = (bf16[320,512]{1,0:T(8,128)(2,1)}, bf16[320,512]{1,0:T(8,128)(2,1)}, u32[]{:S(2)}, u32[]{:S(2)}) collective-permute-start(bf16[320,512]{1,0:T(8,128)(2,1)} %get-tuple-element.30), channel_id=1, source_target_pairs={{0,9},{1,8},{2,11},{3,10},{4,13},{5,12},{6,15},{7,14},{8,1},{9,0},... | collective-permute-start | bytes 983048 | tf_op jit(solution)/shard_map/ppermute | solution.py:228
  29.7 19.1 %copy-start.1 = (f32[2048]{0:T(1024)S(1)}, f32[2048]{0:T(1024)}, u32[]{:S(2)}) copy-start(f32[2048]{0:T(1024)} %param.7) | copy-start | bytes 24580
  52.1 10.8 %all-to-all-start.1 = ((bf16[4,64,768]{2,1,0:T(8,128)(2,1)}), bf16[4,64,768]{2,1,0:T(8,128)(2,1)S(1)}, u32[]{:S(2)}, u32[]{:S(2)}) async-start(bf16[4,64,768]{2,1,0:T(8,128)(2,1)} %bitcast.4), calls=%async_computation.1 | async-start | bytes 786432 | tf_op jit(solution)/shard_map/all_to_all | solution.py:245
  64.0 16.0 %all-to-all-start.2 = ((bf16[16,64,384]{2,1,0:T(8,128)(2,1)}), bf16[16,64,384]{2,1,0:T(8,128)(2,1)S(1)}, u32[]{:S(2)}, u32[]{:S(2)}) async-start(bf16[16,64,384]{2,1,0:T(8,128)(2,1)} %shard_map.79), calls=%async_computation.2 | async-start | bytes 1572864 | tf_op jit(solution)/shard_map/all_to_all | solution.py:254
  80.0 4.2 %collective-permute-start.3 = (bf16[4,256,384]{2,1,0:T(8,128)(2,1)S(1)}, bf16[4,256,384]{2,1,0:T(8,128)(2,1)S(1)}, u32[]{:S(2)}, u32[]{:S(2)}) collective-permute-start(bf16[4,256,384]{2,1,0:T(8,128)(2,1)S(1)} %bitcast.11), channel_id=1, source_target_pairs={{0,256},{256,0},{1,257},{257,1},{2,258},{258,2},{3,259},{259,3},{4... | collective-permute-start | bytes 2359304 | tf_op jit(solution)/shard_map/ppermute | solution.py:256
  116.7 25.4 %all-to-all-start.4 = ((bf16[16,32,512]{2,1,0:T(8,128)(2,1)}), bf16[16,32,512]{2,1,0:T(8,128)(2,1)S(1)}, u32[]{:S(2)}, u32[]{:S(2)}) async-start(bf16[16,32,512]{2,1,0:T(8,128)(2,1)} %shard_map.82), calls=%async_computation.4 | async-start | bytes 1048576 | tf_op jit(solution)/shard_map/all_to_all | solution.py:285
  143.3 19.4 %all-to-all-start.5 = ((f32[16,16,128]{2,1,0:T(8,128)}), f32[16,16,128]{2,1,0:T(8,128)S(1)}, u32[]{:S(2)}, u32[]{:S(2)}) async-start(f32[16,16,128]{2,1,0:T(8,128)} %get-tuple-element.21), calls=%async_computation.5 | async-start | bytes 262144 | tf_op jit(solution)/shard_map/all_to_all | solution.py:306
  146.8 9.2 %collective-permute-start.4 = (bf16[160,512]{1,0:T(8,128)(2,1)S(1)}, bf16[160,512]{1,0:T(8,128)(2,1)S(1)}, u32[]{:S(2)}, u32[]{:S(2)}) collective-permute-start(bf16[160,512]{1,0:T(8,128)(2,1)S(1)} %get-tuple-element.23), channel_id=1, source_target_pairs={{0,1},{1,0},{2,3},{3,2},{4,5},{5,4},{6,7},{7,6},{8,9},{9,8},{10,11... | collective-permute-start | bytes 491528 | tf_op jit(solution)/shard_map/ppermute | solution.py:310
  150.2 7.9 %collective-permute-start.5 = (bf16[160,512]{1,0:T(8,128)(2,1)S(1)}, bf16[160,512]{1,0:T(8,128)(2,1)S(1)}, u32[]{:S(2)}, u32[]{:S(2)}) collective-permute-start(bf16[160,512]{1,0:T(8,128)(2,1)S(1)} %get-tuple-element.24), channel_id=1, source_target_pairs={{0,8},{1,9},{2,10},{3,11},{4,12},{5,13},{6,14},{7,15},{8,0},{9,1},... | collective-permute-start | bytes 491528 | tf_op jit(solution)/shard_map/ppermute | solution.py:310
  153.6 8.1 %collective-permute-start.6 = (bf16[160,512]{1,0:T(8,128)(2,1)S(1)}, bf16[160,512]{1,0:T(8,128)(2,1)S(1)}, u32[]{:S(2)}, u32[]{:S(2)}) collective-permute-start(bf16[160,512]{1,0:T(8,128)(2,1)S(1)} %get-tuple-element.25), channel_id=1, source_target_pairs={{0,9},{1,8},{2,11},{3,10},{4,13},{5,12},{6,15},{7,14},{8,1},{9,0},... | collective-permute-start | bytes 491528 | tf_op jit(solution)/shard_map/ppermute | solution.py:310

commit v12 on v8

--- a/solution.py
+++ b/solution.py
@@ -29,7 +29,6 @@
 
 
 VMEM = pl.BlockSpec(memory_space=pltpu.VMEM)
-SMEM = pl.BlockSpec(memory_space=pltpu.SMEM)
 
 
 def call(kernel, out_shape, in_specs, flops, size, scratch=()):
@@ -45,17 +44,22 @@
     )
 
 
-def spread_kernel(place_ref, tokens_ref, out_ref):
+def block_slot():
+    wide = lax.axis_index("wide")
+    return wide // SIDE % 2 * 2 + wide % 2
+
+
+def spread_kernel(tokens_ref, out_ref):
     width = out_ref.shape[2]
     tokens = tokens_ref[...].astype(jnp.float32)
     left, right = tokens[:, :width], tokens[:, width:]
-    odd = place_ref[1] == 1
+    odd = lax.axis_index("wide") % 2 == 1
     first = jnp.where(odd, right, left)
     second = jnp.where(odd, left, right)
     upper = lax.broadcasted_iota(jnp.int32, first.shape, 0) < 4
     low = jnp.where(upper, first, pltpu.roll(second, 4, 0))
     high = jnp.where(upper, pltpu.roll(first, 4, 0), second)
-    piece = jnp.where(place_ref[0] == 0, low, high).astype(out_ref.dtype)
+    piece = jnp.where(lax.axis_index("var") == 0, low, high).astype(out_ref.dtype)
     for i in range(out_ref.shape[0]):
         out_ref[i] = piece
 
@@ -91,8 +95,8 @@
     out_ref[:, lanes + local :] = jnp.zeros_like(extra).astype(out_ref.dtype)
 
 
-def residual_kernel(slot_ref, own_ref, other_ref, drop_ref, down0, down1, down2, down3, out_ref):
-    slot = slot_ref[0]
+def residual_kernel(own_ref, other_ref, drop_ref, down0, down1, down2, down3, out_ref):
+    slot = block_slot()
     downs = (down0, down1, down2, down3)
     local = down0.shape[0]
     for half, hidden_ref in enumerate((own_ref, other_ref)):
@@ -149,8 +153,8 @@
         out_ref[i] = piece
 
 
-def gradient_kernel(factor, slot_ref, chosen_ref, rounded_ref, out0, out1, out2, out3, error_ref, rows_ref):
-    slot = slot_ref[0]
+def gradient_kernel(factor, chosen_ref, rounded_ref, out0, out1, out2, out3, error_ref, rows_ref):
+    slot = block_slot()
     rounded = rounded_ref[...]
     block = out0.shape[0]
     for pair in range(2):
@@ -170,8 +174,8 @@
         error_ref[i] = lanes
 
 
-def interleave_kernel(slot_ref, in0, in1, in2, in3, out_ref):
-    slot = slot_ref[0]
+def interleave_kernel(in0, in1, in2, in3, out_ref):
+    slot = block_slot()
     width = in0.shape[1]
     for k, in_ref in enumerate((in0, in1, in2, in3)):
         start = pl.multiple_of((slot ^ k) * width, 128)
@@ -181,7 +185,6 @@
 def per_device(tokens, norm_gain, gate_parent, up_parent, down_parent, kept):
     n_wide = lax.axis_size("wide")
     n_tok = lax.axis_size("tok")
-    core = lax.axis_index("var")
     wide = lax.axis_index("wide")
     row, col = wide // SIDE, wide % SIDE
     slot = (row % 2) * 2 + col % 2
@@ -193,10 +196,10 @@
     pieces = call(
         spread_kernel,
         jax.ShapeDtypeStruct((n_wide, 2 * half, width // 2), jnp.bfloat16),
-        [SMEM, VMEM],
+        [VMEM],
         0,
         2 * n_wide * half * width,
-    )(jnp.stack([core, wide % 2]), tokens)
+    )(tokens)
     gathered = lax.all_to_all(pieces, "wide", 0, 0)
 
     quarter = down_parent.shape[1] // 4
@@ -252,10 +255,10 @@
     shares = call(
         residual_kernel,
         jax.ShapeDtypeStruct((2, total_rows // 2, quarter), jnp.bfloat16),
-        [SMEM] + [VMEM] * 7,
+        [VMEM] * 7,
         product_flops,
         4 * total_rows * quarter,
-    )(slot.reshape(1), hidden, other, drop, *downs)
+    )(hidden, other, drop, *downs)
     shares = shares.reshape(n_blocks, total_rows // n_blocks, quarter)
     strides = stride_groups()
     shares = lax.all_to_all(shares, "wide", 0, 0, axis_index_groups=strides)
@@ -276,11 +279,11 @@
             *[jax.ShapeDtypeStruct((block, quarter), jnp.bfloat16)] * 4,
             jax.ShapeDtypeStruct((4 * n_tok, 8, 128), jnp.float32),
         ),
-        [SMEM, VMEM, VMEM],
+        [VMEM, VMEM],
         2 * total_rows * 4 * block * quarter,
         4 * total_rows * quarter,
         [pltpu.VMEM((4, block, quarter), jnp.bfloat16)],
-    )(slot.reshape(1), chosen, rounded)
+    )(chosen, rounded)
     errors = lax.all_to_all(errors, ("tok", "wide"), 0, 0, axis_index_groups=groups)
     loss = jnp.sum(errors) / (total_rows * D)
     for k in range(1, 4):
@@ -289,10 +292,10 @@
     grad = call(
         interleave_kernel,
         jax.ShapeDtypeStruct((block, 4 * quarter), jnp.bfloat16),
-        [SMEM] + [VMEM] * 4,
+        [VMEM] * 4,
         0,
         4 * block * quarter,
-    )(slot.reshape(1), *grads)
+    )(*grads)
     return (loss.reshape(1), grad[None])
 
 

time: 166 us -> 165 us (level)
  no operation moved by 1% of the time
where the time goes in v12:
time: 165 us
  waiting for transfers between devices  54.3 us (33%)
  starting transfers between devices  52.2 us (32%)
  blocking collectives  38.4 us (23%)
  Pallas kernels  11.2 us (7%)
  other arithmetic  3.64 us (2%)
  between operations  2.68 us (2%)
  local copies, waits for them, and re-layouts  2.12 us (1%)
    all_to_all x1, blocking collectives, per_device(): shares = lax.all_to_all(shares, 'wide', 0, 0, axis_index_groups=strides)  29.3 us
    all_to_all x1, waiting for transfers between devices, per_device(): lax.all_to_all(pieces, 'wide', 0, 0, axis_index_groups=strides)  20.4 us
    all_to_all x1, waiting for transfers between devices, per_device(): gathered = lax.all_to_all(pieces, 'wide', 0, 0)  17.1 us
    all_to_all x1, starting transfers between devices, per_device(): gathered = lax.all_to_all(pieces, 'wide', 0, 0)  16.9 us
    all_to_all x1, waiting for transfers between devices, per_device(): lax.all_to_all(hidden, ('tok', 'wide'), 0, 0, axis_index_groups=groups)  9.87 us
    ppermute x3, starting transfers between devices, per_device(): grads[k] = lax.ppermute(grads[k], 'wide', perm)  9.21 us
    ppermute x3, starting transfers between devices, per_device(): downs[k] = lax.ppermute(downs[k], 'wide', perm)  9.2 us
    all_to_all x1, blocking collectives, per_device(): lax.all_to_all(errors, ('tok', 'wide'), 0, 0, axis_index_groups=groups)  9.07 us
  transfers between devices with their start and end apart: 11, of which 6 were waited for; matrix products, arithmetic and copies ran while one was open for 3% of the time, Pallas kernels for 3%

profile of v12, /device:TPU:2, one launch (start us, length us, event | category | flops | bytes accessed | tf_op | source)
XLA Modules:
  0.0 164.5 jit_solution(6690830023885419918)
XLA Ops:
  0.6 0.0 copy-start
  0.6 0.7 copy-done
  1.4 0.0 copy-start.2
  1.4 1.2 shard_map.77
  2.6 16.9 %all-to-all-start = ((bf16[64,8,1024]{2,1,0:T(8,128)(2,1)}), bf16[64,8,1024]{2,1,0:T(8,128)(2,1)}, u32[]{:S(2)}, u32[]{:S(2)}) async-start(bf16[64,8,1024]{2,1,0:T(8,128)(2,1)} %shard_map.77), calls=%async_computation | async-start | bytes 2097152 | tf_op jit(solution)/shard_map/all_to_all | solution.py:203
  19.5 0.0 copy-done.2
  19.5 1.0 constant_dynamic-slice_fusion
  20.5 3.4 %collective-permute-start = (bf16[320,512]{1,0:T(8,128)(2,1)}, bf16[320,512]{1,0:T(8,128)(2,1)S(1)}, u32[]{:S(2)}, u32[]{:S(2)}) collective-permute-start(bf16[320,512]{1,0:T(8,128)(2,1)} %get-tuple-element.31), channel_id=1, source_target_pairs={{0,1},{1,0},{2,3},{3,2},{4,5},{5,4},{6,7},{7,6},{8,9},{9,8},{10,11... | collective-permute-start | bytes 983048 | tf_op jit(solution)/shard_map/ppermute | solution.py:209
  23.9 3.4 %collective-permute-start.1 = (bf16[320,512]{1,0:T(8,128)(2,1)}, bf16[320,512]{1,0:T(8,128)(2,1)}, u32[]{:S(2)}, u32[]{:S(2)}) collective-permute-start(bf16[320,512]{1,0:T(8,128)(2,1)} %get-tuple-element.33), channel_id=1, source_target_pairs={{0,8},{1,9},{2,10},{3,11},{4,12},{5,13},{6,14},{7,15},{8,0},{9,1},... | collective-permute-start | bytes 983048 | tf_op jit(solution)/shard_map/ppermute | solution.py:209
  27.3 2.4 %collective-permute-start.2 = (bf16[320,512]{1,0:T(8,128)(2,1)}, bf16[320,512]{1,0:T(8,128)(2,1)}, u32[]{:S(2)}, u32[]{:S(2)}) collective-permute-start(bf16[320,512]{1,0:T(8,128)(2,1)} %get-tuple-element.30), channel_id=1, source_target_pairs={{0,9},{1,8},{2,11},{3,10},{4,13},{5,12},{6,15},{7,14},{8,1},{9,0},... | collective-permute-start | bytes 983048 | tf_op jit(solution)/shard_map/ppermute | solution.py:209
  29.8 0.0 copy-start.1
  29.8 1.9 %pad_maximum_fusion.weights_ref = bf16[640,2048]{1,0:T(8,128)(2,1)S(1)} fusion(bf16[320,2048]{1,0:T(8,128)(2,1)} %bitcast.17, bf16[320,2048]{1,0:T(8,128)(2,1)} %bitcast.18), kind=kLoop, calls=%fused_computation | loop fusion | flops 5242880 | bytes 5242880 | tf_op jit(solution)/shard_map/concatenate | solution.py:211
  31.7 17.1 %all-to-all-done.tokens_ref = bf16[64,8,1024]{2,1,0:T(8,128)(2,1)} async-done(((bf16[64,8,1024]{2,1,0:T(8,128)(2,1)}), bf16[64,8,1024]{2,1,0:T(8,128)(2,1)}, u32[]{:S(2)}, u32[]{:S(2)}) %all-to-all-start) | async-done | bytes 1048608 | tf_op jit(solution)/shard_map/all_to_all | solution.py:203
  48.8 0.0 copy-done.1
  48.8 3.3 %shard_map.78 = bf16[256,768]{1,0:T(8,128)(2,1)} custom-call(bf16[64,8,1024]{2,1,0:T(8,128)(2,1)} %all-to-all-done.tokens_ref, f32[1,2048]{1,0:T(1,128)S(1)} %bitcast.16, bf16[640,2048]{1,0:T(8,128)(2,1)S(1)} %pad_maximum_fusion.weights_ref), custom_call_target="tpu_custom_call" | custom-call | flops 671088640 | bytes 5242880 | tf_op jit(solution)/shard_map/pallas_call | solution.py:214
  52.1 4.8 %all-to-all-start.1 = ((bf16[4,64,768]{2,1,0:T(8,128)(2,1)}), bf16[4,64,768]{2,1,0:T(8,128)(2,1)S(1)}, u32[]{:S(2)}, u32[]{:S(2)}) async-start(bf16[4,64,768]{2,1,0:T(8,128)(2,1)} %bitcast.4), calls=%async_computation.1 | async-start | bytes 786432 | tf_op jit(solution)/shard_map/all_to_all | solution.py:224
  57.0 0.0 collective-permute-done.down1
  57.0 0.0 collective-permute-done.1.down2
  57.0 1.3 collective-permute-done.2.down3
  58.3 4.6 %all-to-all-done.1.sums_ref = bf16[4,64,768]{2,1,0:T(8,128)(2,1)S(1)} async-done(((bf16[4,64,768]{2,1,0:T(8,128)(2,1)}), bf16[4,64,768]{2,1,0:T(8,128)(2,1)S(1)}, u32[]{:S(2)}, u32[]{:S(2)}) %all-to-all-start.1) | async-done | bytes 393248 | tf_op jit(solution)/shard_map/all_to_all | solution.py:224
  62.9 1.2 shard_map.79
  64.0 6.1 %all-to-all-start.2 = ((bf16[16,64,384]{2,1,0:T(8,128)(2,1)}), bf16[16,64,384]{2,1,0:T(8,128)(2,1)S(1)}, u32[]{:S(2)}, u32[]{:S(2)}) async-start(bf16[16,64,384]{2,1,0:T(8,128)(2,1)} %shard_map.79), calls=%async_computation.2 | async-start | bytes 1572864 | tf_op jit(solution)/shard_map/all_to_all | solution.py:235
  70.1 9.9 %all-to-all-done.2 = bf16[16,64,384]{2,1,0:T(8,128)(2,1)S(1)} async-done(((bf16[16,64,384]{2,1,0:T(8,128)(2,1)}), bf16[16,64,384]{2,1,0:T(8,128)(2,1)S(1)}, u32[]{:S(2)}, u32[]{:S(2)}) %all-to-all-start.2) | async-done | bytes 786464 | tf_op jit(solution)/shard_map/all_to_all | solution.py:235
  80.0 1.9 %collective-permute-start.3 = (bf16[4,256,384]{2,1,0:T(8,128)(2,1)S(1)}, bf16[4,256,384]{2,1,0:T(8,128)(2,1)S(1)}, u32[]{:S(2)}, u32[]{:S(2)}) collective-permute-start(bf16[4,256,384]{2,1,0:T(8,128)(2,1)S(1)} %bitcast.11), channel_id=1, source_target_pairs={{0,256},{256,0},{1,257},{257,1},{2,258},{258,2},{3,259},{259,3},{4... | collective-permute-start | bytes 2359304 | tf_op jit(solution)/shard_map/ppermute | solution.py:237
  81.9 0.8 fusion.2
  82.7 0.3 fusion
  83.0 0.1 convert_element_type.31
  83.1 0.1 convert_element_type.30
  83.2 0.9 collective-permute-done.3.other_ref
  84.2 2.3 %shard_map.81 = bf16[2,256,512]{2,1,0:T(8,128)(2,1)S(1)} custom-call(bf16[4,256,384]{2,1,0:T(8,128)(2,1)S(1)} %bitcast.12, bf16[4,256,384]{2,1,0:T(8,128)(2,1)S(1)} %collective-permute-done.3.other_ref, bf16[4,1,320]{2,1,0:T(2,128)(2,1)S(1)} %pad_maximum_fusion.1.drop_ref, bf16[320,512]{1,0:T(8,128)(2,1)S(1)} %get-tuple-element.17.down0, ...), custom_call_target="tpu_custom_call" | custom-call | flops 671088640 | bytes 1048576 | tf_op jit(solution)/shard_map/pallas_call | solution.py:255
  86.5 29.3 %all_to_all.30.shares_ref = bf16[16,32,512]{2,1,0:T(8,128)(2,1)S(1)} all-to-all(bf16[16,32,512]{2,1,0:T(8,128)(2,1)S(1)} %bitcast.14), channel_id=1, replica_groups={{0,2,4,6,16,18,20,22,32,34,36,38,48,50,52,54},{1,3,5,7,17,19,21,23,33,3..., dimensions={0} | all-to-all | bytes 1048576 | tf_op jit(solution)/shard_map/all_to_all | solution.py:264
  115.8 0.9 shard_map.82
  116.7 4.1 %all-to-all-start.4 = ((bf16[16,32,512]{2,1,0:T(8,128)(2,1)}), bf16[16,32,512]{2,1,0:T(8,128)(2,1)S(1)}, u32[]{:S(2)}, u32[]{:S(2)}) async-start(bf16[16,32,512]{2,1,0:T(8,128)(2,1)} %shard_map.82), calls=%async_computation.4 | async-start | bytes 1048576 | tf_op jit(solution)/shard_map/all_to_all | solution.py:266
  120.8 0.2 copy.11.names_ref
  121.0 0.9 shard_map.80.chosen_ref
  121.9 20.4 %all-to-all-done.4 = bf16[16,32,512]{2,1,0:T(8,128)(2,1)S(1)} async-done(((bf16[16,32,512]{2,1,0:T(8,128)(2,1)}), bf16[16,32,512]{2,1,0:T(8,128)(2,1)S(1)}, u32[]{:S(2)}, u32[]{:S(2)}) %all-to-all-start.4) | async-done | bytes 524320 | tf_op jit(solution)/shard_map/all_to_all | solution.py:266
  142.3 0.6 shard_map.83
  142.9 1.9 %collective-permute-start.4 = (bf16[160,512]{1,0:T(8,128)(2,1)S(1)}, bf16[160,512]{1,0:T(8,128)(2,1)S(1)}, u32[]{:S(2)}, u32[]{:S(2)}) collective-permute-start(bf16[160,512]{1,0:T(8,128)(2,1)S(1)} %get-tuple-element.23), channel_id=1, source_target_pairs={{0,1},{1,0},{2,3},{3,2},{4,5},{5,4},{6,7},{7,6},{8,9},{9,8},{10,11... | collective-permute-start | bytes 491528 | tf_op jit(solution)/shard_map/ppermute | solution.py:291
  144.8 1.9 %collective-permute-start.5 = (bf16[160,512]{1,0:T(8,128)(2,1)S(1)}, bf16[160,512]{1,0:T(8,128)(2,1)S(1)}, u32[]{:S(2)}, u32[]{:S(2)}) collective-permute-start(bf16[160,512]{1,0:T(8,128)(2,1)S(1)} %get-tuple-element.24), channel_id=1, source_target_pairs={{0,8},{1,9},{2,10},{3,11},{4,12},{5,13},{6,14},{7,15},{8,0},{9,1},... | collective-permute-start | bytes 491528 | tf_op jit(solution)/shard_map/ppermute | solution.py:291
  146.7 5.4 %collective-permute-start.6 = (bf16[160,512]{1,0:T(8,128)(2,1)S(1)}, bf16[160,512]{1,0:T(8,128)(2,1)S(1)}, u32[]{:S(2)}, u32[]{:S(2)}) collective-permute-start(bf16[160,512]{1,0:T(8,128)(2,1)S(1)} %get-tuple-element.25), channel_id=1, source_target_pairs={{0,9},{1,8},{2,11},{3,10},{4,13},{5,12},{6,15},{7,14},{8,1},{9,0},... | collective-permute-start | bytes 491528 | tf_op jit(solution)/shard_map/ppermute | solution.py:291
  152.1 9.1 %all_to_all.31 = f32[16,8,128]{2,1,0:T(8,128)S(1)} all-to-all(f32[16,8,128]{2,1,0:T(8,128)S(1)} %get-tuple-element.21), channel_id=1, replica_groups={{0,64,128,192,1,65,129,193,8,72,136,200,9,73,137,201},{2,66,130,194,3,6..., dimensions={0} | all-to-all | bytes 131072 | tf_op jit(solution)/shard_map/all_to_all | solution.py:287
  161.2 0.6 reduce_sum.9
  162.5 0.0 collective-permute-done.4.in1
  162.5 0.0 collective-permute-done.5.in2
  162.5 0.0 collective-permute-done.6.in3
  162.5 0.9 shard_map.84
  (4 shorter events, 0.0 us)
Async XLA Ops:
  0.6 0.8 copy-start
  1.4 18.1 %copy-start.2 = (bf16[320,2048]{1,0:T(8,128)(2,1)S(1)}, bf16[320,2048]{1,0:T(8,128)(2,1)}, u32[]{:S(2)}) copy-start(bf16[320,2048]{1,0:T(8,128)(2,1)} %param.10) | copy-start | bytes 3932164
  2.6 46.3 %all-to-all-start = ((bf16[64,8,1024]{2,1,0:T(8,128)(2,1)}), bf16[64,8,1024]{2,1,0:T(8,128)(2,1)}, u32[]{:S(2)}, u32[]{:S(2)}) async-start(bf16[64,8,1024]{2,1,0:T(8,128)(2,1)} %shard_map.77), calls=%async_computation | async-start | bytes 2097152 | tf_op jit(solution)/shard_map/all_to_all | solution.py:203
  20.5 36.4 %collective-permute-start = (bf16[320,512]{1,0:T(8,128)(2,1)}, bf16[320,512]{1,0:T(8,128)(2,1)S(1)}, u32[]{:S(2)}, u32[]{:S(2)}) collective-permute-start(bf16[320,512]{1,0:T(8,128)(2,1)} %get-tuple-element.31), channel_id=1, source_target_pairs={{0,1},{1,0},{2,3},{3,2},{4,5},{5,4},{6,7},{7,6},{8,9},{9,8},{10,11... | collective-permute-start | bytes 983048 | tf_op jit(solution)/shard_map/ppermute | solution.py:209
  23.9 33.0 %collective-permute-start.1 = (bf16[320,512]{1,0:T(8,128)(2,1)}, bf16[320,512]{1,0:T(8,128)(2,1)}, u32[]{:S(2)}, u32[]{:S(2)}) collective-permute-start(bf16[320,512]{1,0:T(8,128)(2,1)} %get-tuple-element.33), channel_id=1, source_target_pairs={{0,8},{1,9},{2,10},{3,11},{4,12},{5,13},{6,14},{7,15},{8,0},{9,1},... | collective-permute-start | bytes 983048 | tf_op jit(solution)/shard_map/ppermute | solution.py:209
  27.3 31.0 %collective-permute-start.2 = (bf16[320,512]{1,0:T(8,128)(2,1)}, bf16[320,512]{1,0:T(8,128)(2,1)}, u32[]{:S(2)}, u32[]{:S(2)}) collective-permute-start(bf16[320,512]{1,0:T(8,128)(2,1)} %get-tuple-element.30), channel_id=1, source_target_pairs={{0,9},{1,8},{2,11},{3,10},{4,13},{5,12},{6,15},{7,14},{8,1},{9,0},... | collective-permute-start | bytes 983048 | tf_op jit(solution)/shard_map/ppermute | solution.py:209
  29.8 19.1 %copy-start.1 = (f32[2048]{0:T(1024)S(1)}, f32[2048]{0:T(1024)}, u32[]{:S(2)}) copy-start(f32[2048]{0:T(1024)} %param.7) | copy-start | bytes 24580
  52.1 10.8 %all-to-all-start.1 = ((bf16[4,64,768]{2,1,0:T(8,128)(2,1)}), bf16[4,64,768]{2,1,0:T(8,128)(2,1)S(1)}, u32[]{:S(2)}, u32[]{:S(2)}) async-start(bf16[4,64,768]{2,1,0:T(8,128)(2,1)} %bitcast.4), calls=%async_computation.1 | async-start | bytes 786432 | tf_op jit(solution)/shard_map/all_to_all | solution.py:224
  64.0 16.0 %all-to-all-start.2 = ((bf16[16,64,384]{2,1,0:T(8,128)(2,1)}), bf16[16,64,384]{2,1,0:T(8,128)(2,1)S(1)}, u32[]{:S(2)}, u32[]{:S(2)}) async-start(bf16[16,64,384]{2,1,0:T(8,128)(2,1)} %shard_map.79), calls=%async_computation.2 | async-start | bytes 1572864 | tf_op jit(solution)/shard_map/all_to_all | solution.py:235
  80.0 4.2 %collective-permute-start.3 = (bf16[4,256,384]{2,1,0:T(8,128)(2,1)S(1)}, bf16[4,256,384]{2,1,0:T(8,128)(2,1)S(1)}, u32[]{:S(2)}, u32[]{:S(2)}) collective-permute-start(bf16[4,256,384]{2,1,0:T(8,128)(2,1)S(1)} %bitcast.11), channel_id=1, source_target_pairs={{0,256},{256,0},{1,257},{257,1},{2,258},{258,2},{3,259},{259,3},{4... | collective-permute-start | bytes 2359304 | tf_op jit(solution)/shard_map/ppermute | solution.py:237
  116.7 25.6 %all-to-all-start.4 = ((bf16[16,32,512]{2,1,0:T(8,128)(2,1)}), bf16[16,32,512]{2,1,0:T(8,128)(2,1)S(1)}, u32[]{:S(2)}, u32[]{:S(2)}) async-start(bf16[16,32,512]{2,1,0:T(8,128)(2,1)} %shard_map.82), calls=%async_computation.4 | async-start | bytes 1048576 | tf_op jit(solution)/shard_map/all_to_all | solution.py:266
  142.9 19.6 %collective-permute-start.4 = (bf16[160,512]{1,0:T(8,128)(2,1)S(1)}, bf16[160,512]{1,0:T(8,128)(2,1)S(1)}, u32[]{:S(2)}, u32[]{:S(2)}) collective-permute-start(bf16[160,512]{1,0:T(8,128)(2,1)S(1)} %get-tuple-element.23), channel_id=1, source_target_pairs={{0,1},{1,0},{2,3},{3,2},{4,5},{5,4},{6,7},{7,6},{8,9},{9,8},{10,11... | collective-permute-start | bytes 491528 | tf_op jit(solution)/shard_map/ppermute | solution.py:291
  144.8 17.7 %collective-permute-start.5 = (bf16[160,512]{1,0:T(8,128)(2,1)S(1)}, bf16[160,512]{1,0:T(8,128)(2,1)S(1)}, u32[]{:S(2)}, u32[]{:S(2)}) collective-permute-start(bf16[160,512]{1,0:T(8,128)(2,1)S(1)} %get-tuple-element.24), channel_id=1, source_target_pairs={{0,8},{1,9},{2,10},{3,11},{4,12},{5,13},{6,14},{7,15},{8,0},{9,1},... | collective-permute-start | bytes 491528 | tf_op jit(solution)/shard_map/ppermute | solution.py:291
  146.7 15.7 %collective-permute-start.6 = (bf16[160,512]{1,0:T(8,128)(2,1)S(1)}, bf16[160,512]{1,0:T(8,128)(2,1)S(1)}, u32[]{:S(2)}, u32[]{:S(2)}) collective-permute-start(bf16[160,512]{1,0:T(8,128)(2,1)S(1)} %get-tuple-element.25), channel_id=1, source_target_pairs={{0,9},{1,8},{2,11},{3,10},{4,13},{5,12},{6,15},{7,14},{8,1},{9,0},... | collective-permute-start | bytes 491528 | tf_op jit(solution)/shard_map/ppermute | solution.py:291
